TPU v7x, 128 devices: a whole 4x4x4 slice. The times are simulated.
128 devices in a mesh: dp: 8 (over z, x_lo), fsdp: 16 (over y, x_hi, core).
Axes of the slice: x: 4 (x_hi: 2, x_lo: 2; x = x_hi * 2 + x_lo), y: 4, z: 4, core: 2. Of those that a mesh axis runs over, the one named last changes fastest.
Arguments:
- incoming_activations: bfloat16 [16384, 768], P(('dp', 'fsdp')), may hold values from -24 to 24
- sequence_opening_memory: float32 [128, 12, 64, 64], P(('dp', 'fsdp')), may hold values from -10 to 10
- prior_standardize_factor: bfloat16 [768], P(('dp', 'fsdp')), may hold values from 0.099609375 to 1.8984375
- prior_standardize_offset: bfloat16 [768], P(('dp', 'fsdp')), may hold values from -3 to 3
- acceptor_lerp_factor: bfloat16 [768], P(('dp', 'fsdp')), may hold values from 0 to 1
- address_lerp_factor: bfloat16 [768], P(('dp', 'fsdp')), may hold values from 0 to 1
- content_lerp_factor: bfloat16 [768], P(('dp', 'fsdp')), may hold values from 0 to 1
- sigmoid_lerp_factor: bfloat16 [768], P(('dp', 'fsdp')), may hold values from 0 to 1
- acceptor_matrix: bfloat16 [768, 768], P(('dp', 'fsdp')), may hold values from -0.21875 to 0.21875
- address_matrix: bfloat16 [768, 768], P(('dp', 'fsdp')), may hold values from -0.21875 to 0.21875
- content_matrix: bfloat16 [768, 768], P(('dp', 'fsdp')), may hold values from -0.21875 to 0.21875
- sigmoid_matrix: bfloat16 [768, 768], P(('dp', 'fsdp')), may hold values from -0.21875 to 0.21875
- lane_fading_exponent: bfloat16 [768], P(('dp', 'fsdp')), may hold values from -6.5 to -1
- present_reward_vector: bfloat16 [768], P(('dp', 'fsdp')), may hold values from -3 to 3
- cluster_standardize_factor: bfloat16 [768], P(('dp', 'fsdp')), may hold values from 0.099609375 to 1.8984375
- cluster_standardize_offset: bfloat16 [768], P(('dp', 'fsdp')), may hold values from -3 to 3
- mixer_result_matrix: bfloat16 [768, 768], P(('dp', 'fsdp')), may hold values from -0.21875 to 0.21875
- latter_standardize_factor: bfloat16 [768], P(('dp', 'fsdp')), may hold values from 0.099609375 to 1.8984375
- latter_standardize_offset: bfloat16 [768], P(('dp', 'fsdp')), may hold values from -3 to 3
- feedforward_address_lerp: bfloat16 [768], P(('dp', 'fsdp')), may hold values from 0 to 1
- feedforward_sigmoid_lerp: bfloat16 [768], P(('dp', 'fsdp')), may hold values from 0 to 1
- feedforward_address_matrix: bfloat16 [768, 2688], P(('dp', 'fsdp')), may hold values from -0.21875 to 0.21875
- feedforward_content_matrix: bfloat16 [2688, 768], P(('dp', 'fsdp')), may hold values from -0.125 to 0.125
- feedforward_acceptor_matrix: bfloat16 [768, 768], P(('dp', 'fsdp')), may hold values from -0.21875 to 0.21875
- upstream_derivative: bfloat16 [16384, 768], P(('dp', 'fsdp')), may hold values from -6 to 6
Outputs:
- layer_output: float32 [16384, 768], P(('dp', 'fsdp'))
- input_grad: float32 [16384, 768], P(('dp', 'fsdp'))
- grad_first_gain: float32 [768], P(('dp', 'fsdp'))
- grad_first_bias: float32 [768], P(('dp', 'fsdp'))
- grad_lerp_recept: float32 [768], P(('dp', 'fsdp'))
- grad_lerp_key: float32 [768], P(('dp', 'fsdp'))
- grad_lerp_value: float32 [768], P(('dp', 'fsdp'))
- grad_lerp_gate: float32 [768], P(('dp', 'fsdp'))
- grad_proj_recept: float32 [768, 768], P(('dp', 'fsdp'))
- grad_proj_key: float32 [768, 768], P(('dp', 'fsdp'))
- grad_proj_value: float32 [768, 768], P(('dp', 'fsdp'))
- grad_proj_gate: float32 [768, 768], P(('dp', 'fsdp'))
- grad_time_decay: float32 [768], P(('dp', 'fsdp'))
- grad_time_bonus: float32 [768], P(('dp', 'fsdp'))
- grad_group_gain: float32 [768], P(('dp', 'fsdp'))
- grad_group_bias: float32 [768], P(('dp', 'fsdp'))
- grad_proj_output: float32 [768, 768], P(('dp', 'fsdp'))
- grad_second_gain: float32 [768], P(('dp', 'fsdp'))
- grad_second_bias: float32 [768], P(('dp', 'fsdp'))
- grad_lerp_channel: float32 [768], P(('dp', 'fsdp'))
- grad_lerp_gating: float32 [768], P(('dp', 'fsdp'))
- grad_channel_key: float32 [768, 2688], P(('dp', 'fsdp'))
- grad_channel_value: float32 [2688, 768], P(('dp', 'fsdp'))
- grad_channel_gate: float32 [768, 768], P(('dp', 'fsdp'))
All inputs are finite; a program needn't handle non-finite values.
Results may differ from a plain program's by a relative error of at most 0.02.
Values may be sent and summed in bfloat16 or wider, within the bound.
A program may use at most 128 MiB of HBM per device.

v0:
```python
from functools import partial

import jax
import jax.numpy as jnp
from jax import lax
from jax.sharding import PartitionSpec as P

MIXER_LANES = 12
LANE_SIZE = 64
SPAN = 64


highest = lax.Precision.HIGHEST
norm_eps = 1e-05
group_eps = 0.00064


def layer_norm(values, scale_vec, shift_vec):
    average = jnp.mean(values, axis=-1, keepdims=True)
    centred = values - average
    variance = jnp.mean(centred * centred, axis=-1, keepdims=True)
    return centred * lax.rsqrt(variance + norm_eps) * scale_vec + shift_vec


def time_shift(values):
    return jnp.concatenate([jnp.zeros_like(values[..., :1, :]), values[..., :-1, :]], axis=-2)


def blend(normed, previous, weights):
    return normed * weights + previous * (1.0 - weights)


def matmul(left, right):
    return jnp.dot(left, right, preferred_element_type=jnp.float32)


def weight_grad(left, right):
    return lax.dot_general(
        left, right, (((0, 1), (0, 1)), ((), ())), preferred_element_type=jnp.float32
    )


def input_grad_of(grads, matrix):
    return lax.dot_general(
        grads, matrix, (((2,), (1,)), ((), ())), preferred_element_type=jnp.float32
    )


def owner_sums(members):
    return lax.psum_scatter(members, ("dp", "fsdp"), scatter_dimension=0, tiled=True)


def memory_segment_routine(running_memory, result_fragments, fading_exponent, reward_addend):
    acceptor_vectors, address_vectors, content_vectors = result_fragments
    block_len = acceptor_vectors.shape[1]
    places = jnp.arange(block_len).astype(jnp.float32)
    fall_query = jnp.exp(places[:, None, None] * fading_exponent)
    fall_key = jnp.exp(-(places[:, None, None] + 1.0) * fading_exponent)
    tail_key = jnp.exp((block_len - 1.0 - places)[:, None, None] * fading_exponent)
    decayed = acceptor_vectors * fall_query
    scores = jnp.einsum("gthi,gshi->ghts", decayed, address_vectors * fall_key, precision=highest)
    below_diag = places[:, None] > places[None, :]
    scores = jnp.where(below_diag, scores, 0.0)
    present_position = jnp.sum(acceptor_vectors * reward_addend * address_vectors, axis=-1)
    update_results = jnp.einsum("ghts,gshj->gthj", scores, content_vectors, precision=highest)
    update_results = update_results + present_position[..., None] * content_vectors
    update_results = update_results + jnp.einsum(
        "gthi,ghij->gthj", decayed, running_memory, precision=highest
    )
    running_memory = jnp.exp(block_len * fading_exponent)[
        None, :, :, None
    ] * running_memory + jnp.einsum(
        "gshi,gshj->ghij", address_vectors * tail_key, content_vectors, precision=highest
    )
    return (running_memory, update_results)


def memory_recurrence_routine(
    acceptor_vectors,
    address_vectors,
    content_vectors,
    fading_exponent,
    reward_addend,
    opening_memory,
):
    groups, length = (acceptor_vectors.shape[0], acceptor_vectors.shape[1])
    blocks = length // SPAN

    def arrange(tensor):
        return jnp.moveaxis(tensor.reshape(groups, blocks, SPAN, MIXER_LANES, LANE_SIZE), 1, 0)

    recurrence_update = jax.checkpoint(
        lambda running_memory, result_fragments: memory_segment_routine(
            running_memory, result_fragments, fading_exponent, reward_addend
        )
    )
    last_state, update_results = lax.scan(
        recurrence_update,
        opening_memory,
        (arrange(acceptor_vectors), arrange(address_vectors), arrange(content_vectors)),
    )
    return jnp.moveaxis(update_results, 0, 1).reshape(groups, length, MIXER_LANES, LANE_SIZE)


def group_norm(update_results, scale_vec, shift_vec):
    average = jnp.mean(update_results, axis=-1, keepdims=True)
    centred = update_results - average
    variance = jnp.mean(centred * centred, axis=-1, keepdims=True)
    scaled = (centred * lax.rsqrt(variance + group_eps)).reshape(
        update_results.shape[:-2] + (MIXER_LANES * LANE_SIZE,)
    )
    return scaled * scale_vec + shift_vec


def attention_inputs(
    tokens,
    prior_standardize_factor,
    prior_standardize_offset,
    acceptor_lerp_factor,
    address_lerp_factor,
    content_lerp_factor,
    sigmoid_lerp_factor,
):
    normed = layer_norm(tokens, prior_standardize_factor, prior_standardize_offset)
    previous = time_shift(normed)
    return (
        blend(normed, previous, acceptor_lerp_factor),
        blend(normed, previous, address_lerp_factor),
        blend(normed, previous, content_lerp_factor),
        blend(normed, previous, sigmoid_lerp_factor),
    )


def mixer_routine(
    opening_memory,
    acceptor_vectors,
    address_vectors,
    content_vectors,
    sigmoid_preactivation,
    lane_fading_exponent,
    present_reward_vector,
    cluster_standardize_factor,
    cluster_standardize_offset,
):
    divide_among_lanes = acceptor_vectors.shape[:-1] + (MIXER_LANES, LANE_SIZE)
    fading_exponent = -jnp.exp(lane_fading_exponent.reshape(MIXER_LANES, LANE_SIZE))
    update_results = memory_recurrence_routine(
        acceptor_vectors.reshape(divide_among_lanes),
        address_vectors.reshape(divide_among_lanes),
        content_vectors.reshape(divide_among_lanes),
        fading_exponent,
        present_reward_vector.reshape(MIXER_LANES, LANE_SIZE),
        opening_memory,
    )
    grouped = group_norm(update_results, cluster_standardize_factor, cluster_standardize_offset)
    return grouped * jax.nn.silu(sigmoid_preactivation)


def channel_inputs(
    middle,
    latter_standardize_factor,
    latter_standardize_offset,
    feedforward_address_lerp,
    feedforward_sigmoid_lerp,
):
    normed_mid = layer_norm(middle, latter_standardize_factor, latter_standardize_offset)
    previous_mid = time_shift(normed_mid)
    return (
        blend(normed_mid, previous_mid, feedforward_address_lerp),
        blend(normed_mid, previous_mid, feedforward_sigmoid_lerp),
    )


def per_device(
    incoming_activations,
    sequence_opening_memory,
    prior_standardize_factor,
    prior_standardize_offset,
    acceptor_lerp_factor,
    address_lerp_factor,
    content_lerp_factor,
    sigmoid_lerp_factor,
    acceptor_matrix,
    address_matrix,
    content_matrix,
    sigmoid_matrix,
    lane_fading_exponent,
    present_reward_vector,
    cluster_standardize_factor,
    cluster_standardize_offset,
    mixer_result_matrix,
    latter_standardize_factor,
    latter_standardize_offset,
    feedforward_address_lerp,
    feedforward_sigmoid_lerp,
    feedforward_address_matrix,
    feedforward_content_matrix,
    feedforward_acceptor_matrix,
    upstream_derivative,
):
    mix_full = (
        lax.all_gather(prior_standardize_factor, ("dp", "fsdp"), axis=0, tiled=True),
        lax.all_gather(prior_standardize_offset, ("dp", "fsdp"), axis=0, tiled=True),
        lax.all_gather(acceptor_lerp_factor, ("dp", "fsdp"), axis=0, tiled=True),
        lax.all_gather(address_lerp_factor, ("dp", "fsdp"), axis=0, tiled=True),
        lax.all_gather(content_lerp_factor, ("dp", "fsdp"), axis=0, tiled=True),
        lax.all_gather(sigmoid_lerp_factor, ("dp", "fsdp"), axis=0, tiled=True),
        lax.all_gather(acceptor_matrix, ("dp", "fsdp"), axis=0, tiled=True),
        lax.all_gather(address_matrix, ("dp", "fsdp"), axis=0, tiled=True),
        lax.all_gather(content_matrix, ("dp", "fsdp"), axis=0, tiled=True),
        lax.all_gather(sigmoid_matrix, ("dp", "fsdp"), axis=0, tiled=True),
        lax.all_gather(lane_fading_exponent, ("dp", "fsdp"), axis=0, tiled=True),
        lax.all_gather(present_reward_vector, ("dp", "fsdp"), axis=0, tiled=True),
        lax.all_gather(cluster_standardize_factor, ("dp", "fsdp"), axis=0, tiled=True),
        lax.all_gather(cluster_standardize_offset, ("dp", "fsdp"), axis=0, tiled=True),
        lax.all_gather(mixer_result_matrix, ("dp", "fsdp"), axis=0, tiled=True),
    )
    front_vectors = tuple(
        (recurrence_element.astype(jnp.float32) for recurrence_element in mix_full[0:6])
    )
    core_vectors = tuple(
        (recurrence_element.astype(jnp.float32) for recurrence_element in mix_full[10:14])
    )
    mix_matrices = mix_full[6:10] + (mix_full[14],)
    length = incoming_activations.shape[0]
    tokens = incoming_activations.astype(jnp.float32).reshape(1, length, -1)
    blended, pull_front = jax.vjp(attention_inputs, tokens, *front_vectors)
    blended_low = tuple((recurrence_element.astype(jnp.bfloat16) for recurrence_element in blended))
    projected = tuple((matmul(left, right) for left, right in zip(blended_low, mix_matrices[0:4])))
    masked_result, pull_core = jax.vjp(
        partial(mixer_routine, sequence_opening_memory), *projected, *core_vectors
    )
    gated_low = masked_result.astype(jnp.bfloat16)
    middle = tokens + matmul(gated_low, mix_matrices[4])
    ffn_full = (
        lax.all_gather(latter_standardize_factor, ("dp", "fsdp"), axis=0, tiled=True),
        lax.all_gather(latter_standardize_offset, ("dp", "fsdp"), axis=0, tiled=True),
        lax.all_gather(feedforward_address_lerp, ("dp", "fsdp"), axis=0, tiled=True),
        lax.all_gather(feedforward_sigmoid_lerp, ("dp", "fsdp"), axis=0, tiled=True),
        lax.all_gather(feedforward_address_matrix, ("dp", "fsdp"), axis=0, tiled=True),
        lax.all_gather(feedforward_content_matrix, ("dp", "fsdp"), axis=0, tiled=True),
        lax.all_gather(feedforward_acceptor_matrix, ("dp", "fsdp"), axis=0, tiled=True),
    )
    back_vectors = tuple(
        (recurrence_element.astype(jnp.float32) for recurrence_element in ffn_full[0:4])
    )
    ffn_matrices = ffn_full[4:7]
    channel_in, pull_channel = jax.vjp(channel_inputs, middle, *back_vectors)
    hidden_in = channel_in[0].astype(jnp.bfloat16)
    gating_in = channel_in[1].astype(jnp.bfloat16)
    pre_hidden = matmul(hidden_in, ffn_matrices[0])
    hidden_low = jnp.square(jax.nn.relu(pre_hidden)).astype(jnp.bfloat16)
    value_out = matmul(hidden_low, ffn_matrices[1])
    gating = jax.nn.sigmoid(matmul(gating_in, ffn_matrices[2]))
    layer_output = middle + gating * value_out
    ffn_back = (
        lax.all_gather(feedforward_address_matrix, ("dp", "fsdp"), axis=0, tiled=True),
        lax.all_gather(feedforward_content_matrix, ("dp", "fsdp"), axis=0, tiled=True),
        lax.all_gather(feedforward_acceptor_matrix, ("dp", "fsdp"), axis=0, tiled=True),
    )
    upstream = upstream_derivative.astype(jnp.float32).reshape(1, length, -1)
    grad_value_out = (upstream * gating).astype(jnp.bfloat16)
    grad_gating_pre = (upstream * value_out * gating * (1.0 - gating)).astype(jnp.bfloat16)
    grad_value_mat = weight_grad(hidden_low, grad_value_out)
    grad_gate_mat = weight_grad(gating_in, grad_gating_pre)
    grad_hidden = input_grad_of(grad_value_out, ffn_back[1])
    grad_pre_hidden = (grad_hidden * 2.0 * jax.nn.relu(pre_hidden)).astype(jnp.bfloat16)
    grad_key_mat = weight_grad(hidden_in, grad_pre_hidden)
    channel_grads = pull_channel(
        (input_grad_of(grad_pre_hidden, ffn_back[0]), input_grad_of(grad_gating_pre, ffn_back[2]))
    )
    grad_middle = upstream + channel_grads[0]
    ffn_members = (
        channel_grads[1],
        channel_grads[2],
        channel_grads[3],
        channel_grads[4],
        grad_key_mat,
        grad_value_mat,
        grad_gate_mat,
    )
    ffn_shares = owner_sums(ffn_members)
    mix_back = (
        lax.all_gather(acceptor_matrix, ("dp", "fsdp"), axis=0, tiled=True),
        lax.all_gather(address_matrix, ("dp", "fsdp"), axis=0, tiled=True),
        lax.all_gather(content_matrix, ("dp", "fsdp"), axis=0, tiled=True),
        lax.all_gather(sigmoid_matrix, ("dp", "fsdp"), axis=0, tiled=True),
        lax.all_gather(mixer_result_matrix, ("dp", "fsdp"), axis=0, tiled=True),
    )
    grad_attn = grad_middle.astype(jnp.bfloat16)
    grad_out_mat = weight_grad(gated_low, grad_attn)
    grad_gated = input_grad_of(grad_attn, mix_back[4])
    core_grads = pull_core(grad_gated)
    grads_low = tuple(
        (recurrence_element.astype(jnp.bfloat16) for recurrence_element in core_grads[0:4])
    )
    proj_grads = tuple((weight_grad(left, right) for left, right in zip(blended_low, grads_low)))
    front_in = tuple((input_grad_of(left, right) for left, right in zip(grads_low, mix_back[0:4])))
    front_grads = pull_front(front_in)
    input_grad = grad_middle + front_grads[0]
    mix_members = (
        front_grads[1],
        front_grads[2],
        front_grads[3],
        front_grads[4],
        front_grads[5],
        front_grads[6],
        proj_grads[0],
        proj_grads[1],
        proj_grads[2],
        proj_grads[3],
        core_grads[4],
        core_grads[5],
        core_grads[6],
        core_grads[7],
        grad_out_mat,
    )
    shares = owner_sums(mix_members) + ffn_shares
    return (
        layer_output.reshape(length, -1),
        input_grad.reshape(length, -1),
        shares[0],
        shares[1],
        shares[2],
        shares[3],
        shares[4],
        shares[5],
        shares[6],
        shares[7],
        shares[8],
        shares[9],
        shares[10],
        shares[11],
        shares[12],
        shares[13],
        shares[14],
        shares[15],
        shares[16],
        shares[17],
        shares[18],
        shares[19],
        shares[20],
        shares[21],
    )


def solution(mesh):
    return jax.shard_map(
        per_device,
        mesh=mesh,
        in_specs=(
            P(("dp", "fsdp"), None),
            P(("dp", "fsdp"), None, None, None),
            P(("dp", "fsdp")),
            P(("dp", "fsdp")),
            P(("dp", "fsdp")),
            P(("dp", "fsdp")),
            P(("dp", "fsdp")),
            P(("dp", "fsdp")),
            P(("dp", "fsdp"), None),
            P(("dp", "fsdp"), None),
            P(("dp", "fsdp"), None),
            P(("dp", "fsdp"), None),
            P(("dp", "fsdp")),
            P(("dp", "fsdp")),
            P(("dp", "fsdp")),
            P(("dp", "fsdp")),
            P(("dp", "fsdp"), None),
            P(("dp", "fsdp")),
            P(("dp", "fsdp")),
            P(("dp", "fsdp")),
            P(("dp", "fsdp")),
            P(("dp", "fsdp"), None),
            P(("dp", "fsdp"), None),
            P(("dp", "fsdp"), None),
            P(("dp", "fsdp"), None),
        ),
        out_specs=(
            P(("dp", "fsdp"), None),
            P(("dp", "fsdp"), None),
            P(("dp", "fsdp")),
            P(("dp", "fsdp")),
            P(("dp", "fsdp")),
            P(("dp", "fsdp")),
            P(("dp", "fsdp")),
            P(("dp", "fsdp")),
            P(("dp", "fsdp"), None),
            P(("dp", "fsdp"), None),
            P(("dp", "fsdp"), None),
            P(("dp", "fsdp"), None),
            P(("dp", "fsdp")),
            P(("dp", "fsdp")),
            P(("dp", "fsdp")),
            P(("dp", "fsdp")),
            P(("dp", "fsdp"), None),
            P(("dp", "fsdp")),
            P(("dp", "fsdp")),
            P(("dp", "fsdp")),
            P(("dp", "fsdp")),
            P(("dp", "fsdp"), None),
            P(("dp", "fsdp"), None),
            P(("dp", "fsdp"), None),
        ),
        check_vma=False,
    )
```

profile of v0, /device:TPU:1, one launch (start us, length us, event | category | flops | bytes accessed | tf_op | source)
XLA Modules:
  0.0 2901.9 jit_solution(2185395370427259684)
XLA Ops:
  24.9 69.9 %all-reduce.48 = (bf16[768]{0:T(1024)(128)(2,1)S(1)}, bf16[768]{0:T(1024)(128)(2,1)S(1)}, bf16[768]{0:T(1024)(128)(2,1)S(1)}, bf16[768]{0:T(1024)(128)(2,1)S(1)}...) all-reduce(bf16[768]{0:T(1024)(128)(2,1)S(1)} %dynamic-update-slice, ...), channel_id=1, replica_groups=mesh['dp'=8,'fsdp'=16] {'dp','fsdp'}, use_global_device_ids=true, to_apply=%add.4 | all-reduce | flops 10752 | bytes 43008
  106.1 100.2 %all-gather.19.cloned.1.call-done = bf16[128,6,768]{2,1,0:T(8,128)(2,1)} async-done(((bf16[1,6,768]{2,1,0:T(8,128)(2,1)}), bf16[128,6,768]{2,1,0:T(8,128)(2,1)}) %all-gather.19.cloned.1.call-update) | async-done | bytes 1179664 | tf_op jit(solution)/shard_map/all_gather | solution.py:210
  210.2 189.7 %all-gather.17.cloned.1.call-done = bf16[128,6,768]{2,1,0:T(8,128)(2,1)} async-done(((bf16[1,6,768]{2,1,0:T(8,128)(2,1)}), bf16[128,6,768]{2,1,0:T(8,128)(2,1)}) %all-gather.17.cloned.1.call-update) | async-done | bytes 1179664 | tf_op jit(solution)/shard_map/all_gather | solution.py:209
  403.8 189.8 %all-gather.21.cloned.1.call-done = bf16[128,6,768]{2,1,0:T(8,128)(2,1)} async-done(((bf16[1,6,768]{2,1,0:T(8,128)(2,1)}), bf16[128,6,768]{2,1,0:T(8,128)(2,1)}) %all-gather.21.cloned.1.call-update) | async-done | bytes 1179664 | tf_op jit(solution)/shard_map/all_gather | solution.py:208
  601.6 19.7 while.45
  634.3 152.9 %all-gather.23.cloned.1.call-done = bf16[128,6,768]{2,1,0:T(8,128)(2,1)} async-done(((bf16[1,6,768]{2,1,0:T(8,128)(2,1)}), bf16[128,6,768]{2,1,0:T(8,128)(2,1)}) %all-gather.23.cloned.1.call-update) | async-done | bytes 1179664 | tf_op jit(solution)/shard_map/all_gather | solution.py:211
  790.4 190.3 %all-gather.25.cloned.1.call-done = bf16[128,6,768]{2,1,0:T(8,128)(2,1)} async-done(((bf16[1,6,768]{2,1,0:T(8,128)(2,1)}), bf16[128,6,768]{2,1,0:T(8,128)(2,1)}) %all-gather.25.cloned.1.call-update) | async-done | bytes 1179664 | tf_op jit(solution)/shard_map/all_gather | solution.py:216
  984.1 190.1 %all-gather.27.cloned.1.call-done = bf16[128,6,768]{2,1,0:T(8,128)(2,1)} async-done(((bf16[1,6,768]{2,1,0:T(8,128)(2,1)}), bf16[128,6,768]{2,1,0:T(8,128)(2,1)}) %all-gather.27.cloned.1.call-update) | async-done | bytes 1179664 | tf_op jit(solution)/shard_map/all_gather | solution.py:242
  1182.2 192.6 %all-gather.29.cloned.1.call-done = bf16[128,6,2688]{2,1,0:T(8,128)(2,1)} async-done(((bf16[1,6,2688]{2,1,0:T(8,128)(2,1)}), bf16[128,6,2688]{2,1,0:T(8,128)(2,1)}) %all-gather.29.cloned.1.call-update) | async-done | bytes 4128784 | tf_op jit(solution)/shard_map/all_gather | solution.py:240
  1374.9 7.3 reshape.1208
  1386.3 188.7 %all-gather.31.cloned.1.call-done = bf16[128,21,768]{2,1,0:T(8,128)(2,1)} async-done(((bf16[1,21,768]{2,1,0:T(8,128)(2,1)}), bf16[128,21,768]{2,1,0:T(8,128)(2,1)}) %all-gather.31.cloned.1.call-update) | async-done | bytes 4128784 | tf_op jit(solution)/shard_map/all_gather | solution.py:241
  1575.0 7.2 reshape.1210
  1616.8 39.0 %while.44 = (s32[]{:T(128)}, f32[12,64]{1,0:T(8,128)}, f32[12,64]{1,0:T(8,128)}, f32[1,12,64,64]{2,3,1,0:T(8,128)}, bf16[2,1,64,12,64]{4,2,3,1,0:T(8,128)(2,1)},...) while((s32[]{:T(128)}, f32[12,64]{1,0:T(8,128)}, ...), condition=%wide.region_21.22_spmd.clone.clone, body=%wide.region_13.0_spmd.clone.sunk.clone | while | flops 342645312 | bytes 20061820 | solution.py:97
  1666.9 410.2 %fusion.183 = (f32[8,768]{1,0:T(8,128)S(1)}, f32[8,768]{1,0:T(8,128)S(1)}, f32[8,768]{1,0:T(8,128)S(1)}, f32[8,768]{1,0:T(8,128)}, f32[8,768]{1,0:T(8,128)S(1)}, /*index=5*/f32[24,768]{1,0:T(8,128)}, f32[8,768]{1,0:T(8,128)S(1)}) fusion(f32[768,768]{1,0:T(8,128)} %fusion.163, f32[768,768]{1,0:T(8,128)} %fusion.161, f32[768,768]{1,0:T(8,128)} %fusion.159, ...), kind=kCustom, calls=%all-reduce-scatter.7 | all-reduce-scatter fusion | flops 7077890 | bytes 22634496
  2087.2 9.4 collective-permute-start.29
  2104.5 9.9 collective-permute-start.22
  2405.2 6.4 collective-permute-start.97
  2571.0 63.0 %all-reduce.47 = (f32[768]{0:T(1024)S(1)}, f32[768]{0:T(1024)S(1)}, f32[768]{0:T(1024)S(1)}, f32[768]{0:T(1024)S(1)}, f32[768]{0:T(1024)S(1)}, /*index=5*/f32[76...) all-reduce(f32[768]{0:T(1024)S(1)} %get-tuple-element.707, ...), channel_id=2, replica_groups=mesh['dp'=8,'fsdp'=16] {'dp','fsdp'}, use_global_device_ids=true, to_apply=%region_25.26.clone | all-reduce | flops 10752 | bytes 86016
  2643.3 6.4 concatenate.8
  2649.8 26.5 concatenate.9
  2676.5 26.5 concatenate.10
  2703.3 46.3 %concatenate.11 = f32[262,768]{1,0:T(8,128)} concatenate(f32[6,768]{1,0:T(8,128)S(1)} %copy-done.152, f32[8,768]{1,0:T(8,128)} %collective-permute-done.126, f32[8,768]{1,0:T(8,128)} %collective-permute-done.125, f32[8,768]{1,0:T(8,128)} %collective-permute-done.124, f32[8,768]{1,0:T(8,128)} %collective-permute-done.123, f32[8,768]{1,0:T(8,128)} %collective-permute-done.122, ...), dimensions={0} | concatenate | bytes 1609728
  2749.6 25.7 concatenate.12
  2792.5 46.6 %concatenate.14 = f32[262,768]{1,0:T(8,128)} concatenate(f32[6,768]{1,0:T(8,128)S(1)} %copy-done.148, f32[8,768]{1,0:T(8,128)} %copy-done.288, f32[8,768]{1,0:T(8,128)} %copy-done.289, f32[8,768]{1,0:T(8,128)} %copy-done.290, f32[8,768]{1,0:T(8,128)} %copy-done.291, f32[8,768]{1,0:T(8,128)} %copy-done.292, f32[8,768]{1,0:T(8,128)} %copy-done.293, f32[8,768]{1,0:T(8,128)} %copy-done.294, ...), dimensions={0} | concatenate | bytes 1609728
  (1385 shorter events, 724.9 us)
Async XLA Ops:
  7.2 199.1 %all-gather.19.cloned.1.call-start = ((), (), s32[]{:S(2)}) async-start(), calls=%async_computation.1 | async-start | bytes 1585152 | tf_op jit(solution)/shard_map/all_gather | solution.py:210
  7.9 392.0 %all-gather.17.cloned.1.call-start = ((), (), s32[]{:S(2)}) async-start(), calls=%async_computation | async-start | bytes 1585152 | tf_op jit(solution)/shard_map/all_gather | solution.py:209
  8.7 584.9 %all-gather.21.cloned.1.call-start = ((), (), s32[]{:S(2)}) async-start(), calls=%async_computation.2 | async-start | bytes 1585152 | tf_op jit(solution)/shard_map/all_gather | solution.py:208
  9.4 777.8 %all-gather.23.cloned.1.call-start = ((), (), s32[]{:S(2)}) async-start(), calls=%async_computation.3 | async-start | bytes 1585152 | tf_op jit(solution)/shard_map/all_gather | solution.py:211
  10.0 970.7 %all-gather.25.cloned.1.call-start = ((), (), s32[]{:S(2)}) async-start(), calls=%async_computation.4 | async-start | bytes 1585152 | tf_op jit(solution)/shard_map/all_gather | solution.py:216
  10.6 1163.6 %all-gather.27.cloned.1.call-start = ((), (), s32[]{:S(2)}) async-start(), calls=%async_computation.5 | async-start | bytes 1585152 | tf_op jit(solution)/shard_map/all_gather | solution.py:242
  11.2 1363.7 %all-gather.29.cloned.1.call-start = ((), (), s32[]{:S(2)}) async-start(), calls=%async_computation.6 | async-start | bytes 5548032 | tf_op jit(solution)/shard_map/all_gather | solution.py:240
  11.9 1563.0 %all-gather.31.cloned.1.call-start = ((), (), s32[]{:S(2)}) async-start(), calls=%async_computation.7 | async-start | bytes 4755456 | tf_op jit(solution)/shard_map/all_gather | solution.py:241
  12.7 2881.0 %all-reduce.52.cloned.1.call-start = ((), (), s32[]{:S(2)}) async-start(), calls=%async_computation.8 | async-start | bytes 16515072
  2079.8 20.7 collective-permute-start.30
  2552.4 223.0 %collective-permute-start.180 = (f32[8,768]{1,0:T(8,128)S(1)}, f32[8,768]{1,0:T(8,128)}, u32[]{:S(2)}, u32[]{:S(2)}) collective-permute-start(f32[8,768]{1,0:T(8,128)S(1)} %copy-done.89), channel_id=1, source_target_pairs={{0,5},{1,6},{2,7},{3,8},{4,9},{5,10},{6,11},{7,12},{8,13},{9,14},{... | collective-permute-start | bytes 73736
  2557.4 221.4 %collective-permute-start.179 = (f32[8,768]{1,0:T(8,128)S(1)}, f32[8,768]{1,0:T(8,128)}, u32[]{:S(2)}, u32[]{:S(2)}) collective-permute-start(f32[8,768]{1,0:T(8,128)S(1)} %copy-done.89), channel_id=1, source_target_pairs={{0,4},{1,5},{2,6},{3,7},{4,8},{5,9},{6,10},{7,11},{8,12},{9,13},{1... | collective-permute-start | bytes 73736
  2559.3 224.0 %collective-permute-start.178 = (f32[8,768]{1,0:T(8,128)S(1)}, f32[8,768]{1,0:T(8,128)}, u32[]{:S(2)}, u32[]{:S(2)}) collective-permute-start(f32[8,768]{1,0:T(8,128)S(1)} %copy-done.89), channel_id=1, source_target_pairs={{0,3},{1,4},{2,5},{3,6},{4,7},{5,8},{6,9},{7,10},{8,11},{9,12},{10... | collective-permute-start | bytes 73736
  2561.2 225.2 %collective-permute-start.177 = (f32[8,768]{1,0:T(8,128)S(1)}, f32[8,768]{1,0:T(8,128)}, u32[]{:S(2)}, u32[]{:S(2)}) collective-permute-start(f32[8,768]{1,0:T(8,128)S(1)} %copy-done.89), channel_id=1, source_target_pairs={{0,2},{1,3},{2,4},{3,5},{4,6},{5,7},{6,8},{7,9},{8,10},{9,11},{10,... | collective-permute-start | bytes 73736
  2566.8 223.6 %collective-permute-start.176 = (f32[8,768]{1,0:T(8,128)S(1)}, f32[8,768]{1,0:T(8,128)}, u32[]{:S(2)}, u32[]{:S(2)}) collective-permute-start(f32[8,768]{1,0:T(8,128)S(1)} %copy-done.89), channel_id=1, source_target_pairs={{0,1},{1,2},{2,3},{3,4},{4,5},{5,6},{6,7},{7,8},{8,9},{9,10},{10,1... | collective-permute-start | bytes 73736
  2775.3 70.7 %collective-permute-start.174 = (f32[24,768]{1,0:T(8,128)S(1)}, f32[24,768]{1,0:T(8,128)S(1)}, u32[]{:S(2)}, u32[]{:S(2)}) collective-permute-start(f32[24,768]{1,0:T(8,128)S(1)} %copy-done.70), channel_id=1, source_target_pairs={{0,15},{1,16},{2,17},{3,18},{4,19},{5,20},{6,21},{7,22},{8,23},{9,... | collective-permute-start | bytes 221192
  2778.9 71.2 %collective-permute-start.173 = (f32[24,768]{1,0:T(8,128)S(1)}, f32[24,768]{1,0:T(8,128)S(1)}, u32[]{:S(2)}, u32[]{:S(2)}) collective-permute-start(f32[24,768]{1,0:T(8,128)S(1)} %copy-done.70), channel_id=1, source_target_pairs={{0,14},{1,15},{2,16},{3,17},{4,18},{5,19},{6,20},{7,21},{8,22},{9,... | collective-permute-start | bytes 221192
  2783.3 72.3 %collective-permute-start.172 = (f32[24,768]{1,0:T(8,128)S(1)}, f32[24,768]{1,0:T(8,128)}, u32[]{:S(2)}, u32[]{:S(2)}) collective-permute-start(f32[24,768]{1,0:T(8,128)S(1)} %copy-done.70), channel_id=1, source_target_pairs={{0,13},{1,14},{2,15},{3,16},{4,17},{5,18},{6,19},{7,20},{8,21},{9,... | collective-permute-start | bytes 221192
  2786.4 73.8 %collective-permute-start.171 = (f32[24,768]{1,0:T(8,128)S(1)}, f32[24,768]{1,0:T(8,128)}, u32[]{:S(2)}, u32[]{:S(2)}) collective-permute-start(f32[24,768]{1,0:T(8,128)S(1)} %copy-done.70), channel_id=1, source_target_pairs={{0,12},{1,13},{2,14},{3,15},{4,16},{5,17},{6,18},{7,19},{8,20},{9,... | collective-permute-start | bytes 221192
  2790.4 50.5 %collective-permute-start.175 = (f32[21,768]{1,0:T(8,128)}, f32[21,768]{1,0:T(8,128)}, u32[]{:S(2)}, u32[]{:S(2)}) collective-permute-start(f32[21,768]{1,0:T(8,128)} %slice.15), channel_id=1, source_target_pairs={{0,16},{1,17},{2,18},{3,19},{4,20},{5,21},{6,22},{7,23},{8,24},{9,... | collective-permute-start | bytes 193544
  2840.9 20.6 collective-permute-start.170
  2846.0 20.8 collective-permute-start.169
  2850.1 22.3 collective-permute-start.168
  2866.8 21.3 collective-permute-start.164
  (540 other events, 32219.5 us)
Sparse Core Ops, SparseCore 0:
  9.8 196.4 all-gather.18
  208.0 191.8 all-gather.16
  401.7 191.9 all-gather.20
  595.2 191.9 all-gather.22
  788.7 191.8 all-gather.24
  982.3 191.9 all-gather.26
  1175.9 198.8 all-gather.28
  1376.6 198.3 all-gather.30
  2374.9 156.6 all-reduce.51
where the time goes:
time: 2930 us; the launch traced here: 2900 us
  waiting for transfers between devices  1400 us (48%)
  blocking collectives  543 us (19%)
  starting transfers between devices  534 us (18%)
  local copies, waits for them, and re-layouts  297 us (10%)
  matrix products  75.5 us (3%)
  other arithmetic  30.7 us (1%)
    unnamed x3, blocking collectives  543 us
    unnamed x209, starting transfers between devices  534 us
    unnamed x666, local copies, waits for them, and re-layouts  251 us
    all_gather x1, waiting for transfers between devices, per_device(): lax.all_gather(feedforward_address_matrix, ('dp', 'fsdp'), axis=0, tiled=...  193 us
    all_gather x1, waiting for transfers between devices, per_device(): lax.all_gather(mixer_result_matrix, ('dp', 'fsdp'), axis=0, tiled=True)  190 us
    all_gather x1, waiting for transfers between devices, per_device(): lax.all_gather(feedforward_acceptor_matrix, ('dp', 'fsdp'), axis=0, tiled...  190 us
    all_gather x1, waiting for transfers between devices, per_device(): lax.all_gather(acceptor_matrix, ('dp', 'fsdp'), axis=0, tiled=True)  190 us
    all_gather x1, waiting for transfers between devices, per_device(): lax.all_gather(address_matrix, ('dp', 'fsdp'), axis=0, tiled=True)  190 us
  transfers between devices with their start and end apart: 217, of which 8 were waited for; matrix products, arithmetic and copies ran while one was open for 11% of the time, Pallas kernels for 0%

commit v1 on v0

v1 whole, which is shorter than its diff:
```python
from functools import partial

import jax
import jax.numpy as jnp
import numpy as np
from jax import lax
from jax.experimental import pallas as pl
from jax.experimental.pallas import tpu as pltpu
from jax.sharding import PartitionSpec as P

MESH = pl.DeviceIdType.MESH
BF = jnp.bfloat16
F32 = jnp.float32
HIGHEST = lax.Precision.HIGHEST
VMEM = pl.BlockSpec(memory_space=pltpu.VMEM)
ANY = pl.BlockSpec(memory_space=pl.ANY)

NORM_EPS = 1e-05
GROUP_EPS = 0.00064
TOK = 128
EMB = 768
HALF = 3328
COLS = 384
W1A, W1B = 1408, 1280
FF = 2688
VEC = 3200


def _order():
    order = np.zeros(EMB, np.int64)
    for x in range(4):
        for y in range(4):
            for z in range(4):
                for c in range(2):
                    device = z * 32 + (x % 2) * 16 + y * 4 + (x // 2) * 2 + c
                    place = (x * 4 + y) * 48 + (z * 2 + c) * 6
                    order[place : place + 6] = 6 * device + np.arange(6)
    return order


def _spread():
    spread = np.zeros((EMB, EMB), np.float32)
    spread[_order(), np.arange(EMB)] = 1.0
    return spread


def _line_pick():
    pick = np.zeros((48, 64), np.float32)
    for z in range(4):
        for c in range(2):
            for r in range(6):
                pick[(z * 2 + c) * 6 + r, z * 16 + c * 8 + r] = 1.0
    return pick


def _plane_pick():
    pick = np.zeros((432, 512), np.float32)
    for chip in range(8):
        for c in range(2):
            base = chip * 64 + c * 32
            for r in range(6):
                pick[(chip * 2 + c) * 6 + r, base + r] = 1.0
            for r in range(21):
                pick[96 + (chip * 2 + c) * 21 + r, base + 6 + r] = 1.0
    return pick


def rem4(value):
    return lax.rem(value, 4)


class Place:
    def __init__(self):
        dp, fs = lax.axis_index("dp"), lax.axis_index("fsdp")
        self.z, self.xlo = lax.div(dp, 2), lax.rem(dp, 2)
        self.y, self.xhi = lax.div(fs, 4), lax.rem(lax.div(fs, 2), 2)
        self.c = lax.rem(fs, 2)
        self.x = self.xhi * 2 + self.xlo
        self.dp = dp

    def device(self, z, y, x, c):
        return (z * 2 + lax.rem(x, 2), y * 4 + lax.div(x, 2) * 2 + c)

    def sibling(self):
        return self.device(self.z, self.y, self.x, 1 - self.c)

    def up(self, k):
        return self.device(rem4(self.z + k), self.y, self.x, self.c)

    def first(self, k):
        y, x = rem4(self.y + k * (1 - self.c)), rem4(self.x + k * self.c)
        return self.device(self.z, y, x, self.c)

    def last(self, k):
        y, x = rem4(self.y + k * self.c), rem4(self.x + k * (1 - self.c))
        return self.device(self.z, y, x, self.c)

    def slot(self, m, k, core=None):
        c = self.c if core is None else core
        x = rem4(self.x + m * c + k * (1 - c))
        y = rem4(self.y + m * (1 - c) + k * c)
        return x * 4 + y

    def plane(self, k):
        index = lax.rem(self.y * 2 + self.xhi + k, 8)
        y, xhi = lax.div(index, 2), lax.rem(index, 2)
        return self.device(self.z, y, xhi * 2 + self.xlo, self.c), index

    def twin(self):
        return self.device(self.z, self.y, self.xhi * 2 + 1 - self.xlo, self.c)

    def meet(self):
        barrier = pltpu.get_barrier_semaphore()
        mates = [self.sibling(), self.twin()]
        mates += [self.up(k) for k in (1, 2, 3)]
        mates += [self.first(k) for k in (1, 2, 3)]
        mates += [self.last(k) for k in (1, 2, 3)]
        mates += [self.plane(k)[0] for k in range(1, 8)]
        for mate in mates:
            pl.semaphore_signal(barrier, inc=1, device_id=mate, device_id_type=MESH)
        pl.semaphore_wait(barrier, len(mates))


class Sender:
    def __init__(self, send_sems, recv_sems):
        self.send_sems, self.recv_sems = send_sems, recv_sems
        self.started = []

    def send(self, source, target, device):
        index = len(self.started)
        copy = pltpu.make_async_remote_copy(
            src_ref=source,
            dst_ref=target,
            send_sem=self.send_sems.at[index],
            recv_sem=self.recv_sems.at[index],
            device_id=device,
            device_id_type=MESH,
        )
        copy.start()
        self.started.append(copy)
        return copy

    def finish(self):
        for copy in self.started:
            copy.wait_send()


def rows(start, size, unit=16):
    return pl.ds(pl.multiple_of(start, unit), size)


GATHER_COPIES = 96


def gather_kernel(
    pack_n, pack_z, pick_n, pick_z, out_n, out_o, out_2,
    got_n, stage_n, block_n, half_z, stage_z, block_o, block_2,
    send_sems, recv_sems, local_sems,
):
    at = Place()
    c = at.c
    at.meet()
    net = Sender(send_sems, recv_sems)
    sib = at.sibling()

    swap_n = net.send(pack_n.at[1 - c], got_n, sib)
    swap_z = net.send(pack_z.at[1 - c], half_z.at[c], sib)
    half_z[c] = pack_z[c]
    swap_n.wait_recv()
    stage_n[at.z] = pack_n[c] + got_n[...]
    ups = [net.send(stage_n.at[at.z], stage_n.at[at.z], at.up(k)) for k in (1, 2, 3)]
    swap_z.wait_recv()
    mine = at.y * 2 + at.xhi
    planes = []
    for k in range(1, 8):
        mate, _ = at.plane(k)
        planes.append(net.send(half_z, stage_z.at[mine], mate))
    stage_z[mine] = half_z[...]

    for copy in ups:
        copy.wait_recv()
    block_n[...] = jnp.dot(
        pick_n[...], stage_n[...].reshape(64, HALF), preferred_element_type=F32
    ).astype(BF)

    def place_n(slot):
        return out_n.at[c, rows(48 * slot, 48)]

    spot = place_n(at.slot(0, 0))
    firsts = [net.send(block_n, spot, at.first(k)) for k in (1, 2, 3)]
    lasts = [[net.send(block_n, spot, at.last(k)) for k in (1, 2, 3)]]
    to_sib = [net.send(block_n, spot, sib)]
    keep_n = pltpu.make_async_copy(block_n, spot, local_sems.at[0])
    keep_n.start()

    for copy in planes:
        copy.wait_recv()
    block_z = jnp.dot(
        pick_z[...], stage_z[...].reshape(512, COLS), preferred_element_type=F32
    ).astype(BF)
    block_o[...] = block_z[:96]
    block_2[...] = block_z[96:]

    def place_o(dp):
        return out_o.at[c, rows(96 * dp, 96)]

    def place_2(dp):
        return out_2.at[c, rows(336 * dp, 336)]

    me = at.dp
    twin_o = net.send(block_o, place_o(me), at.twin())
    twin_2 = net.send(block_2, place_2(me), at.twin())
    ups_o = [[net.send(block_o, place_o(me), at.up(k)) for k in (1, 2, 3)]]
    ups_2 = [[net.send(block_2, place_2(me), at.up(k)) for k in (1, 2, 3)]]
    to_sib.append(net.send(block_o, place_o(me), sib))
    to_sib.append(net.send(block_2, place_2(me), sib))
    keep_o = pltpu.make_async_copy(block_o, place_o(me), local_sems.at[1])
    keep_2 = pltpu.make_async_copy(block_2, place_2(me), local_sems.at[2])
    keep_o.start()
    keep_2.start()

    for m in (1, 2, 3):
        firsts[m - 1].wait_recv()
        spot = place_n(at.slot(4 - m, 0))
        lasts.append([net.send(spot, spot, at.last(k)) for k in (1, 2, 3)])
        to_sib.append(net.send(spot, spot, sib))
    twin_o.wait_recv()
    twin_2.wait_recv()
    other = at.z * 2 + 1 - at.xlo
    ups_o.append([net.send(place_o(other), place_o(other), at.up(k)) for k in (1, 2, 3)])
    ups_2.append([net.send(place_2(other), place_2(other), at.up(k)) for k in (1, 2, 3)])
    to_sib.append(net.send(place_o(other), place_o(other), sib))
    to_sib.append(net.send(place_2(other), place_2(other), sib))

    for m in range(4):
        for k in (1, 2, 3):
            lasts[m][k - 1].wait_recv()
            spot = place_n(at.slot(4 - m, 4 - k))
            to_sib.append(net.send(spot, spot, sib))
    for m in range(2):
        for k in (1, 2, 3):
            z = rem4(at.z + 4 - k)
            xlo = at.xlo if m == 0 else 1 - at.xlo
            dp = z * 2 + xlo
            ups_o[m][k - 1].wait_recv()
            to_sib.append(net.send(place_o(dp), place_o(dp), sib))
            ups_2[m][k - 1].wait_recv()
            to_sib.append(net.send(place_2(dp), place_2(dp), sib))
    for copy in to_sib:
        copy.wait_recv()
    keep_n.wait()
    keep_o.wait()
    keep_2.wait()
    net.finish()


def gather(pack_n, pack_z, pick_n, pick_z):
    return pl.pallas_call(
        gather_kernel,
        out_shape=(
            jax.ShapeDtypeStruct((2, EMB, HALF), BF),
            jax.ShapeDtypeStruct((2, EMB, COLS), BF),
            jax.ShapeDtypeStruct((2, FF, COLS), BF),
        ),
        in_specs=[VMEM] * 4,
        out_specs=(ANY,) * 3,
        scratch_shapes=[
            pltpu.VMEM((16, HALF), BF),
            pltpu.VMEM((4, 16, HALF), BF),
            pltpu.VMEM((48, HALF), BF),
            pltpu.VMEM((2, 32, COLS), BF),
            pltpu.VMEM((8, 2, 32, COLS), BF),
            pltpu.VMEM((96, COLS), BF),
            pltpu.VMEM((336, COLS), BF),
            pltpu.SemaphoreType.DMA((GATHER_COPIES,)),
            pltpu.SemaphoreType.DMA((GATHER_COPIES,)),
            pltpu.SemaphoreType.DMA((3,)),
        ],
        compiler_params=pltpu.CompilerParams(
            collective_id=1, has_side_effects=True, vmem_limit_bytes=56 << 20
        ),
        name="gather_weights",
    )(pack_n, pack_z, pick_n, pick_z)


SCATTER_COPIES = 96


def scatter_kernel(
    grad_n, grad_o, grad_2, turn_n, turn_z, out_n, out_z,
    sib_n, last_n, first_n, piece_n, up_n, end_n,
    sib_o, sib_2, up_o, up_2, twin_o, twin_2, send_o, send_2, piece_z, plane_z, end_z,
    send_sems, recv_sems,
):
    at = Place()
    c = at.c
    at.meet()
    net = Sender(send_sems, recv_sems)
    sib = at.sibling()

    def band(slot):
        return rows(48 * slot, 48)

    swaps = {}
    swap_o, swap_2 = {}, {}
    for k in (1, 2, 3, 0):
        for m in range(4):
            part = band(at.slot(m, k, 1 - c))
            swaps[k, m] = net.send(grad_n.at[1 - c, part], sib_n.at[part], sib)
        z = rem4(at.z + k)
        part_o, part_2 = rows(192 * z, 192), rows(672 * z, 672)
        swap_o[k] = net.send(grad_o.at[1 - c, part_o], sib_o.at[part_o], sib)
        swap_2[k] = net.send(grad_2.at[1 - c, part_2], sib_2.at[part_2], sib)

    lasts, ups_o, ups_2 = {}, {}, {}
    for k in (1, 2, 3):
        for m in range(4):
            swaps[k, m].wait_recv()
            part = band(at.slot(m, k))
            sib_n[part] = (grad_n[c, part].astype(F32) + sib_n[part].astype(F32)).astype(BF)
            lasts[k, m] = net.send(sib_n.at[part], last_n.at[k - 1, m], at.last(k))
        z = rem4(at.z + k)
        part_o, part_2 = rows(192 * z, 192), rows(672 * z, 672)
        swap_o[k].wait_recv()
        sib_o[part_o] = (grad_o[c, part_o].astype(F32) + sib_o[part_o].astype(F32)).astype(BF)
        ups_o[k] = net.send(sib_o.at[part_o], up_o.at[k - 1], at.up(k))
        swap_2[k].wait_recv()
        sib_2[part_2] = (grad_2[c, part_2].astype(F32) + sib_2[part_2].astype(F32)).astype(BF)
        ups_2[k] = net.send(sib_2.at[part_2], up_2.at[k - 1], at.up(k))

    firsts = {}
    for m in (1, 2, 3, 0):
        swaps[0, m].wait_recv()
        part = band(at.slot(m, 0))
        total = grad_n[c, part].astype(F32) + sib_n[part].astype(F32)
        for k in (1, 2, 3):
            lasts[k, m].wait_recv()
            total += last_n[k - 1, m].astype(F32)
        if m:
            sib_n[part] = total.astype(BF)
            firsts[m] = net.send(sib_n.at[part], first_n.at[m - 1], at.first(m))
    for m in (1, 2, 3):
        firsts[m].wait_recv()
        total += first_n[m - 1].astype(F32)
    spread = jnp.dot(turn_n[...], total.astype(BF), preferred_element_type=F32)
    piece_n[...] = spread.astype(BF).reshape(4, 16, HALF)
    ups_n = {}
    for k in (1, 2, 3):
        ups_n[k] = net.send(piece_n.at[rem4(at.z + k)], up_n.at[k - 1], at.up(k))

    swap_o[0].wait_recv()
    swap_2[0].wait_recv()
    for own, away in ((False, True), (True, False)):
        xlo = at.xlo if own else 1 - at.xlo
        dp = at.z * 2 + xlo
        part_o, part_2 = rows(96 * dp, 96), rows(336 * dp, 336)
        sub_o, sub_2 = rows(96 * xlo, 96), rows(336 * xlo, 336)
        total_o = grad_o[c, part_o].astype(F32) + sib_o[part_o].astype(F32)
        total_2 = grad_2[c, part_2].astype(F32) + sib_2[part_2].astype(F32)
        for k in (1, 2, 3):
            if away:
                ups_o[k].wait_recv()
                ups_2[k].wait_recv()
            total_o += up_o[k - 1, sub_o].astype(F32)
            total_2 += up_2[k - 1, sub_2].astype(F32)
        if away:
            send_o[...] = total_o.astype(BF)
            send_2[...] = total_2.astype(BF)
            twins = [net.send(send_o, twin_o, at.twin()), net.send(send_2, twin_2, at.twin())]
    for copy in twins:
        copy.wait_recv()
    total_o += twin_o[...].astype(F32)
    total_2 += twin_2[...].astype(F32)
    spread_z = jnp.dot(turn_z[:, :96], total_o.astype(BF), preferred_element_type=F32)
    spread_z += jnp.dot(turn_z[:, 96:], total_2.astype(BF), preferred_element_type=F32)
    piece_z[...] = spread_z.astype(BF).reshape(8, 64, COLS)
    planes = []
    for k in range(1, 8):
        mate, index = at.plane(k)
        planes.append(net.send(piece_z.at[index], plane_z.at[k - 1], mate))

    total = piece_n[at.z].astype(F32)
    for k in (1, 2, 3):
        ups_n[k].wait_recv()
        total += up_n[k - 1].astype(F32)
    end_n[...] = total
    away_n, own_n = rows(8 * (1 - c), 8, 8), rows(8 * c, 8, 8)
    swap_n = net.send(end_n.at[away_n], out_n.at[c], sib)
    out_n[c] = end_n[own_n]

    total = piece_z[at.y * 2 + at.xhi].astype(F32)
    for k in range(1, 8):
        planes[k - 1].wait_recv()
        total += plane_z[k - 1].astype(F32)
    end_z[...] = total
    away_z, own_z = rows(32 * (1 - c), 32, 8), rows(32 * c, 32, 8)
    swap_z = net.send(end_z.at[away_z], out_z.at[c], sib)
    out_z[c] = end_z[own_z]
    swap_n.wait_recv()
    swap_z.wait_recv()
    net.finish()


def scatter(grad_n, grad_o, grad_2, turn_n, turn_z):
    return pl.pallas_call(
        scatter_kernel,
        out_shape=(
            jax.ShapeDtypeStruct((2, 8, HALF), F32),
            jax.ShapeDtypeStruct((2, 32, COLS), F32),
        ),
        in_specs=[VMEM] * 5,
        out_specs=(VMEM, VMEM),
        scratch_shapes=[
            pltpu.VMEM((EMB, HALF), BF),
            pltpu.VMEM((3, 4, 48, HALF), BF),
            pltpu.VMEM((3, 48, HALF), BF),
            pltpu.VMEM((4, 16, HALF), BF),
            pltpu.VMEM((3, 16, HALF), BF),
            pltpu.VMEM((16, HALF), F32),
            pltpu.VMEM((EMB, COLS), BF),
            pltpu.VMEM((FF, COLS), BF),
            pltpu.VMEM((3, 192, COLS), BF),
            pltpu.VMEM((3, 672, COLS), BF),
            pltpu.VMEM((96, COLS), BF),
            pltpu.VMEM((336, COLS), BF),
            pltpu.VMEM((96, COLS), BF),
            pltpu.VMEM((336, COLS), BF),
            pltpu.VMEM((8, 64, COLS), BF),
            pltpu.VMEM((7, 64, COLS), BF),
            pltpu.VMEM((64, COLS), F32),
            pltpu.SemaphoreType.DMA((SCATTER_COPIES,)),
            pltpu.SemaphoreType.DMA((SCATTER_COPIES,)),
        ],
        compiler_params=pltpu.CompilerParams(
            collective_id=2, has_side_effects=True, vmem_limit_bytes=56 << 20
        ),
        name="scatter_grads",
    )(grad_n, grad_o, grad_2, turn_n, turn_z)


def mm(left, right):
    return jnp.dot(left, right, preferred_element_type=F32)


def mm_t(left, right):
    return lax.dot_general(left, right, (((1,), (1,)), ((), ())), preferred_element_type=F32)


def t_mm(left, right):
    return lax.dot_general(left, right, (((0,), (0,)), ((), ())), preferred_element_type=F32)


def split(value, parts):
    found = []
    for _ in range(parts - 1):
        high = value.astype(BF)
        found.append(high)
        value = value - high.astype(F32)
    found.append(value.astype(BF))
    return found


def fine(dims, left, right):
    lh, ll = split(left, 2)
    rh, rl = split(right, 2)
    dot = partial(lax.dot_general, dimension_numbers=(dims, ((), ())), preferred_element_type=F32)
    return dot(lh, rh) + (dot(lh, rl) + dot(ll, rh))


NN, NT, TN = ((1,), (0,)), ((1,), (1,)), ((0,), (0,))


def layer_kernel(
    x_ref, up_ref, memory, spread, wn, wo, w2,
    out_ref, in_grad_ref, gn, go, g2,
    scores,
):
    lanes = lax.broadcasted_iota(jnp.int32, (1, 128), 1)
    left_head = lanes < 64
    token = lax.broadcasted_iota(jnp.int32, (TOK, 1), 0)

    def shift_down(value):
        return jnp.where(token == 0, 0.0, pltpu.roll(value, 1, 0))

    def shift_up(value):
        return jnp.where(token == TOK - 1, 0.0, pltpu.roll(value, TOK - 1, 0))

    def mean(value):
        return jnp.mean(value, axis=-1, keepdims=True)

    def tsum(value):
        return jnp.sum(value, axis=0, keepdims=True)

    def unspread(value):
        a, b, c = split(value, 3)
        return mm_t(a, spread[...]) + (mm_t(b, spread[...]) + mm_t(c, spread[...]))

    eye = (
        lax.broadcasted_iota(jnp.int32, (16, 128), 0)
        == lax.broadcasted_iota(jnp.int32, (16, 128), 1)
    ).astype(F32).astype(BF)
    vec = mm_t(eye, wn[1, :, VEC:HALF])
    gain1, bias1 = vec[0:1], vec[1:2]
    lerps = [vec[2 + i : 3 + i] for i in range(4)]
    gain2, bias2, lerp_h, lerp_g = vec[6:7], vec[7:8], vec[8:9], vec[9:10]
    heads = mm_t(vec.astype(BF), spread[...])
    rate, bonus, gain_w, bias_w = heads[10:11], heads[11:12], heads[12:13], heads[13:14]

    pair_rows = lax.broadcasted_iota(jnp.int32, (256, 128), 0)
    pair_cols = lax.broadcasted_iota(jnp.int32, (256, 128), 1)
    pair_ones = ((lax.rem(pair_rows, 128) // 64) == (pair_cols // 64)).astype(F32).astype(BF)
    below = lax.rem(pair_rows, 128) > pair_cols

    def head_sum(value):
        found = []
        for g in range(6):
            part = value[:, 128 * g : 128 * g + 128]
            found.append(mm(jnp.concatenate(split(part, 2), axis=1), pair_ones))
        return jnp.concatenate(found, axis=1)

    def stack(value):
        return jnp.concatenate(
            [jnp.where(left_head, value, 0.0), jnp.where(left_head, 0.0, value)], axis=0
        )

    def beside(value):
        return jnp.concatenate([value[:TOK], value[TOK:]], axis=1)

    tokens = mm(x_ref[...], spread[...])
    centred = tokens - mean(tokens)
    scale1 = lax.rsqrt(mean(centred * centred) + NORM_EPS)
    unit1 = centred * scale1
    normed = unit1 * gain1 + bias1
    previous = shift_down(normed)
    blended = [(normed * l + previous * (1.0 - l)).astype(BF) for l in lerps]
    recept = mm(blended[0], wn[0, :, 0:768])
    keys = mm(blended[1], wn[0, :, 768:1536])
    vals = mm(blended[2], wn[1, :, 0:768])
    gate_pre = mm(blended[3], wn[1, :, 768:1536])

    fade = -jnp.exp(rate)
    steps = token.astype(F32)
    fall_r = jnp.exp(steps * fade)
    fall_k = jnp.exp(-(steps + 1.0) * fade)
    recept_f = recept * fall_r
    keys_f = keys * fall_k
    present = head_sum(recept * bonus * keys)
    parts = []
    for g in range(6):
        cut = slice(128 * g, 128 * g + 128)
        rg, kg, vg = recept_f[:, cut], keys_f[:, cut], vals[:, cut]
        sc = jnp.where(below, fine(NT, stack(rg), kg), 0.0)
        scores[g] = sc
        parts.append(fine(NN, beside(sc), stack(vg)) + fine(NN, rg, memory[g]))
    wkv = jnp.concatenate(parts, axis=1) + present * vals

    centred_w = wkv - head_sum(wkv) * (1.0 / 64.0)
    scale_w = lax.rsqrt(head_sum(centred_w * centred_w) * (1.0 / 64.0) + GROUP_EPS)
    unit_w = centred_w * scale_w
    grouped = unit_w * gain_w + bias_w
    sig = 1.0 / (1.0 + jnp.exp(-gate_pre))
    silu = gate_pre * sig
    gated = (grouped * silu).astype(BF)
    mixed_out = jnp.concatenate([mm(gated, wo[0]), mm(gated, wo[1])], axis=1)
    middle = tokens + mixed_out

    centred = middle - mean(middle)
    scale2 = lax.rsqrt(mean(centred * centred) + NORM_EPS)
    unit2 = centred * scale2
    normed2 = unit2 * gain2 + bias2
    previous2 = shift_down(normed2)
    mixed_h = (normed2 * lerp_h + previous2 * (1.0 - lerp_h)).astype(BF)
    mixed_g = (normed2 * lerp_g + previous2 * (1.0 - lerp_g)).astype(BF)
    pre = jnp.concatenate(
        [mm(mixed_h, wn[0, :, 1536 : 1536 + W1A]), mm(mixed_h, wn[1, :, 1536 : 1536 + W1B])],
        axis=1,
    )
    pre = jnp.maximum(pre, 0.0)
    hidden = (pre * pre).astype(BF)
    value_out = jnp.concatenate([mm(hidden, w2[0]), mm(hidden, w2[1])], axis=1)
    gating = jnp.concatenate(
        [mm(mixed_g, wn[0, :, 2944:3328]), mm(mixed_g, wn[1, :, 2816:3200])], axis=1
    )
    gating = 1.0 / (1.0 + jnp.exp(-gating))
    out_ref[...] = unspread(middle + gating * value_out)

    upstream = mm(up_ref[...], spread[...])
    grad_vo = upstream * gating
    grad_gp = (grad_vo * value_out * (1.0 - gating)).astype(BF)
    grad_vo = grad_vo.astype(BF)
    for h in range(2):
        g2[h] = t_mm(hidden, grad_vo[:, COLS * h : COLS * h + COLS]).astype(BF)
    gn[0, :, 2944:3328] = t_mm(mixed_g, grad_gp[:, :COLS]).astype(BF)
    gn[1, :, 2816:3200] = t_mm(mixed_g, grad_gp[:, COLS:]).astype(BF)
    grad_hidden = mm_t(grad_vo[:, :COLS], w2[0]) + mm_t(grad_vo[:, COLS:], w2[1])
    grad_pre = (grad_hidden * 2.0 * pre).astype(BF)
    gn[0, :, 1536 : 1536 + W1A] = t_mm(mixed_h, grad_pre[:, :W1A]).astype(BF)
    gn[1, :, 1536 : 1536 + W1B] = t_mm(mixed_h, grad_pre[:, W1A:]).astype(BF)
    grad_mh = mm_t(grad_pre[:, :W1A], wn[0, :, 1536 : 1536 + W1A])
    grad_mh += mm_t(grad_pre[:, W1A:], wn[1, :, 1536 : 1536 + W1B])
    grad_mg = mm_t(grad_gp[:, :COLS], wn[0, :, 2944:3328])
    grad_mg += mm_t(grad_gp[:, COLS:], wn[1, :, 2816:3200])
    grad_n2 = grad_mh * lerp_h + grad_mg * lerp_g
    grad_n2 += shift_up(grad_mh * (1.0 - lerp_h) + grad_mg * (1.0 - lerp_g))
    delta2 = normed2 - previous2
    g_lerp_h, g_lerp_g = tsum(grad_mh * delta2), tsum(grad_mg * delta2)
    g_gain2, g_bias2 = tsum(grad_n2 * unit2), tsum(grad_n2)
    q = grad_n2 * gain2
    grad_middle = upstream + scale2 * (q - mean(q) - unit2 * mean(q * unit2))

    grad_attn = grad_middle.astype(BF)
    for h in range(2):
        go[h] = t_mm(gated, grad_attn[:, COLS * h : COLS * h + COLS]).astype(BF)
    grad_gated = mm_t(grad_attn[:, :COLS], wo[0]) + mm_t(grad_attn[:, COLS:], wo[1])
    grad_gate = (grad_gated * grouped * (sig * (1.0 + gate_pre * (1.0 - sig)))).astype(BF)
    grad_grouped = grad_gated * silu
    g_gain_w, g_bias_w = tsum(grad_grouped * unit_w), tsum(grad_grouped)
    q = grad_grouped * gain_w
    grad_wkv = scale_w * (
        q
        - head_sum(q) * (1.0 / 64.0)
        - unit_w * (head_sum(q * unit_w) * (1.0 / 64.0))
    )

    weight = head_sum(grad_wkv * vals)
    parts_r, parts_k, parts_v = [], [], []
    for g in range(6):
        cut = slice(128 * g, 128 * g + 128)
        rg, kg, vg, dg = recept_f[:, cut], keys_f[:, cut], vals[:, cut], grad_wkv[:, cut]
        ds = stack(dg)
        da = jnp.where(below, fine(NT, ds, vg), 0.0)
        parts_r.append(fine(NN, beside(da), stack(kg)) + fine(NT, dg, memory[g]))
        parts_k.append(fine(TN, da, stack(rg)))
        parts_v.append(fine(TN, scores[g], ds))
    grad_r = jnp.concatenate(parts_r, axis=1) * fall_r
    grad_k = jnp.concatenate(parts_k, axis=1) * fall_k
    grad_v = jnp.concatenate(parts_v, axis=1) + grad_wkv * present
    g_rate = fade * tsum(steps * recept * grad_r - (steps + 1.0) * keys * grad_k)
    g_bonus = tsum(recept * keys * weight)
    grad_r = (grad_r + bonus * keys * weight).astype(BF)
    grad_k = (grad_k + bonus * recept * weight).astype(BF)
    grad_v = grad_v.astype(BF)

    gn[0, :, 0:768] = t_mm(blended[0], grad_r).astype(BF)
    gn[0, :, 768:1536] = t_mm(blended[1], grad_k).astype(BF)
    gn[1, :, 0:768] = t_mm(blended[2], grad_v).astype(BF)
    gn[1, :, 768:1536] = t_mm(blended[3], grad_gate).astype(BF)
    grad_blended = [
        mm_t(grad_r, wn[0, :, 0:768]),
        mm_t(grad_k, wn[0, :, 768:1536]),
        mm_t(grad_v, wn[1, :, 0:768]),
        mm_t(grad_gate, wn[1, :, 768:1536]),
    ]
    delta = normed - previous
    g_lerps = [tsum(g * delta) for g in grad_blended]
    grad_n1 = sum(g * l for g, l in zip(grad_blended, lerps))
    grad_n1 += shift_up(sum(g * (1.0 - l) for g, l in zip(grad_blended, lerps)))
    g_gain1, g_bias1 = tsum(grad_n1 * unit1), tsum(grad_n1)
    q = grad_n1 * gain1
    grad_x = grad_middle + scale1 * (q - mean(q) - unit1 * mean(q * unit1))
    in_grad_ref[...] = unspread(grad_x)

    zero = jnp.zeros((1, EMB), F32)
    natural = jnp.concatenate([g_rate, g_bonus, g_gain_w, g_bias_w] + [zero] * 4, axis=0)
    a, b, c = split(natural, 3)
    moved = mm(a, spread[...]) + (mm(b, spread[...]) + mm(c, spread[...]))
    table = jnp.concatenate(
        [g_gain1, g_bias1] + g_lerps + [g_gain2, g_bias2, g_lerp_h, g_lerp_g]
        + [moved[0:4], jnp.zeros((114, EMB), F32)],
        axis=0,
    )
    gn[1, :, VEC:HALF] = table.T.astype(BF)


def layer(x, up, memory, spread, wn, wo, w2):
    return pl.pallas_call(
        layer_kernel,
        out_shape=(
            jax.ShapeDtypeStruct((TOK, EMB), F32),
            jax.ShapeDtypeStruct((TOK, EMB), F32),
            jax.ShapeDtypeStruct((2, EMB, HALF), BF),
            jax.ShapeDtypeStruct((2, EMB, COLS), BF),
            jax.ShapeDtypeStruct((2, FF, COLS), BF),
        ),
        in_specs=[VMEM] * 7,
        out_specs=(VMEM,) * 5,
        scratch_shapes=[pltpu.VMEM((6, 256, 128), F32)],
        compiler_params=pltpu.CompilerParams(vmem_limit_bytes=60 << 20),
        cost_estimate=pl.CostEstimate(
            flops=6 * TOK * 7667712, bytes_accessed=4 * 7667712, transcendentals=10 * TOK * EMB
        ),
        name="layer",
    )(x, up, memory, spread, wn, wo, w2)


def per_device(
    incoming_activations,
    sequence_opening_memory,
    prior_standardize_factor,
    prior_standardize_offset,
    acceptor_lerp_factor,
    address_lerp_factor,
    content_lerp_factor,
    sigmoid_lerp_factor,
    acceptor_matrix,
    address_matrix,
    content_matrix,
    sigmoid_matrix,
    lane_fading_exponent,
    present_reward_vector,
    cluster_standardize_factor,
    cluster_standardize_offset,
    mixer_result_matrix,
    latter_standardize_factor,
    latter_standardize_offset,
    feedforward_address_lerp,
    feedforward_sigmoid_lerp,
    feedforward_address_matrix,
    feedforward_content_matrix,
    feedforward_acceptor_matrix,
    upstream_derivative,
):
    spread = jnp.asarray(_spread(), BF)
    pick_n = jnp.asarray(_line_pick(), BF)
    pick_z = jnp.asarray(_plane_pick(), BF)

    columns = jnp.concatenate(
        [feedforward_acceptor_matrix, mixer_result_matrix, feedforward_content_matrix,
         jnp.zeros((31, EMB), BF)], axis=0,
    )
    columns = jnp.dot(columns, spread, preferred_element_type=F32).astype(BF)
    acceptor = columns[:6]
    pack_z = columns[6:38]
    pack_z = jnp.stack([pack_z[:, :COLS], pack_z[:, COLS:]])
    vectors = jnp.stack(
        [prior_standardize_factor, prior_standardize_offset, acceptor_lerp_factor,
         address_lerp_factor, content_lerp_factor, sigmoid_lerp_factor,
         latter_standardize_factor, latter_standardize_offset, feedforward_address_lerp,
         feedforward_sigmoid_lerp, lane_fading_exponent, present_reward_vector,
         cluster_standardize_factor, cluster_standardize_offset], axis=1,
    )
    vectors = jnp.pad(vectors, ((0, 0), (0, 114)))
    key_matrix = feedforward_address_matrix
    pack_n = jnp.stack([
        jnp.concatenate([acceptor_matrix, address_matrix, key_matrix[:, :W1A], acceptor[:, :COLS]], axis=1),
        jnp.concatenate([content_matrix, sigmoid_matrix, key_matrix[:, W1A:], acceptor[:, COLS:], vectors], axis=1),
    ])
    core = lax.rem(lax.axis_index("fsdp"), 2)
    pack_n = jnp.where(
        core == 0,
        jnp.pad(pack_n, ((0, 0), (0, 10), (0, 0))),
        jnp.pad(pack_n, ((0, 0), (8, 2), (0, 0))),
    )
    wn, wo, w2 = gather(pack_n, pack_z, pick_n, pick_z)

    memory = sequence_opening_memory.reshape(6, 2, 64, 64)
    nothing = jnp.zeros((6, 64, 64), F32)
    memory = jnp.concatenate(
        [jnp.concatenate([memory[:, 0], nothing], axis=2),
         jnp.concatenate([nothing, memory[:, 1]], axis=2)], axis=1,
    )
    out, in_grad, gn, go, g2 = layer(
        incoming_activations, upstream_derivative, memory, spread, wn, wo, w2
    )
    end_n, end_z = scatter(gn, go, g2, pick_n.T, pick_z.T)

    first, second = end_n[0, :6], end_n[1, :6]
    acceptor = jnp.concatenate([first[:, 2944:], second[:, 2816:VEC]], axis=1)
    columns = jnp.concatenate([acceptor, jnp.concatenate([end_z[0, :27], end_z[1, :27]], axis=1)], axis=0)
    columns = lax.dot_general(
        columns, spread.astype(F32), (((1,), (1,)), ((), ())),
        precision=HIGHEST, preferred_element_type=F32,
    )
    vectors = second[:, VEC : VEC + 14]
    key_matrix = jnp.concatenate([first[:, 1536:2944], second[:, 1536:2816]], axis=1)
    return (
        out,
        in_grad,
        vectors[:, 0], vectors[:, 1],
        vectors[:, 2], vectors[:, 3], vectors[:, 4], vectors[:, 5],
        first[:, 0:768], first[:, 768:1536], second[:, 0:768], second[:, 768:1536],
        vectors[:, 10], vectors[:, 11], vectors[:, 12], vectors[:, 13],
        columns[6:12],
        vectors[:, 6], vectors[:, 7], vectors[:, 8], vectors[:, 9],
        key_matrix,
        columns[12:33],
        columns[0:6],
    )


def solution(mesh):
    split_rows, split_all, split_one = P(("dp", "fsdp"), None), P(("dp", "fsdp"), None, None, None), P(("dp", "fsdp"))
    r, v = split_rows, split_one
    return jax.shard_map(
        per_device,
        mesh=mesh,
        in_specs=(r, split_all) + (v,) * 6 + (r,) * 4 + (v,) * 4 + (r,) + (v,) * 4 + (r,) * 4,
        out_specs=(r, r) + (v,) * 6 + (r,) * 4 + (v,) * 4 + (r,) + (v,) * 4 + (r,) * 3,
        check_vma=False,
    )
```

time: 2930 us -> 195 us (0.07)
  waiting for transfers between devices: 1400 us -> 0 us
  blocking collectives: 543 us -> 0 us
  starting transfers between devices: 534 us -> 0 us
  local copies, waits for them, and re-layouts: 297 us -> 17.8 us
  Pallas kernels: 0 us -> 171 us
  matrix products: 75.5 us -> 2.85 us
    all_gather x8 -> x0, waiting for transfers between devices: 1390 us -> none  [the longest x1 193 us: per_device(): lax.all_gather(feedforward_address_matrix, ('dp', 'fsdp'), axis=0, tiled=...]
    unnamed x3 -> x0, blocking collectives: 543 us -> none
    unnamed x209 -> x0, starting transfers between devices: 534 us -> none
    unnamed x666 -> x11, local copies, waits for them, and re-layouts: 251 us -> 2.22 us
    pallas_call x0 -> x3, Pallas kernels: none -> 171 us  [the longest x1 70.8 us: scatter(): pl.pallas_call(scatter_kernel, out_shape=(jax.ShapeDtypeStruct((2, 8, HAL...]
    dot_general x50 -> x2, matrix products: 75.5 us -> 2.85 us  [the longest x1 1.7 us: per_device(): columns = jnp.dot(columns, spread, preferred_element_type=F32).astype(BF)]
  transfers between devices with their start and end apart: 217 -> 0, of which waited for: 8 -> 0; matrix products, arithmetic and copies ran while one was open for 11% -> 0% of each run, Pallas kernels for 0% -> 0%
where the time goes in v1:
time: 195 us
  Pallas kernels  171 us (88%)
  local copies, waits for them, and re-layouts  17.8 us (9%)
  other arithmetic  2.93 us (2%)
  matrix products  2.85 us (1%)
    pallas_call x1, Pallas kernels, scatter(): pl.pallas_call(scatter_kernel, out_shape=(jax.ShapeDtypeStruct((2, 8, HAL...  70.8 us
    pallas_call x1, Pallas kernels, gather(): pl.pallas_call(gather_kernel, out_shape=(jax.ShapeDtypeStruct((2, EMB, HA...  68.5 us
    pallas_call x1, Pallas kernels, layer(): pl.pallas_call(layer_kernel, out_shape=(jax.ShapeDtypeStruct((TOK, EMB),...  31.2 us
    another operation x15, local copies, waits for them, and re-layouts, per_device(): jnp.stack([prior_standardize_factor, prior_standardize_offset, acceptor_l...  10.7 us

profile of v1, /device:TPU:1, one launch (start us, length us, event | category | flops | bytes accessed | tf_op | source)
XLA Modules:
  0.0 194.8 jit_solution(15036004228616153922)
XLA Ops:
  0.8 0.8 copy.68
  1.5 0.8 copy.69
  2.3 0.8 copy.70
  3.0 0.8 copy.71
  3.8 0.8 copy.72
  4.6 0.8 copy.73
  5.3 0.8 copy.78
  6.1 0.8 copy.79
  6.8 0.8 copy.80
  7.6 0.8 copy.81
  8.3 0.8 copy.74
  9.1 0.8 copy.75
  9.8 0.8 copy.76
  10.6 0.8 copy.77
  11.5 0.8 constant_dynamic-update-slice_fusion.3
  13.7 1.7 convolution_convert_fusion
  16.9 0.9 select_maximum_fusion.memory
  17.8 68.5 %gather_weights.1 = (bf16[2,768,3328]{2,1,0:T(8,128)(2,1)}, bf16[2,768,384]{2,1,0:T(8,128)(2,1)}, bf16[2,2688,384]{2,1,0:T(8,128)(2,1)}) custom-call(bf16[2,16,3328]{2,1,0:T(8,128)(2,1)} %pad_select_fusion.pack_n, bf16[2,32,384]{2,1,0:T(8,128)(2,1)} %pad_maximum_fusion.2.pack_z, bf16[48,64]{1,0:T(8,128)(2,1)} %constant.22.clone.pick_n, ...), custom_call_target="tpu_custom_call" | custom-call | tf_op jit(solution)/shard_map/gather_weights/pallas_call | solution.py:258
  86.2 31.2 %layer.1 = (f32[128,768]{1,0:T(8,128)}, f32[128,768]{1,0:T(8,128)}, bf16[2,768,3328]{2,1,0:T(8,128)(2,1)}, bf16[2,768,384]{2,1,0:T(8,128)(2,1)}, bf16[2,2688,384]{2,1,0:T(8,128)(2,1)}) custom-call(bf16[128,768]{1,0:T(8,128)(2,1)} %x_ref.1, bf16[128,768]{1,0:T(8,128)(2,1)} %up_ref.1, f32[6,128,128]{2,1,0:T(8,128)} %select_maximum_fusion.memory, ...), custom_call_target="tpu_custom_call" | custom-call | flops 5888802816 | bytes 30670848 | tf_op jit(solution)/shard_map/layer/pallas_call | solution.py:676
  117.5 70.8 %scatter_grads.1 = (f32[2,8,3328]{2,1,0:T(8,128)}, f32[2,32,384]{2,1,0:T(8,128)}) custom-call(bf16[2,768,3328]{2,1,0:T(8,128)(2,1)} %get-tuple-element.39.grad_n, bf16[2,768,384]{2,1,0:T(8,128)(2,1)} %get-tuple-element.40.grad_o, bf16[2,2688,384]{2,1,0:T(8,128)(2,1)} %get-tuple-element.41.grad_2, bf16[64,48]{1,0:T(8,128)(2,1)} %constant.57.turn_n, ...), custom_call_target="tpu_custom_call" | custom-call | tf_op jit(solution)/shard_map/scatter_grads/pallas_call | solution.py:405
  188.3 1.1 slice_bitcast_fusion.2
  189.4 0.9 slice_reduce_fusion
  191.6 0.8 slice_bitcast_fusion.5
  192.4 1.1 fusion
  (31 shorter events, 5.7 us)
Async XLA Ops:
  0.7 15.4 %slice-start = ((bf16[6,2688]{1,0:T(8,128)(2,1)}), bf16[6,1408]{1,0:T(8,128)(2,1)S(1)}, s32[]{:S(2)}) async-start(bf16[6,2688]{1,0:T(8,128)(2,1)} %param.49), calls=%async_computation | async-start | bytes 45056 | tf_op jit(solution)/shard_map/slice | solution.py:745
  0.7 15.4 %copy-start.2 = (bf16[6,768]{1,0:T(8,128)(2,1)S(1)}, bf16[6,768]{1,0:T(8,128)(2,1)}, u32[]{:S(2)}) copy-start(bf16[6,768]{1,0:T(8,128)(2,1)} %param.37) | copy-start | bytes 27652
  0.7 15.4 %copy-start.3 = (bf16[6,768]{1,0:T(8,128)(2,1)S(1)}, bf16[6,768]{1,0:T(8,128)(2,1)}, u32[]{:S(2)}) copy-start(bf16[6,768]{1,0:T(8,128)(2,1)} %param.36) | copy-start | bytes 27652
  11.4 5.4 %copy-start.1 = (f32[1,12,64,64]{3,2,1,0:T(8,128)S(1)}, f32[1,12,64,64]{3,2,1,0:T(8,128)}, u32[]{:S(2)}) copy-start(f32[1,12,64,64]{3,2,1,0:T(8,128)} %param.29) | copy-start | bytes 589828
  188.3 4.1 %copy-start = (bf16[768,768]{1,0:T(8,128)(2,1)S(1)}, bf16[768,768]{1,0:T(8,128)(2,1)}, u32[]{:S(2)}) copy-start(bf16[768,768]{1,0:T(8,128)(2,1)} %constant.21.clone.spread) | copy-start | bytes 3538948

commit v2 on v1

v2 whole, which is shorter than its diff:
```python
from functools import partial

import jax
import jax.numpy as jnp
import numpy as np
from jax import lax
from jax.experimental import pallas as pl
from jax.experimental.pallas import tpu as pltpu
from jax.sharding import PartitionSpec as P

MESH = pl.DeviceIdType.MESH
BF = jnp.bfloat16
F32 = jnp.float32
VMEM = pl.BlockSpec(memory_space=pltpu.VMEM)

NORM_EPS = 1e-05
GROUP_EPS = 0.00064
TOK = 128
EMB = 768
FF = 2688
QUART = 1664
COLS = 384
VEC = 1536
COPIES = 256


def _order():
    order = np.zeros(EMB, np.int64)
    for x in range(4):
        for y in range(4):
            for z in range(4):
                for c in range(2):
                    device = z * 32 + (x % 2) * 16 + y * 4 + (x // 2) * 2 + c
                    place = (x * 4 + y) * 48 + (z * 2 + c) * 6
                    order[place : place + 6] = 6 * device + np.arange(6)
    return order


def _spread():
    spread = np.zeros((EMB, EMB), np.float32)
    spread[_order(), np.arange(EMB)] = 1.0
    return spread


def _line_pick():
    pick = np.zeros((96, 128), np.float32)
    for member in range(8):
        for r in range(6):
            pick[member * 6 + r, member * 16 + r] = 1.0
            pick[48 + member * 6 + r, member * 16 + 8 + r] = 1.0
    return pick


def _plane_pick():
    pick = np.zeros((432, 512), np.float32)
    for member in range(16):
        for r in range(6):
            pick[member * 6 + r, member * 32 + r] = 1.0
        for r in range(21):
            pick[96 + member * 21 + r, member * 32 + 8 + r] = 1.0
    return pick


def rem4(value):
    return lax.rem(value, 4)


class Place:
    def __init__(self):
        dp, fs = lax.axis_index("dp"), lax.axis_index("fsdp")
        self.z, self.xlo = lax.div(dp, 2), lax.rem(dp, 2)
        self.y, self.xhi = lax.div(fs, 4), lax.rem(lax.div(fs, 2), 2)
        self.c = lax.rem(fs, 2)
        self.x = self.xhi * 2 + self.xlo
        self.chip = self.y * 2 + self.xhi

    def device(self, z, y, x, c):
        return (z * 2 + lax.rem(x, 2), y * 4 + lax.div(x, 2) * 2 + c)

    def sibling(self):
        return self.device(self.z, self.y, self.x, 1 - self.c)

    def up(self, k):
        return self.device(rem4(self.z + k), self.y, self.x, self.c)

    def line(self, k):
        z = rem4(self.z + k // 2)
        core = self.c if k % 2 == 0 else 1 - self.c
        return self.device(z, self.y, self.x, core), z * 2 + core, core

    def first(self, k):
        y, x = rem4(self.y + k * (1 - self.c)), rem4(self.x + k * self.c)
        return self.device(self.z, y, x, self.c)

    def last(self, k):
        y, x = rem4(self.y + k * self.c), rem4(self.x + k * (1 - self.c))
        return self.device(self.z, y, x, self.c)

    def band(self, m, k, core=None):
        c = self.c if core is None else core
        x = rem4(self.x + m * c + k * (1 - c))
        y = rem4(self.y + m * (1 - c) + k * c)
        return rows(48 * (x * 4 + y), 48)

    def plane(self, k):
        index = lax.rem(self.chip + k, 8)
        y, xhi = lax.div(index, 2), lax.rem(index, 2)
        return self.device(self.z, y, xhi * 2 + self.xlo, self.c), index

    def twin(self):
        return self.device(self.z, self.y, self.xhi * 2 + 1 - self.xlo, self.c)

    def order(self, m, k):
        return rem4(self.z + k) * 2 + (self.xlo if m == 0 else 1 - self.xlo)

    def greet(self):
        mates = [self.twin()]
        mates += [self.line(k)[0] for k in range(1, 8)]
        mates += [self.first(k) for k in (1, 2, 3)]
        mates += [self.last(k) for k in (1, 2, 3)]
        mates += [self.plane(k)[0] for k in range(1, 8)]
        barrier = pltpu.get_barrier_semaphore()
        for mate in mates:
            pl.semaphore_signal(barrier, inc=1, device_id=mate, device_id_type=MESH)
        return lambda: pl.semaphore_wait(barrier, len(mates))


class Sender:
    def __init__(self, send_sems, recv_sems):
        self.send_sems, self.recv_sems = send_sems, recv_sems
        self.count = 0
        self.open = []

    def send(self, source, target, device):
        copy = pltpu.make_async_remote_copy(
            src_ref=source,
            dst_ref=target,
            send_sem=self.send_sems.at[self.count],
            recv_sem=self.recv_sems.at[self.count],
            device_id=device,
            device_id_type=MESH,
        )
        copy.start()
        self.count += 1
        self.open.append(copy)
        return copy

    def drain(self):
        for copy in self.open:
            copy.wait_send()
        self.open = []


def rows(start, size, unit=16):
    return pl.ds(pl.multiple_of(start, unit), size)


def mm(left, right):
    return jnp.dot(left, right, preferred_element_type=F32)


def mm_t(left, right):
    return lax.dot_general(left, right, (((1,), (1,)), ((), ())), preferred_element_type=F32)


def t_mm(left, right):
    return lax.dot_general(left, right, (((0,), (0,)), ((), ())), preferred_element_type=F32)


def split(value, parts):
    found = []
    for _ in range(parts - 1):
        high = value.astype(BF)
        found.append(high)
        value = value - high.astype(F32)
    found.append(value.astype(BF))
    return found


def fine(dims, left, right):
    lh, ll = split(left, 2)
    rh, rl = split(right, 2)
    dot = partial(lax.dot_general, dimension_numbers=(dims, ((), ())), preferred_element_type=F32)
    return dot(lh, rh) + (dot(lh, rl) + dot(ll, rh))


NN, NT, TN = ((1,), (0,)), ((1,), (1,)), ((0,), (0,))


def wide(ref):
    return ref[...].astype(F32)


def layer_kernel(
    x_ref, up_ref, memory, spread, pick_n, pick_z, turn_n, turn_z, vecs,
    acceptor, address, content, sigmoid, mixer, ff_address, ff_content, ff_acceptor,
    out_ref, in_grad_ref, end_n, end_z,
    wn, wo, w2, scores,
    pack_f, pack_n, stage_n, cols_f, pack_z, half_z, stage_z,
    sib_n, sib_o, sib_2, relay_n, last_n, first_n, acc_n, piece_n, line_n,
    relay_o, relay_2, up_o, up_2, sent_o, sent_2, twin_o, twin_2, piece_z, plane_z, swap_f,
    send_sems, recv_sems,
):
    at = Place()
    c = at.c
    sib = at.sibling()
    net = Sender(send_sems, recv_sems)
    met = at.greet()

    pack_f[...] = jnp.zeros_like(pack_f)
    cols_f[...] = jnp.zeros_like(cols_f)
    cols_f[0:6] = wide(mixer)
    cols_f[8:29] = wide(ff_content)
    cols_f[32:38] = wide(ff_acceptor)
    moved = mm(cols_f[...].astype(BF), spread[...])
    pack_f[0, 0:6, 0:768] = wide(acceptor)
    pack_f[0, 0:6, 768:1536] = wide(address)
    pack_f[1, 0:6, 0:768] = wide(content)
    pack_f[1, 0:6, 768:1536] = wide(sigmoid)
    pack_f[0, 0:6, 1536:1664] = wide(ff_address.at[:, 0:128])
    pack_f[0, 8:14, 0:1280] = wide(ff_address.at[:, 128:1408])
    pack_f[1, 8:14, 0:1280] = wide(ff_address.at[:, 1408:2688])
    eye = (
        lax.broadcasted_iota(jnp.int32, (16, 128), 0)
        == lax.broadcasted_iota(jnp.int32, (16, 128), 1)
    ).astype(F32).astype(BF)
    pack_f[1, 0:6, VEC:QUART] = mm_t(eye, vecs[...])[0:6]
    for h in range(2):
        pack_f[h, 8:16, 1280:1664] = moved[32:40, COLS * h : COLS * h + COLS]
        pack_z[h] = moved[0:32, COLS * h : COLS * h + COLS].astype(BF)
        pack_n[h] = pack_f[h].astype(BF)
    met()

    swap_z = net.send(pack_z.at[1 - c], half_z.at[c], sib)
    own = at.z * 2 + c
    lines = []
    for k in range(1, 8):
        mate, _, core = at.line(k)
        lines.append(net.send(pack_n.at[core], stage_n.at[own], mate))
    stage_n[own] = pack_n[c]
    half_z[c] = pack_z[c]
    swap_z.wait_recv()
    planes = []
    for k in range(1, 8):
        planes.append(net.send(half_z, stage_z.at[at.chip], at.plane(k)[0]))
    stage_z[at.chip] = half_z[...]

    tokens = mm(x_ref[...], spread[...])
    centred = tokens - jnp.mean(tokens, axis=-1, keepdims=True)
    scale1 = lax.rsqrt(jnp.mean(centred * centred, axis=-1, keepdims=True) + NORM_EPS)
    unit1 = centred * scale1
    upstream = mm(up_ref[...], spread[...])

    for copy in lines:
        copy.wait_recv()
    picked = mm(pick_n[...], stage_n[...].reshape(128, QUART)).astype(BF)

    def place_n(q, m, k):
        return wn.at[c, q, at.band(m, k)]

    firsts, lasts, sibs = {}, {}, {0: [], 1: [], "o": [], "2": []}

    def pass_on(q, m):
        spot = place_n(q, 4 - m, 0)
        for k in (1, 3):
            lasts[q, m, k] = net.send(spot, spot, at.last(k))
        sibs[q].append(net.send(spot, spot, sib))

    def begin(q):
        spot = place_n(q, 0, 0)
        spot[...] = picked[48 * q : 48 * q + 48]
        for k in (1, 2, 3):
            firsts[q, k] = net.send(spot, spot, at.first(k))
        pass_on(q, 0)

    def relay(q, m):
        firsts[q, m].wait_recv()
        pass_on(q, m)

    def arrive(q, m, k):
        lasts[q, m, k].wait_recv()
        spot = place_n(q, 4 - m, 4 - k)
        if k == (1 if m % 2 == 0 else 3):
            lasts[q, m, 2] = net.send(spot, spot, at.last(k))
        sibs[q].append(net.send(spot, spot, sib))

    def arrive_far(q, m):
        lasts[q, m, 2].wait_recv()
        spot = place_n(q, 4 - m, 2)
        sibs[q].append(net.send(spot, spot, sib))

    def place_z(w, m, k):
        unit = 96 if w == "o" else 336
        return (wo if w == "o" else w2).at[c, rows(unit * at.order(m, k), unit)]

    def pass_z(w, m):
        spot = place_z(w, m, 0)
        for k in (1, 3):
            lasts[w, m, k] = net.send(spot, spot, at.up(k))
        sibs[w].append(net.send(spot, spot, sib))

    def relay_z(w):
        firsts[w].wait_recv()
        pass_z(w, 1)

    def arrive_z(w, m, k):
        lasts[w, m, k].wait_recv()
        spot = place_z(w, m, 4 - k)
        if k == (1 if m == 0 else 3):
            lasts[w, m, 2] = net.send(spot, spot, at.up(k))
        sibs[w].append(net.send(spot, spot, sib))

    def arrive_z_far(w, m):
        lasts[w, m, 2].wait_recv()
        spot = place_z(w, m, 2)
        sibs[w].append(net.send(spot, spot, sib))

    begin(0)
    begin(1)
    for copy in planes:
        copy.wait_recv()
    picked_z = mm(pick_z[...], stage_z[...].reshape(512, COLS)).astype(BF)
    place_z("o", 0, 0)[...] = picked_z[:96]
    place_z("2", 0, 0)[...] = picked_z[96:]
    for w in ("o", "2"):
        spot = place_z(w, 0, 0)
        firsts[w] = net.send(spot, spot, at.twin())
        pass_z(w, 0)
    for m in (1, 2, 3):
        relay(0, m)
    for w in ("o", "2"):
        relay_z(w)
    for m in (1, 2, 3):
        relay(1, m)
    for m in range(4):
        for k in (1, 3):
            arrive(0, m, k)
    for m in range(4):
        arrive_far(0, m)
    for copy in sibs[0]:
        copy.wait_recv()

    tasks = []
    for m in range(2):
        for k in (1, 3):
            tasks.append(partial(arrive_z, "o", m, k))
    for m in range(2):
        tasks.append(partial(arrive_z_far, "o", m))
    for m in range(2):
        for k in (1, 3):
            tasks.append(partial(arrive, 1, m, k))
            tasks.append(partial(arrive_z, "2", m, k))
    for m in (2, 3):
        for k in (1, 3):
            tasks.append(partial(arrive, 1, m, k))
    for m in range(4):
        tasks.append(partial(arrive_far, 1, m))
    for m in range(2):
        tasks.append(partial(arrive_z_far, "2", m))

    def work(count):
        for _ in range(min(count, len(tasks))):
            tasks.pop(0)()

    lanes = lax.broadcasted_iota(jnp.int32, (1, 128), 1)
    left_head = lanes < 64
    token = lax.broadcasted_iota(jnp.int32, (TOK, 1), 0)

    def shift_down(value):
        return jnp.where(token == 0, 0.0, pltpu.roll(value, 1, 0))

    def shift_up(value):
        return jnp.where(token == TOK - 1, 0.0, pltpu.roll(value, TOK - 1, 0))

    def mean(value):
        return jnp.mean(value, axis=-1, keepdims=True)

    def tsum(value):
        return jnp.sum(value, axis=0, keepdims=True)

    def unspread(value):
        a, b, d = split(value, 3)
        return mm_t(a, spread[...]) + (mm_t(b, spread[...]) + mm_t(d, spread[...]))

    vec = mm_t(eye, wn[1, 0, :, VEC:QUART])
    gain1, bias1 = vec[0:1], vec[1:2]
    lerps = [vec[2 + i : 3 + i] for i in range(4)]
    gain2, bias2, lerp_h, lerp_g = vec[6:7], vec[7:8], vec[8:9], vec[9:10]
    heads = mm_t(vec.astype(BF), spread[...])
    rate, bonus, gain_w, bias_w = heads[10:11], heads[11:12], heads[12:13], heads[13:14]

    pair_rows = lax.broadcasted_iota(jnp.int32, (256, 128), 0)
    pair_cols = lax.broadcasted_iota(jnp.int32, (256, 128), 1)
    pair_ones = ((lax.rem(pair_rows, 128) // 64) == (pair_cols // 64)).astype(F32).astype(BF)
    below = lax.rem(pair_rows, 128) > pair_cols

    def head_sum(value):
        found = []
        for g in range(6):
            part = value[:, 128 * g : 128 * g + 128]
            found.append(mm(jnp.concatenate(split(part, 2), axis=1), pair_ones))
        return jnp.concatenate(found, axis=1)

    def stack(value):
        return jnp.concatenate(
            [jnp.where(left_head, value, 0.0), jnp.where(left_head, 0.0, value)], axis=0
        )

    def beside(value):
        return jnp.concatenate([value[:TOK], value[TOK:]], axis=1)

    normed = unit1 * gain1 + bias1
    previous = shift_down(normed)
    blended = [(normed * l + previous * (1.0 - l)).astype(BF) for l in lerps]
    recept = mm(blended[0], wn[0, 0, :, 0:768])
    keys = mm(blended[1], wn[0, 0, :, 768:1536])
    vals = mm(blended[2], wn[1, 0, :, 0:768])
    gate_pre = mm(blended[3], wn[1, 0, :, 768:1536])
    work(6)

    fade = -jnp.exp(rate)
    steps = token.astype(F32)
    fall_r = jnp.exp(steps * fade)
    fall_k = jnp.exp(-(steps + 1.0) * fade)
    recept_f = recept * fall_r
    keys_f = keys * fall_k
    present = head_sum(recept * bonus * keys)
    parts = []
    for g in range(6):
        cut = slice(128 * g, 128 * g + 128)
        rg, kg, vg = recept_f[:, cut], keys_f[:, cut], vals[:, cut]
        sc = jnp.where(below, fine(NT, stack(rg), kg), 0.0)
        scores[g] = sc
        parts.append(fine(NN, beside(sc), stack(vg)) + fine(NN, rg, memory[g]))
        if g % 2 == 1:
            work(4)
    wkv = jnp.concatenate(parts, axis=1) + present * vals

    centred_w = wkv - head_sum(wkv) * (1.0 / 64.0)
    scale_w = lax.rsqrt(head_sum(centred_w * centred_w) * (1.0 / 64.0) + GROUP_EPS)
    unit_w = centred_w * scale_w
    grouped = unit_w * gain_w + bias_w
    sig = 1.0 / (1.0 + jnp.exp(-gate_pre))
    silu = gate_pre * sig
    gated = (grouped * silu).astype(BF)
    for copy in sibs["o"]:
        copy.wait_recv()
    middle = tokens + jnp.concatenate([mm(gated, wo[0]), mm(gated, wo[1])], axis=1)

    centred = middle - mean(middle)
    scale2 = lax.rsqrt(mean(centred * centred) + NORM_EPS)
    unit2 = centred * scale2
    normed2 = unit2 * gain2 + bias2
    previous2 = shift_down(normed2)
    mixed_h = (normed2 * lerp_h + previous2 * (1.0 - lerp_h)).astype(BF)
    mixed_g = (normed2 * lerp_g + previous2 * (1.0 - lerp_g)).astype(BF)
    work(len(tasks))
    for copy in sibs[1]:
        copy.wait_recv()
    pre = jnp.concatenate(
        [
            mm(mixed_h, wn[0, 0, :, 1536:1664]),
            mm(mixed_h, wn[0, 1, :, 0:1280]),
            mm(mixed_h, wn[1, 1, :, 0:1280]),
        ],
        axis=1,
    )
    pre = jnp.maximum(pre, 0.0)
    hidden = (pre * pre).astype(BF)
    gating = jnp.concatenate(
        [mm(mixed_g, wn[0, 1, :, 1280:1664]), mm(mixed_g, wn[1, 1, :, 1280:1664])], axis=1
    )
    gating = 1.0 / (1.0 + jnp.exp(-gating))
    for copy in sibs["2"]:
        copy.wait_recv()
    value_out = jnp.concatenate([mm(hidden, w2[0]), mm(hidden, w2[1])], axis=1)
    layer_out = middle + gating * value_out
    net.drain()

    swaps = {}

    def fold(mine, other, *more):
        total = wide(mine) + wide(other)
        for ref in more:
            total += wide(ref)
        return total

    def swap(q):
        for k in (2, 1, 3, 0):
            for m in range(4):
                part = at.band(m, k, 1 - c)
                swaps[q, m, k] = net.send(wn.at[1 - c, q, part], sib_n.at[q, part], sib)

    def scatter_far(q, m):
        part = at.band(m, 2)
        via = 1 if m % 2 == 0 else 3
        swaps[q, m, 2].wait_recv()
        spot = sib_n.at[q, part]
        spot[...] = fold(wn.at[c, q, part], spot).astype(BF)
        lasts["g", q, m, 2] = net.send(spot, relay_n.at[q, m], at.last(via))

    def scatter_near(q, m, k):
        part = at.band(m, k)
        swaps[q, m, k].wait_recv()
        spot = sib_n.at[q, part]
        more = []
        if k == (1 if m % 2 == 0 else 3):
            lasts["g", q, m, 2].wait_recv()
            more = [relay_n.at[q, m]]
        spot[...] = fold(wn.at[c, q, part], spot, *more).astype(BF)
        lasts["g", q, m, k] = net.send(spot, last_n.at[q, k // 2, m], at.last(k))

    def scatter_own(q, m):
        part = at.band(m, 0)
        swaps[q, m, 0].wait_recv()
        spot = sib_n.at[q, part]
        lasts["g", q, m, 1].wait_recv()
        lasts["g", q, m, 3].wait_recv()
        total = fold(wn.at[c, q, part], spot, last_n.at[q, 0, m], last_n.at[q, 1, m])
        if m == 0:
            acc_n[q] = total
        else:
            spot[...] = total.astype(BF)
            firsts["g", q, m] = net.send(spot, first_n.at[q, m - 1], at.first(m))

    def scatter_end(q):
        total = acc_n[q]
        for m in (1, 2, 3):
            firsts["g", q, m].wait_recv()
            total += wide(first_n.at[q, m - 1])
        acc_n[q] = total

    def scatter_steps(q):
        steps_ = [partial(scatter_far, q, m) for m in range(4)]
        for late in (False, True):
            for m in range(4):
                for k in (1, 3):
                    if late == (k == (1 if m % 2 == 0 else 3)):
                        steps_.append(partial(scatter_near, q, m, k))
        steps_ += [partial(scatter_own, q, m) for m in (1, 2, 3, 0)]
        steps_.append(partial(scatter_end, q))
        return steps_

    z_parts = {
        "o": (96, wo, sib_o, relay_o, up_o, sent_o, twin_o),
        "2": (336, w2, sib_2, relay_2, up_2, sent_2, twin_2),
    }

    def swap_w(w):
        unit, mine, theirs = z_parts[w][:3]
        for k in (2, 1, 3, 0):
            part = rows(2 * unit * rem4(at.z + k), 2 * unit)
            swaps[w, k] = net.send(mine.at[1 - c, part], theirs.at[part], sib)

    def part_w(w, m, k):
        unit = z_parts[w][0]
        return rows(unit * at.order(m, k), unit)

    def scatter_far_w(w, m):
        unit, mine, theirs, relayed = z_parts[w][:4]
        part = part_w(w, m, 2)
        if m == 0:
            swaps[w, 2].wait_recv()
        spot = theirs.at[part]
        spot[...] = fold(mine.at[c, part], spot).astype(BF)
        lasts["g", w, m, 2] = net.send(spot, relayed.at[m], at.up(1 if m == 0 else 3))

    def scatter_near_w(w, m, k):
        unit, mine, theirs, relayed, arrived = z_parts[w][:5]
        part = part_w(w, m, k)
        if (m == 1) == (k == 1):
            swaps[w, k].wait_recv()
        more = []
        if k == (1 if m == 0 else 3):
            lasts["g", w, m, 2].wait_recv()
            more = [relayed.at[m]]
        spot = theirs.at[part]
        spot[...] = fold(mine.at[c, part], spot, *more).astype(BF)
        lasts["g", w, m, k] = net.send(spot, arrived.at[k // 2, m], at.up(k))

    def scatter_own_w(w, m):
        unit, mine, theirs, relayed, arrived, sent, twin = z_parts[w]
        part = part_w(w, m, 0)
        if m == 1:
            swaps[w, 0].wait_recv()
        lasts["g", w, m, 1].wait_recv()
        lasts["g", w, m, 3].wait_recv()
        total = fold(mine.at[c, part], theirs.at[part], arrived.at[0, m], arrived.at[1, m])
        if m == 1:
            sent[...] = total.astype(BF)
            firsts["g", w] = net.send(sent, twin, at.twin())
        else:
            firsts["g", w].wait_recv()
            sums_z[w] = (total + wide(twin)).astype(BF)

    def scatter_steps_w(w):
        steps_ = [partial(scatter_far_w, w, 0), partial(scatter_far_w, w, 1)]
        steps_ += [partial(scatter_near_w, w, 1, 1), partial(scatter_near_w, w, 0, 3)]
        steps_ += [partial(scatter_near_w, w, 0, 1), partial(scatter_near_w, w, 1, 3)]
        steps_ += [partial(scatter_own_w, w, 1), partial(scatter_own_w, w, 0)]
        return steps_

    sums_z = {}

    grad_vo = upstream * gating
    grad_gp = (grad_vo * value_out * (1.0 - gating)).astype(BF)
    grad_vo = grad_vo.astype(BF)
    grad_hidden = mm_t(grad_vo[:, :COLS], w2[0]) + mm_t(grad_vo[:, COLS:], w2[1])
    grad_pre = (grad_hidden * 2.0 * pre).astype(BF)
    for h in range(2):
        w2[h] = t_mm(hidden, grad_vo[:, COLS * h : COLS * h + COLS]).astype(BF)
    swap_w("2")
    grad_mh = mm_t(grad_pre[:, :128], wn[0, 0, :, 1536:1664])
    grad_mh += mm_t(grad_pre[:, 128:1408], wn[0, 1, :, 0:1280])
    grad_mh += mm_t(grad_pre[:, 1408:], wn[1, 1, :, 0:1280])
    grad_mg = mm_t(grad_gp[:, :COLS], wn[0, 1, :, 1280:1664])
    grad_mg += mm_t(grad_gp[:, COLS:], wn[1, 1, :, 1280:1664])
    wn[0, 1, :, 0:1280] = t_mm(mixed_h, grad_pre[:, 128:1408]).astype(BF)
    wn[1, 1, :, 0:1280] = t_mm(mixed_h, grad_pre[:, 1408:]).astype(BF)
    wn[0, 0, :, 1536:1664] = t_mm(mixed_h, grad_pre[:, :128]).astype(BF)
    wn[0, 1, :, 1280:1664] = t_mm(mixed_g, grad_gp[:, :COLS]).astype(BF)
    wn[1, 1, :, 1280:1664] = t_mm(mixed_g, grad_gp[:, COLS:]).astype(BF)
    swap(1)
    steps_2, steps_1 = scatter_steps_w("2"), scatter_steps(1)
    tasks += steps_2[:2] + steps_1[:4] + steps_2[2:4] + steps_1[4:8]
    work(len(tasks))
    tasks += steps_2[4:6] + steps_1[8:12]

    grad_n2 = grad_mh * lerp_h + grad_mg * lerp_g
    grad_n2 += shift_up(grad_mh * (1.0 - lerp_h) + grad_mg * (1.0 - lerp_g))
    delta2 = normed2 - previous2
    g_lerp_h, g_lerp_g = tsum(grad_mh * delta2), tsum(grad_mg * delta2)
    g_gain2, g_bias2 = tsum(grad_n2 * unit2), tsum(grad_n2)
    q2 = grad_n2 * gain2
    grad_middle = upstream + scale2 * (q2 - mean(q2) - unit2 * mean(q2 * unit2))

    grad_attn = grad_middle.astype(BF)
    grad_gated = mm_t(grad_attn[:, :COLS], wo[0]) + mm_t(grad_attn[:, COLS:], wo[1])
    for h in range(2):
        wo[h] = t_mm(gated, grad_attn[:, COLS * h : COLS * h + COLS]).astype(BF)
    swap_w("o")
    work(len(tasks))
    steps_o = scatter_steps_w("o")
    tasks += steps_o[:4] + steps_1[12:16] + steps_2[6:8] + steps_o[4:]
    grad_gate = (grad_gated * grouped * (sig * (1.0 + gate_pre * (1.0 - sig)))).astype(BF)
    grad_grouped = grad_gated * silu
    g_gain_w, g_bias_w = tsum(grad_grouped * unit_w), tsum(grad_grouped)
    qw = grad_grouped * gain_w
    grad_wkv = scale_w * (
        qw
        - head_sum(qw) * (1.0 / 64.0)
        - unit_w * (head_sum(qw * unit_w) * (1.0 / 64.0))
    )

    weight = head_sum(grad_wkv * vals)
    parts_r, parts_k, parts_v = [], [], []
    for g in range(6):
        cut = slice(128 * g, 128 * g + 128)
        rg, kg, vg, dg = recept_f[:, cut], keys_f[:, cut], vals[:, cut], grad_wkv[:, cut]
        ds = stack(dg)
        da = jnp.where(below, fine(NT, ds, vg), 0.0)
        parts_r.append(fine(NN, beside(da), stack(kg)) + fine(NT, dg, memory[g]))
        parts_k.append(fine(TN, da, stack(rg)))
        parts_v.append(fine(TN, scores[g], ds))
        work(2)
    grad_r = jnp.concatenate(parts_r, axis=1) * fall_r
    grad_k = jnp.concatenate(parts_k, axis=1) * fall_k
    grad_v = jnp.concatenate(parts_v, axis=1) + grad_wkv * present
    g_rate = fade * tsum(steps * recept * grad_r - (steps + 1.0) * keys * grad_k)
    g_bonus = tsum(recept * keys * weight)
    grad_r = (grad_r + bonus * keys * weight).astype(BF)
    grad_k = (grad_k + bonus * recept * weight).astype(BF)
    grad_v = grad_v.astype(BF)

    grad_blended = [
        mm_t(grad_r, wn[0, 0, :, 0:768]),
        mm_t(grad_k, wn[0, 0, :, 768:1536]),
        mm_t(grad_v, wn[1, 0, :, 0:768]),
        mm_t(grad_gate, wn[1, 0, :, 768:1536]),
    ]
    wn[0, 0, :, 0:768] = t_mm(blended[0], grad_r).astype(BF)
    wn[0, 0, :, 768:1536] = t_mm(blended[1], grad_k).astype(BF)
    wn[1, 0, :, 0:768] = t_mm(blended[2], grad_v).astype(BF)
    wn[1, 0, :, 768:1536] = t_mm(blended[3], grad_gate).astype(BF)
    delta = normed - previous
    g_lerps = [tsum(g * delta) for g in grad_blended]
    grad_n1 = sum(g * l for g, l in zip(grad_blended, lerps))
    grad_n1 += shift_up(sum(g * (1.0 - l) for g, l in zip(grad_blended, lerps)))
    g_gain1, g_bias1 = tsum(grad_n1 * unit1), tsum(grad_n1)

    zero = jnp.zeros((1, EMB), F32)
    natural = jnp.concatenate([g_rate, g_bonus, g_gain_w, g_bias_w] + [zero] * 4, axis=0)
    va, vb, vc = split(natural, 3)
    moved = mm(va, spread[...]) + (mm(vb, spread[...]) + mm(vc, spread[...]))
    table = jnp.concatenate(
        [g_gain1, g_bias1] + g_lerps + [g_gain2, g_bias2, g_lerp_h, g_lerp_g]
        + [moved[0:4], jnp.zeros((114, EMB), F32)],
        axis=0,
    )
    wn[1, 0, :, VEC:QUART] = table.T.astype(BF)
    swap(0)
    steps_0 = scatter_steps(0)
    tasks += steps_0[:8] + steps_1[16:] + steps_0[8:12]
    work(len(tasks))
    out_ref[...] = unspread(layer_out)
    q1 = grad_n1 * gain1
    grad_x = grad_middle + scale1 * (q1 - mean(q1) - unit1 * mean(q1 * unit1))
    in_grad_ref[...] = unspread(grad_x)

    spread_z = mm(turn_z[:, :96], sums_z["o"]) + mm(turn_z[:, 96:], sums_z["2"])
    piece_z[...] = spread_z.astype(BF).reshape(8, 64, COLS)
    planes = []
    for k in range(1, 8):
        mate, index = at.plane(k)
        planes.append(net.send(piece_z.at[index], plane_z.at[k - 1], mate))
    tasks += steps_0[12:]
    work(len(tasks))

    spread_n = mm(turn_n[...], jnp.concatenate([acc_n[0], acc_n[1]], axis=0).astype(BF))
    piece_n[...] = spread_n.astype(BF).reshape(8, 16, QUART)
    lines = []
    for k in range(1, 8):
        mate, index, _ = at.line(k)
        lines.append(net.send(piece_n.at[index], line_n.at[own], mate))

    total = wide(piece_z.at[at.chip])
    for k in range(1, 8):
        planes[k - 1].wait_recv()
        total += wide(plane_z.at[k - 1])
    swap_f[...] = total
    away, kept = rows(32 * (1 - c), 32, 8), rows(32 * c, 32, 8)
    last_swap = net.send(swap_f.at[away], end_z.at[c], sib)
    end_z[c] = swap_f[kept]

    line_n[own] = piece_n[own]
    for copy in lines:
        copy.wait_recv()
    for h in range(2):
        total = wide(line_n.at[h])
        for z in (1, 2, 3):
            total += wide(line_n.at[2 * z + h])
        end_n[h] = total
    last_swap.wait_recv()
    net.drain()


def layer(*operands):
    bf = lambda *shape: pltpu.VMEM(shape, BF)
    f32 = lambda *shape: pltpu.VMEM(shape, F32)
    return pl.pallas_call(
        layer_kernel,
        out_shape=(
            jax.ShapeDtypeStruct((TOK, EMB), F32),
            jax.ShapeDtypeStruct((TOK, EMB), F32),
            jax.ShapeDtypeStruct((2, 16, QUART), F32),
            jax.ShapeDtypeStruct((2, 32, COLS), F32),
        ),
        in_specs=[VMEM] * len(operands),
        out_specs=(VMEM,) * 4,
        scratch_shapes=[
            bf(2, 2, EMB, QUART), bf(2, EMB, COLS), bf(2, FF, COLS), f32(6, 256, 128),
            f32(2, 16, QUART), bf(2, 16, QUART), bf(8, 16, QUART),
            f32(48, EMB), bf(2, 32, COLS), bf(2, 32, COLS), bf(8, 2, 32, COLS),
            bf(2, EMB, QUART), bf(EMB, COLS), bf(FF, COLS),
            bf(2, 4, 48, QUART), bf(2, 2, 4, 48, QUART), bf(2, 3, 48, QUART),
            f32(2, 48, QUART), bf(8, 16, QUART), bf(8, 16, QUART),
            bf(2, 96, COLS), bf(2, 336, COLS), bf(2, 2, 96, COLS), bf(2, 2, 336, COLS),
            bf(96, COLS), bf(336, COLS), bf(96, COLS), bf(336, COLS),
            bf(8, 64, COLS), bf(7, 64, COLS), f32(64, COLS),
            pltpu.SemaphoreType.DMA((COPIES,)),
            pltpu.SemaphoreType.DMA((COPIES,)),
        ],
        compiler_params=pltpu.CompilerParams(
            collective_id=1, has_side_effects=True, vmem_limit_bytes=62 << 20
        ),
        cost_estimate=pl.CostEstimate(
            flops=6 * TOK * 7667712, bytes_accessed=4 * 7667712, transcendentals=10 * TOK * EMB
        ),
        name="layer",
    )(*operands)


def finish_kernel(end_n, end_z, spread, out_in, grad_in, out, grad, vec, *mats):
    acceptor, address, content, sigmoid, mixer, ff_address, ff_content, ff_acceptor = mats
    out[...] = out_in[...]
    grad[...] = grad_in[...]
    acceptor[...] = end_n[0, 0:6, 0:768]
    address[...] = end_n[0, 0:6, 768:1536]
    content[...] = end_n[1, 0:6, 0:768]
    sigmoid[...] = end_n[1, 0:6, 768:1536]
    ff_address[:, 0:128] = end_n[0, 0:6, 1536:1664]
    ff_address[:, 128:1408] = end_n[0, 8:14, 0:1280]
    ff_address[:, 1408:2688] = end_n[1, 8:14, 0:1280]
    vec[...] = end_n[1, 0:8, VEC:QUART]
    columns = jnp.concatenate(
        [
            jnp.concatenate([end_z[0], end_z[1]], axis=1),
            jnp.concatenate([end_n[0, 8:16, 1280:1664], end_n[1, 8:16, 1280:1664]], axis=1),
        ],
        axis=0,
    )
    a, b, d = split(columns, 3)
    moved = mm_t(a, spread[...]) + (mm_t(b, spread[...]) + mm_t(d, spread[...]))
    mixer[...] = moved[0:6]
    ff_content[...] = moved[8:29]
    ff_acceptor[...] = moved[32:38]


def finish(end_n, end_z, spread, out, grad):
    shapes = [(TOK, EMB), (TOK, EMB), (8, 128)]
    shapes += [(6, EMB)] * 5 + [(6, FF), (21, EMB), (6, EMB)]
    return pl.pallas_call(
        finish_kernel,
        out_shape=tuple(jax.ShapeDtypeStruct(shape, F32) for shape in shapes),
        in_specs=[VMEM] * 5,
        out_specs=(VMEM,) * len(shapes),
        name="finish",
    )(end_n, end_z, spread, out, grad)


def per_device(
    incoming_activations,
    sequence_opening_memory,
    prior_standardize_factor,
    prior_standardize_offset,
    acceptor_lerp_factor,
    address_lerp_factor,
    content_lerp_factor,
    sigmoid_lerp_factor,
    acceptor_matrix,
    address_matrix,
    content_matrix,
    sigmoid_matrix,
    lane_fading_exponent,
    present_reward_vector,
    cluster_standardize_factor,
    cluster_standardize_offset,
    mixer_result_matrix,
    latter_standardize_factor,
    latter_standardize_offset,
    feedforward_address_lerp,
    feedforward_sigmoid_lerp,
    feedforward_address_matrix,
    feedforward_content_matrix,
    feedforward_acceptor_matrix,
    upstream_derivative,
):
    spread = jnp.asarray(_spread(), BF)
    vectors = jnp.stack(
        [prior_standardize_factor, prior_standardize_offset, acceptor_lerp_factor,
         address_lerp_factor, content_lerp_factor, sigmoid_lerp_factor,
         latter_standardize_factor, latter_standardize_offset, feedforward_address_lerp,
         feedforward_sigmoid_lerp, lane_fading_exponent, present_reward_vector,
         cluster_standardize_factor, cluster_standardize_offset], axis=0,
    )
    vectors = jnp.pad(vectors, ((0, 114), (0, 122)))
    memory = sequence_opening_memory.reshape(6, 2, 64, 64)
    nothing = jnp.zeros((6, 64, 64), F32)
    memory = jnp.concatenate(
        [jnp.concatenate([memory[:, 0], nothing], axis=2),
         jnp.concatenate([nothing, memory[:, 1]], axis=2)], axis=1,
    )
    out, in_grad, end_n, end_z = layer(
        incoming_activations, upstream_derivative, memory, spread,
        jnp.asarray(_line_pick(), BF), jnp.asarray(_plane_pick(), BF),
        jnp.asarray(_line_pick().T, BF), jnp.asarray(_plane_pick().T, BF),
        vectors, acceptor_matrix, address_matrix, content_matrix, sigmoid_matrix,
        mixer_result_matrix, feedforward_address_matrix, feedforward_content_matrix,
        feedforward_acceptor_matrix,
    )
    (out, in_grad, vec, acceptor, address, content, sigmoid, mixer,
     ff_address, ff_content, ff_acceptor) = finish(end_n, end_z, spread, out, in_grad)
    v = [vec[:6, i] for i in range(14)]
    return (
        out, in_grad,
        v[0], v[1], v[2], v[3], v[4], v[5],
        acceptor, address, content, sigmoid,
        v[10], v[11], v[12], v[13],
        mixer,
        v[6], v[7], v[8], v[9],
        ff_address, ff_content, ff_acceptor,
    )


def solution(mesh):
    r, v = P(("dp", "fsdp"), None), P(("dp", "fsdp"))
    state = P(("dp", "fsdp"), None, None, None)
    return jax.shard_map(
        per_device,
        mesh=mesh,
        in_specs=(r, state) + (v,) * 6 + (r,) * 4 + (v,) * 4 + (r,) + (v,) * 4 + (r,) * 4,
        out_specs=(r, r) + (v,) * 6 + (r,) * 4 + (v,) * 4 + (r,) + (v,) * 4 + (r,) * 3,
        check_vma=False,
    )
```

time: 195 us -> 157 us (0.81)
  Pallas kernels: 171 us -> 150 us
  local copies, waits for them, and re-layouts: 17.8 us -> 5.34 us
  matrix products: 2.85 us -> 0 us
  other arithmetic: 2.93 us -> 0.87 us
    pallas_call x2 -> x1, Pallas kernels: 139 us -> 3.71 us  [finish(): pl.pallas_call(finish_kernel, out_shape=tuple((jax.ShapeDtypeStruct(shape...]
    pallas_call x1, Pallas kernels: 31.2 us -> 146 us  [layer(): pl.pallas_call(layer_kernel, out_shape=(jax.ShapeDtypeStruct((TOK, EMB),...]
    another operation x15 -> x1, local copies, waits for them, and re-layouts: 10.7 us -> 1.56 us  [per_device(): jnp.stack([prior_standardize_factor, prior_standardize_offset, acceptor_l...]
    dot_general x2 -> x0, matrix products: 2.85 us -> none  [the longest x1 1.7 us: per_device(): columns = jnp.dot(columns, spread, preferred_element_type=F32).astype(BF)]
    unnamed x11 -> x0, local copies, waits for them, and re-layouts: 2.22 us -> none
where the time goes in v2:
time: 157 us; the launch traced here: 156 us
  Pallas kernels  150 us (96%)
  local copies, waits for them, and re-layouts  5.34 us (3%)
    pallas_call x1, Pallas kernels, layer(): pl.pallas_call(layer_kernel, out_shape=(jax.ShapeDtypeStruct((TOK, EMB),...  146 us
    pallas_call x1, Pallas kernels, finish(): pl.pallas_call(finish_kernel, out_shape=tuple((jax.ShapeDtypeStruct(shape...  3.71 us

profile of v2, /device:TPU:1, one launch (start us, length us, event | category | flops | bytes accessed | tf_op | source)
XLA Modules:
  0.0 156.4 jit_solution(5120717472510789046)
XLA Ops:
  0.7 1.6 stack.59
  2.2 0.6 pad.6.vecs
  2.8 1.0 slice_bitcast_fusion.1
  3.9 0.9 select_maximum_fusion.memory
  4.8 145.8 %layer.1 = (f32[128,768]{1,0:T(8,128)}, f32[128,768]{1,0:T(8,128)}, f32[2,16,1664]{2,1,0:T(8,128)}, f32[2,32,384]{2,1,0:T(8,128)}) custom-call(bf16[128,768]{1,0:T(8,128)(2,1)} %x_ref.1, bf16[128,768]{1,0:T(8,128)(2,1)} %up_ref.1, f32[6,128,128]{2,1,0:T(8,128)} %select_maximum_fusion.memory, bf16[768,768]{1,0:T(8,128)(2,1)} %constant.15.clone.spread, ...), custom_call_target="tpu_custom_call" | custom-call | flops 5888802816 | bytes 30670848 | tf_op jit(solution)/shard_map/layer/pallas_call | solution.py:750
  150.6 3.7 %finish.1 = (f32[128,768]{1,0:T(8,128)}, f32[128,768]{1,0:T(8,128)}, f32[8,128]{1,0:T(8,128)}, f32[6,768]{1,0:T(8,128)}, f32[6,768]{1,0:T(8,128)}, /*index=5*/f3...) custom-call(f32[2,16,1664]{2,1,0:T(8,128)} %get-tuple-element.39.end, ...), custom_call_target="tpu_custom_call" | custom-call | tf_op jit(solution)/shard_map/finish/pallas_call | solution.py:812
  154.3 2.1 %slice_reduce_fusion = (f32[6]{0:T(128)}, f32[6]{0:T(128)}, f32[6]{0:T(128)}, f32[6]{0:T(128)}, f32[6]{0:T(128)}, /*index=5*/f32[6]{0:T(128)}, f32[6]{0:T(128)},...) fusion(f32[8,128]{1,0:T(8,128)} %get-tuple-element.45), kind=kLoop, calls=%fused_computation.5 | loop fusion | bytes 672 | tf_op jit(solution)/shard_map/slice | solution.py:873

commit v3 on v2

v3 whole, which is shorter than its diff:
```python
from functools import partial

import jax
import jax.numpy as jnp
import numpy as np
from jax import lax
from jax.experimental import pallas as pl
from jax.experimental.pallas import tpu as pltpu
from jax.sharding import PartitionSpec as P

MESH = pl.DeviceIdType.MESH
BF = jnp.bfloat16
F32 = jnp.float32
VMEM = pl.BlockSpec(memory_space=pltpu.VMEM)

NORM_EPS = 1e-05
GROUP_EPS = 0.00064
TOK = 128
EMB = 768
FF = 2688
COLS = 384
SENDS, ARRIVALS = 96, 160
LEFT, RIGHT = 896, 768

WIDTH = {"A": 1664, "B": 1280, "C": 384, "R": 768, "K": 896}
VEC = 1536
ORDER = (0, 1, 3, 2)


def _order():
    order = np.zeros(EMB, np.int64)
    for x in range(4):
        for y in range(4):
            for z in range(4):
                for c in range(2):
                    device = z * 32 + (x % 2) * 16 + y * 4 + (x // 2) * 2 + c
                    place = (x * 4 + y) * 48 + (z * 2 + c) * 6
                    order[place : place + 6] = 6 * device + np.arange(6)
    return order


def _spread():
    spread = np.zeros((EMB, EMB), np.float32)
    spread[_order(), np.arange(EMB)] = 1.0
    return spread


def _line_pick():
    pick = np.zeros((96, 128), np.float32)
    for member in range(8):
        for r in range(6):
            pick[member * 6 + r, member * 16 + r] = 1.0
            pick[48 + member * 6 + r, member * 16 + 8 + r] = 1.0
    return pick


def _plane_pick():
    pick = np.zeros((432, 512), np.float32)
    for member in range(16):
        for r in range(6):
            pick[member * 6 + r, member * 32 + r] = 1.0
        for r in range(21):
            pick[96 + member * 21 + r, member * 32 + 8 + r] = 1.0
    return pick


def rem4(value):
    return lax.rem(value, 4)


class Place:
    def __init__(self):
        dp, fs = lax.axis_index("dp"), lax.axis_index("fsdp")
        self.z, self.xlo = lax.div(dp, 2), lax.rem(dp, 2)
        self.y, self.xhi = lax.div(fs, 4), lax.rem(lax.div(fs, 2), 2)
        self.c = lax.rem(fs, 2)
        self.x = self.xhi * 2 + self.xlo

    def device(self, z, y, x, c):
        return (z * 2 + lax.rem(x, 2), y * 4 + lax.div(x, 2) * 2 + c)

    def sibling(self):
        return self.device(self.z, self.y, self.x, 1 - self.c)

    def up(self, k):
        return self.device(rem4(self.z + k), self.y, self.x, self.c)

    def line(self, k):
        z = rem4(self.z + k // 2)
        core = self.c if k % 2 == 0 else 1 - self.c
        return self.device(z, self.y, self.x, core), z * 2 + core, core

    def turn(self, q, sibling=False):
        return 1 if q == "C" else (1 - self.c if sibling else self.c)

    def first(self, q, k):
        t = self.turn(q)
        y, x = rem4(self.y + k * (1 - t)), rem4(self.x + k * t)
        return self.device(self.z, y, x, self.c)

    def last(self, q, k):
        t = self.turn(q)
        y, x = rem4(self.y + k * t), rem4(self.x + k * (1 - t))
        return self.device(self.z, y, x, self.c)

    def band(self, q, m, k, sibling=False):
        t = self.turn(q, sibling)
        x = rem4(self.x + m * t + k * (1 - t))
        y = rem4(self.y + m * (1 - t) + k * t)
        return rows(48 * (x * 4 + y), 48)

    def across(self, k):
        return self.device(self.z, self.y, rem4(self.x + k), self.c)

    def side(self, k):
        return self.device(self.z, rem4(self.y + k), self.x, self.c)

    def twin(self):
        return self.device(self.z, self.y, self.xhi * 2 + 1 - self.xlo, self.c)

    def pair(self):
        return self.across(2)

    def order(self, m, k):
        return rem4(self.z + k) * 2 + (self.xlo if m == 0 else 1 - self.xlo)

    def greet(self):
        mates = [self.line(k)[0] for k in range(1, 8)]
        mates += [self.across(k) for k in (1, 2, 3)]
        mates += [self.side(k) for k in (1, 2, 3)]
        barrier = pltpu.get_barrier_semaphore()
        for mate in mates:
            pl.semaphore_signal(barrier, inc=1, device_id=mate, device_id_type=MESH)
        return lambda: pl.semaphore_wait(barrier, len(mates))


class Sender:
    def __init__(self, send_sems, recv_sems):
        self.send_sems, self.recv_sems = send_sems, recv_sems
        self.sends = self.arrivals = 0
        self.open = []
        self.groups = {}

    def send(self, source, target, device, group=None):
        index = self.sends % SENDS
        if len(self.open) >= SENDS:
            self.open.pop(0).wait_send()
        self.sends += 1
        if group not in self.groups:
            self.groups[group if group is not None else self.sends] = self.arrivals
            arrival = self.arrivals
            self.arrivals += 1
        else:
            arrival = self.groups[group]
        copy = pltpu.make_async_remote_copy(
            src_ref=source,
            dst_ref=target,
            send_sem=self.send_sems.at[index],
            recv_sem=self.recv_sems.at[arrival],
            device_id=device,
            device_id_type=MESH,
        )
        copy.start()
        self.open.append(copy)
        return copy

    def wait_group(self, group, like, device):
        pltpu.make_async_remote_copy(
            src_ref=like,
            dst_ref=like,
            send_sem=self.send_sems.at[0],
            recv_sem=self.recv_sems.at[self.groups[group]],
            device_id=device,
            device_id_type=MESH,
        ).wait_recv()

    def drain(self):
        for copy in self.open:
            copy.wait_send()
        self.open = []


def rows(start, size, unit=16):
    return pl.ds(pl.multiple_of(start, unit), size)


def mm(left, right):
    return jnp.dot(left, right, preferred_element_type=F32)


def mm_t(left, right):
    return lax.dot_general(left, right, (((1,), (1,)), ((), ())), preferred_element_type=F32)


def t_mm(left, right):
    return lax.dot_general(left, right, (((0,), (0,)), ((), ())), preferred_element_type=F32)


def split(value, parts):
    found = []
    for _ in range(parts - 1):
        high = value.astype(BF)
        found.append(high)
        value = value - high.astype(F32)
    found.append(value.astype(BF))
    return found


def fine(dims, left, right):
    lh, ll = split(left, 2)
    rh, rl = split(right, 2)
    dot = partial(lax.dot_general, dimension_numbers=(dims, ((), ())), preferred_element_type=F32)
    return dot(lh, rh) + (dot(lh, rl) + dot(ll, rh))


NN, NT, TN = ((1,), (0,)), ((1,), (1,)), ((0,), (0,))


def wide(ref):
    return ref[...].astype(F32)


def layer_kernel(
    x_in, up_in, state, spread_in, pick_n_in, pick_z_in, turn_n_in, turn_z_in, *refs
):
    vecs, refs = refs[:14], refs[14:]
    (acceptor, address, content, sigmoid, mixer, ff_address, ff_content, ff_acceptor), refs = refs[:8], refs[8:]
    (
        out_ref, in_grad_ref, end_n, end_z,
        x_ref, up_ref, state_v, spread, pick_n, pick_z, turn_n, turn_z, memory,
        wa, wb, wc, wo, w2, gk, gb, gc, scores,
        vec_f, pack_f, pack_n, stage_a, stage_b, cols_f, pack_z, half_z, pair_z, stage_z,
        sib_r, sib_k, sib_b, sib_c, relay_r, relay_k, relay_b, relay_c,
        last_r, last_k, last_b, last_c, first_r, first_k, first_b, first_c,
        acc_r, acc_k, acc_b, acc_c,
        piece_a, piece_b, line_a, line_b,
        sib_o, sib_2, relay_o, relay_2, up_o, up_2, sent_o, sent_2, twin_o, twin_2,
        piece_z, side_z, half_f, sent_z, got_z, swap_f,
        send_sems, recv_sems, load_sems,
    ) = refs
    at = Place()
    c = at.c
    sib = at.sibling()
    net = Sender(send_sems, recv_sems)
    met = at.greet()

    loads = {}
    for i, (name, source, target) in enumerate([
        ("spread", spread_in, spread), ("x", x_in, x_ref), ("pick_n", pick_n_in, pick_n),
        ("up", up_in, up_ref), ("pick_z", pick_z_in, pick_z), ("state", state, state_v),
        ("turn_n", turn_n_in, turn_n), ("turn_z", turn_z_in, turn_z),
    ]):
        loads[name] = pltpu.make_async_copy(source, target, load_sems.at[i])
        loads[name].start()

    vec_f[...] = jnp.zeros_like(vec_f)
    for i, ref in enumerate(vecs):
        vec_f[i : i + 1, 0:6] = wide(ref).reshape(1, 6)
    eye = (
        lax.broadcasted_iota(jnp.int32, (16, 128), 0)
        == lax.broadcasted_iota(jnp.int32, (16, 128), 1)
    ).astype(F32).astype(BF)
    pack_f[...] = jnp.zeros_like(pack_f)
    pack_f[0, 0, 0:6, 0:768] = wide(acceptor)
    pack_f[0, 0, 0:6, 768:896] = wide(address.at[:, 0:128])
    pack_f[0, 0, 8:14, 0:640] = wide(address.at[:, 128:768])
    pack_f[0, 0, 8:14, 640:768] = wide(ff_address.at[:, 0:128])
    pack_f[1, 0, 0:6, 0:768] = wide(content)
    pack_f[1, 0, 0:6, 768:896] = wide(sigmoid.at[:, 0:128])
    pack_f[1, 0, 8:14, 0:640] = wide(sigmoid.at[:, 128:768])
    pack_f[1, 0, 8:14, 640:768] = mm_t(eye, vec_f[...].astype(BF))[0:6]
    for h in range(2):
        pack_n[0, h] = pack_f[h, 0].astype(BF)
    met()

    own = at.z * 2 + c

    def send_lines(i, stage):
        for k in range(1, 8):
            mate, _, core = at.line(k)
            net.send(pack_n.at[i, core], stage.at[own], mate, ("lines", i))
        stage[own] = pack_n[i, c]

    send_lines(0, stage_a)
    cols_f[...] = jnp.zeros_like(cols_f)
    cols_f[0:6] = wide(mixer)
    cols_f[8:29] = wide(ff_content)
    cols_f[32:38] = wide(ff_acceptor)
    loads["spread"].wait()
    moved = mm(cols_f[...].astype(BF), spread[...])
    for h in range(2):
        pack_z[h] = moved[0:32, COLS * h : COLS * h + COLS].astype(BF)
        first_col = 128 + 1280 * h
        pack_f[h, 1, 0:6, 0:896] = wide(ff_address.at[:, first_col : first_col + 896])
        pack_f[h, 1, 8:14, 0:384] = wide(ff_address.at[:, first_col + 896 : first_col + 1280])
        pack_f[h, 1, 8:16, 384:768] = moved[32:40, COLS * h : COLS * h + COLS]
        pack_n[1, h] = pack_f[h, 1].astype(BF)
    swap_z = net.send(pack_z.at[1 - c], half_z.at[c], sib)
    half_z[c] = pack_z[c]
    send_lines(1, stage_b)

    loads["x"].wait()
    tokens = mm(x_ref[...], spread[...])
    centred = tokens - jnp.mean(tokens, axis=-1, keepdims=True)
    scale1 = lax.rsqrt(jnp.mean(centred * centred, axis=-1, keepdims=True) + NORM_EPS)
    unit1 = centred * scale1
    loads["up"].wait()
    upstream = mm(up_ref[...], spread[...])
    swap_z.wait_recv()
    to_pair = net.send(half_z, pair_z.at[at.xhi], at.pair())
    pair_z[at.xhi] = half_z[...]
    loads["pick_n"].wait()
    for name in ("state", "turn_n", "turn_z", "pick_z"):
        loads[name].wait()
    blank = jnp.zeros((64, 64), F32)
    for g in range(6):
        memory[g, 0:64] = jnp.concatenate([state_v[2 * g], blank], axis=1)
        memory[g, 64:128] = jnp.concatenate([blank, state_v[2 * g + 1]], axis=1)

    def pick(i, stage):
        net.wait_group(("lines", i), stage.at[0:7], sib)
        return mm(pick_n[...], stage[...].reshape(128, LEFT)).astype(BF)

    full = {"A": wa, "B": wb, "C": wc, "o": wo, "2": w2}

    def place_n(q, m, k):
        return full[q].at[c, at.band(q, m, k)]

    firsts, lasts = {}, {}

    def pass_on(q, m):
        spot = place_n(q, 4 - m, 0)
        for k in (1, 3):
            lasts[q, m, k] = net.send(spot, spot, at.last(q, k))
        net.send(spot, spot, sib, ("sib", q))

    def begin(q, *parts):
        spot = place_n(q, 0, 0)
        spot[...] = jnp.concatenate(parts, axis=1) if len(parts) > 1 else parts[0]
        for k in (1, 3, 2):
            firsts[q, k] = net.send(spot, spot, at.first(q, k))
        pass_on(q, 0)

    def relay(q, m):
        firsts[q, m].wait_recv()
        pass_on(q, m)

    def arrive(q, m, k):
        lasts[q, m, k].wait_recv()
        spot = place_n(q, 4 - m, 4 - k)
        if k == (1 if m % 2 == 0 else 3):
            lasts[q, m, 2] = net.send(spot, spot, at.last(q, k))
        net.send(spot, spot, sib, ("sib", q))

    def arrive_far(q, m):
        lasts[q, m, 2].wait_recv()
        spot = place_n(q, 4 - m, 2)
        net.send(spot, spot, sib, ("sib", q))

    def place_z(w, m, k):
        unit = 96 if w == "o" else 336
        return full[w].at[c, rows(unit * at.order(m, k), unit)]

    def pass_z(w, m):
        spot = place_z(w, m, 0)
        for k in (1, 3):
            lasts[w, m, k] = net.send(spot, spot, at.up(k))
        net.send(spot, spot, sib, ("sib", w))

    def relay_z(w):
        firsts[w].wait_recv()
        pass_z(w, 1)

    def arrive_z(w, m, k):
        lasts[w, m, k].wait_recv()
        spot = place_z(w, m, 4 - k)
        if k == (1 if m == 0 else 3):
            lasts[w, m, 2] = net.send(spot, spot, at.up(k))
        net.send(spot, spot, sib, ("sib", w))

    def arrive_z_far(w, m):
        lasts[w, m, 2].wait_recv()
        spot = place_z(w, m, 2)
        net.send(spot, spot, sib, ("sib", w))

    picked = pick(0, stage_a)
    begin("A", picked[0:48], picked[48:96, 0:RIGHT])
    to_pair.wait_recv()
    for k in (1, 2, 3):
        net.send(pair_z, stage_z.at[at.y], at.side(k), "side")
    stage_z[at.y] = pair_z[...]
    relay("A", 1)
    relay("A", 3)
    for k in (1, 3):
        arrive("A", 0, k)
    picked = pick(1, stage_b)
    relay("A", 2)
    begin("B", picked[0:48], picked[48:96, 0:384])
    begin("C", picked[48:96, 384:768])
    net.wait_group("side", stage_z.at[0:3], sib)
    picked_z = mm(pick_z[...], stage_z[...].reshape(512, COLS)).astype(BF)
    place_z("o", 0, 0)[...] = picked_z[:96]
    place_z("2", 0, 0)[...] = picked_z[96:]
    for w in ("o", "2"):
        spot = place_z(w, 0, 0)
        firsts[w] = net.send(spot, spot, at.twin())
        pass_z(w, 0)
    for m in (1, 3):
        for k in (1, 3):
            arrive("A", m, k)
    arrive_far("A", 0)
    relay("B", 1)
    relay("B", 3)
    for k in (1, 3):
        arrive("A", 2, k)
    for w in ("o", "2"):
        relay_z(w)
    relay("B", 2)
    for m in (1, 3, 2):
        relay("C", m)
    for m in (1, 3, 2):
        arrive_far("A", m)
    tasks = []

    def plan(kind, *steps_):
        for step in steps_:
            tasks.append((kind, step))

    for m in (0, 1):
        for k in (1, 3):
            plan("B", partial(arrive, "B", m, k))
            plan("o", partial(arrive_z, "o", m, k))
            plan("2", partial(arrive_z, "2", m, k))
    for m in (0, 1):
        plan("o", partial(arrive_z_far, "o", m))
    for m in (3, 2):
        for k in (1, 3):
            plan("B", partial(arrive, "B", m, k))
    for m in ORDER:
        for k in (1, 3):
            plan("C", partial(arrive, "C", m, k))
    for m in (0, 1):
        plan("2", partial(arrive_z_far, "2", m))
    for q in ("B", "C"):
        for m in ORDER:
            plan(q, partial(arrive_far, q, m))

    def work(count=1000):
        for _ in range(min(count, len(tasks))):
            tasks.pop(0)[1]()

    def need(q):
        while any(kind == q for kind, _ in tasks):
            work(1)
        net.wait_group(("sib", q), full[q].at[1 - c], sib)

    need("A")

    lanes = lax.broadcasted_iota(jnp.int32, (1, 128), 1)
    left_head = lanes < 64
    token = lax.broadcasted_iota(jnp.int32, (TOK, 1), 0)

    def shift_down(value):
        return jnp.where(token == 0, 0.0, pltpu.roll(value, 1, 0))

    def shift_up(value):
        return jnp.where(token == TOK - 1, 0.0, pltpu.roll(value, TOK - 1, 0))

    def mean(value):
        return jnp.mean(value, axis=-1, keepdims=True)

    def tsum(value):
        return jnp.sum(value, axis=0, keepdims=True)

    def unspread(value):
        a, b, d = split(value, 3)
        return mm_t(a, spread[...]) + (mm_t(b, spread[...]) + mm_t(d, spread[...]))

    vec = mm_t(eye, wa[1, :, VEC:1664])
    gain1, bias1 = vec[0:1], vec[1:2]
    lerps = [vec[2 + i : 3 + i] for i in range(4)]
    gain2, bias2, lerp_h, lerp_g = vec[6:7], vec[7:8], vec[8:9], vec[9:10]
    heads = mm_t(vec.astype(BF), spread[...])
    rate, bonus, gain_w, bias_w = heads[10:11], heads[11:12], heads[12:13], heads[13:14]

    pair_rows = lax.broadcasted_iota(jnp.int32, (256, 128), 0)
    pair_cols = lax.broadcasted_iota(jnp.int32, (256, 128), 1)
    pair_ones = ((lax.rem(pair_rows, 128) // 64) == (pair_cols // 64)).astype(F32).astype(BF)
    below = lax.rem(pair_rows, 128) > pair_cols

    def head_sum(value):
        found = []
        for g in range(6):
            part = value[:, 128 * g : 128 * g + 128]
            found.append(mm(jnp.concatenate(split(part, 2), axis=1), pair_ones))
        return jnp.concatenate(found, axis=1)

    def stack(value):
        return jnp.concatenate(
            [jnp.where(left_head, value, 0.0), jnp.where(left_head, 0.0, value)], axis=0
        )

    def beside(value):
        return jnp.concatenate([value[:TOK], value[TOK:]], axis=1)

    normed = unit1 * gain1 + bias1
    previous = shift_down(normed)
    blended = [(normed * l + previous * (1.0 - l)).astype(BF) for l in lerps]
    recept = mm(blended[0], wa[0, :, 0:768])
    keys = mm(blended[1], wa[0, :, 768:1536])
    vals = mm(blended[2], wa[1, :, 0:768])
    gate_pre = mm(blended[3], wa[1, :, 768:1536])
    work(6)

    fade = -jnp.exp(rate)
    steps = token.astype(F32)
    fall_r = jnp.exp(steps * fade)
    fall_k = jnp.exp(-(steps + 1.0) * fade)
    recept_f = recept * fall_r
    keys_f = keys * fall_k
    present = head_sum(recept * bonus * keys)
    parts = []
    for g in range(6):
        cut = slice(128 * g, 128 * g + 128)
        rg, kg, vg = recept_f[:, cut], keys_f[:, cut], vals[:, cut]
        sc = jnp.where(below, fine(NT, stack(rg), kg), 0.0)
        scores[g] = sc
        parts.append(fine(NN, beside(sc), stack(vg)) + fine(NN, rg, memory[g]))
        if g % 2 == 1:
            work(4)
    wkv = jnp.concatenate(parts, axis=1) + present * vals

    centred_w = wkv - head_sum(wkv) * (1.0 / 64.0)
    scale_w = lax.rsqrt(head_sum(centred_w * centred_w) * (1.0 / 64.0) + GROUP_EPS)
    unit_w = centred_w * scale_w
    grouped = unit_w * gain_w + bias_w
    sig = 1.0 / (1.0 + jnp.exp(-gate_pre))
    silu = gate_pre * sig
    gated = (grouped * silu).astype(BF)
    need("o")
    middle = tokens + jnp.concatenate([mm(gated, wo[0]), mm(gated, wo[1])], axis=1)

    centred = middle - mean(middle)
    scale2 = lax.rsqrt(mean(centred * centred) + NORM_EPS)
    unit2 = centred * scale2
    normed2 = unit2 * gain2 + bias2
    previous2 = shift_down(normed2)
    mixed_h = (normed2 * lerp_h + previous2 * (1.0 - lerp_h)).astype(BF)
    mixed_g = (normed2 * lerp_g + previous2 * (1.0 - lerp_g)).astype(BF)
    need("B")
    need("C")
    pre = jnp.concatenate(
        [mm(mixed_h, wa[0, :, 1536:1664]), mm(mixed_h, wb[0]), mm(mixed_h, wb[1])], axis=1
    )
    pre = jnp.maximum(pre, 0.0)
    hidden = (pre * pre).astype(BF)
    gating = jnp.concatenate([mm(mixed_g, wc[0]), mm(mixed_g, wc[1])], axis=1)
    gating = 1.0 / (1.0 + jnp.exp(-gating))
    grad_vo = upstream * gating
    grad_vo_low = grad_vo.astype(BF)
    swaps = {}

    def fold(mine, other, *more):
        total = wide(mine) + wide(other)
        for ref in more:
            total += wide(ref)
        return total

    gr, go = wb.at[:, :, 0:768], wb.at[:, :, 768:1152]
    grads = {"R": gr, "K": gk, "B": gb, "C": gc}
    sib_of = {"R": sib_r, "K": sib_k, "B": sib_b, "C": sib_c}
    relay_of = {"R": relay_r, "K": relay_k, "B": relay_b, "C": relay_c}
    last_of = {"R": last_r, "K": last_k, "B": last_b, "C": last_c}
    first_of = {"R": first_r, "K": first_k, "B": first_b, "C": first_c}
    acc_of = {"R": acc_r, "K": acc_k, "B": acc_b, "C": acc_c}

    def swap(q):
        swaps[q] = net.send(grads[q].at[1 - c], sib_of[q], sib)

    def swapped(q):
        if q in swaps:
            swaps.pop(q).wait_recv()

    def scatter_far(q, m):
        part = at.band(q, m, 2)
        via = 1 if m % 2 == 0 else 3
        swapped(q)
        spot = sib_of[q].at[part]
        spot[...] = fold(grads[q].at[c, part], spot).astype(BF)
        lasts["g", q, m, 2] = net.send(spot, relay_of[q].at[m], at.last(q, via))

    def scatter_near(q, m, k):
        part = at.band(q, m, k)
        spot = sib_of[q].at[part]
        more = []
        if k == (1 if m % 2 == 0 else 3):
            lasts["g", q, m, 2].wait_recv()
            more = [relay_of[q].at[m]]
        spot[...] = fold(grads[q].at[c, part], spot, *more).astype(BF)
        lasts["g", q, m, k] = net.send(spot, last_of[q].at[k // 2, m], at.last(q, k))

    def scatter_own(q, m):
        part = at.band(q, m, 0)
        spot = sib_of[q].at[part]
        lasts["g", q, m, 1].wait_recv()
        lasts["g", q, m, 3].wait_recv()
        arrived = last_of[q]
        total = fold(grads[q].at[c, part], spot, arrived.at[0, m], arrived.at[1, m])
        if m == 0:
            acc_of[q][...] = total
        else:
            spot[...] = total.astype(BF)
            firsts["g", q, m] = net.send(spot, first_of[q].at[m - 1], at.first(q, m))

    def scatter_end(q):
        total = acc_of[q][...]
        for m in (1, 3, 2):
            firsts["g", q, m].wait_recv()
            total += wide(first_of[q].at[m - 1])
        acc_of[q][...] = total

    def spread_lines(i, left, right, piece, line):
        right = jnp.concatenate([right, jnp.zeros((48, LEFT - RIGHT), F32)], axis=1)
        table = jnp.concatenate([left, right], axis=0).astype(BF)
        piece[...] = mm(turn_n[...], table).astype(BF).reshape(8, 16, LEFT)
        for k in range(1, 8):
            mate, index, _ = at.line(k)
            net.send(piece.at[index], line.at[own], mate, ("grad lines", i))
        line[own] = piece[own]

    def sum_lines(i, line):
        net.wait_group(("grad lines", i), line.at[0:7], sib)
        for h in range(2):
            total = wide(line.at[h])
            for z in (1, 2, 3):
                total += wide(line.at[2 * z + h])
            end_n[h, i] = total

    def scatter_steps(q):
        steps_ = [partial(scatter_far, q, m) for m in ORDER]
        for late in (False, True):
            for m in ORDER:
                for k in (1, 3):
                    if late == (k == (1 if m % 2 == 0 else 3)):
                        steps_.append(partial(scatter_near, q, m, k))
        steps_ += [partial(scatter_own, q, m) for m in (1, 3, 2, 0)]
        steps_.append(partial(scatter_end, q))
        return steps_

    z_parts = {
        "o": (96, go, sib_o, relay_o, up_o, sent_o, twin_o),
        "2": (336, w2, sib_2, relay_2, up_2, sent_2, twin_2),
    }

    def swap_w(w):
        unit, mine, theirs = z_parts[w][:3]
        swaps[w] = net.send(mine.at[1 - c], theirs, sib)

    def part_w(w, m, k):
        unit = z_parts[w][0]
        return rows(unit * at.order(m, k), unit)

    def scatter_far_w(w, m):
        unit, mine, theirs, relayed = z_parts[w][:4]
        part = part_w(w, m, 2)
        swapped(w)
        spot = theirs.at[part]
        spot[...] = fold(mine.at[c, part], spot).astype(BF)
        lasts["g", w, m, 2] = net.send(spot, relayed.at[m], at.up(1 if m == 0 else 3))

    def scatter_near_w(w, m, k):
        unit, mine, theirs, relayed, arrived = z_parts[w][:5]
        part = part_w(w, m, k)
        more = []
        if k == (1 if m == 0 else 3):
            lasts["g", w, m, 2].wait_recv()
            more = [relayed.at[m]]
        spot = theirs.at[part]
        spot[...] = fold(mine.at[c, part], spot, *more).astype(BF)
        lasts["g", w, m, k] = net.send(spot, arrived.at[k // 2, m], at.up(k))

    def scatter_own_w(w, m):
        unit, mine, theirs, relayed, arrived, sent, twin = z_parts[w]
        part = part_w(w, m, 0)
        lasts["g", w, m, 1].wait_recv()
        lasts["g", w, m, 3].wait_recv()
        total = fold(mine.at[c, part], theirs.at[part], arrived.at[0, m], arrived.at[1, m])
        if m == 1:
            sent[...] = total.astype(BF)
            firsts["g", w] = net.send(sent, twin, at.twin())
        else:
            firsts["g", w].wait_recv()
            sums_z[w] = (total + wide(twin)).astype(BF)

    def scatter_steps_w(w):
        steps_ = [partial(scatter_far_w, w, 0), partial(scatter_far_w, w, 1)]
        steps_ += [partial(scatter_near_w, w, 1, 1), partial(scatter_near_w, w, 0, 3)]
        steps_ += [partial(scatter_near_w, w, 0, 1), partial(scatter_near_w, w, 1, 3)]
        steps_ += [partial(scatter_own_w, w, 1), partial(scatter_own_w, w, 0)]
        return steps_

    sums_z = {}

    need("2")
    steps_2, steps_o = scatter_steps_w("2"), scatter_steps_w("o")
    steps_b, steps_c = scatter_steps("B"), scatter_steps("C")
    steps_r, steps_k = scatter_steps("R"), scatter_steps("K")

    def run(*steps_):
        for step in steps_:
            step()

    grad_hidden = mm_t(grad_vo_low[:, :COLS], w2[0]) + mm_t(grad_vo_low[:, COLS:], w2[1])
    grad_pre = (grad_hidden * 2.0 * pre).astype(BF)
    gb[0] = t_mm(mixed_h, grad_pre[:, 128:1408]).astype(BF)
    gb[1] = t_mm(mixed_h, grad_pre[:, 1408:]).astype(BF)
    swap("B")
    value_out = jnp.concatenate([mm(hidden, w2[0]), mm(hidden, w2[1])], axis=1)
    layer_out = middle + gating * value_out
    net.drain()
    for h in range(2):
        w2[h] = t_mm(hidden, grad_vo_low[:, COLS * h : COLS * h + COLS]).astype(BF)
    swap_w("2")
    run(*steps_b[:8])
    grad_gp = (grad_vo * value_out * (1.0 - gating)).astype(BF)
    for h in range(2):
        gc[h] = t_mm(mixed_g, grad_gp[:, COLS * h : COLS * h + COLS]).astype(BF)
    swap("C")
    run(*steps_2[:4])
    grad_mg = mm_t(grad_gp[:, :COLS], wc[0]) + mm_t(grad_gp[:, COLS:], wc[1])
    grad_mh = mm_t(grad_pre[:, :128], wa[0, :, 1536:1664])
    grad_mh += mm_t(grad_pre[:, 128:1408], wb[0]) + mm_t(grad_pre[:, 1408:], wb[1])
    gk[0, :, 768:896] = t_mm(mixed_h, grad_pre[:, :128]).astype(BF)
    run(*steps_c[:8])

    grad_n2 = grad_mh * lerp_h + grad_mg * lerp_g
    grad_n2 += shift_up(grad_mh * (1.0 - lerp_h) + grad_mg * (1.0 - lerp_g))
    delta2 = normed2 - previous2
    g_lerp_h, g_lerp_g = tsum(grad_mh * delta2), tsum(grad_mg * delta2)
    g_gain2, g_bias2 = tsum(grad_n2 * unit2), tsum(grad_n2)
    q2 = grad_n2 * gain2
    grad_middle = upstream + scale2 * (q2 - mean(q2) - unit2 * mean(q2 * unit2))

    grad_attn = grad_middle.astype(BF)
    grad_gated = mm_t(grad_attn[:, :COLS], wo[0]) + mm_t(grad_attn[:, COLS:], wo[1])
    for h in range(2):
        go[h] = t_mm(gated, grad_attn[:, COLS * h : COLS * h + COLS]).astype(BF)
    swap_w("o")
    grad_gate = (grad_gated * grouped * (sig * (1.0 + gate_pre * (1.0 - sig)))).astype(BF)
    grad_grouped = grad_gated * silu
    g_gain_w, g_bias_w = tsum(grad_grouped * unit_w), tsum(grad_grouped)
    qw = grad_grouped * gain_w
    grad_wkv = scale_w * (
        qw
        - head_sum(qw) * (1.0 / 64.0)
        - unit_w * (head_sum(qw * unit_w) * (1.0 / 64.0))
    )

    weight = head_sum(grad_wkv * vals)
    parts_r, parts_k, parts_v = [], [], []
    for g in range(6):
        cut = slice(128 * g, 128 * g + 128)
        rg, kg, vg, dg = recept_f[:, cut], keys_f[:, cut], vals[:, cut], grad_wkv[:, cut]
        ds = stack(dg)
        da = jnp.where(below, fine(NT, ds, vg), 0.0)
        parts_r.append(fine(NN, beside(da), stack(kg)) + fine(NT, dg, memory[g]))
        parts_k.append(fine(TN, da, stack(rg)))
        parts_v.append(fine(TN, scores[g], ds))
        if g == 0:
            run(*steps_o[:4])
        if g == 3:
            run(*steps_2[4:6], *steps_b[8:12])
    grad_r = jnp.concatenate(parts_r, axis=1) * fall_r
    grad_k = jnp.concatenate(parts_k, axis=1) * fall_k
    grad_v = jnp.concatenate(parts_v, axis=1) + grad_wkv * present
    g_rate = fade * tsum(steps * recept * grad_r - (steps + 1.0) * keys * grad_k)
    g_bonus = tsum(recept * keys * weight)
    grad_r = (grad_r + bonus * keys * weight).astype(BF)
    grad_k = (grad_k + bonus * recept * weight).astype(BF)
    grad_v = grad_v.astype(BF)

    gr[0] = t_mm(blended[0], grad_r).astype(BF)
    gr[1] = t_mm(blended[2], grad_v).astype(BF)
    swap("R")
    gk[0, :, 0:768] = t_mm(blended[1], grad_k).astype(BF)
    gk[1, :, 0:768] = t_mm(blended[3], grad_gate).astype(BF)
    grad_blended = [
        mm_t(grad_r, wa[0, :, 0:768]),
        mm_t(grad_k, wa[0, :, 768:1536]),
        mm_t(grad_v, wa[1, :, 0:768]),
        mm_t(grad_gate, wa[1, :, 768:1536]),
    ]
    run(*steps_c[8:12], *steps_o[4:6], *steps_r[:8])
    delta = normed - previous
    g_lerps = [tsum(g * delta) for g in grad_blended]
    grad_n1 = sum(g * l for g, l in zip(grad_blended, lerps))
    grad_n1 += shift_up(sum(g * (1.0 - l) for g, l in zip(grad_blended, lerps)))
    g_gain1, g_bias1 = tsum(grad_n1 * unit1), tsum(grad_n1)

    zero = jnp.zeros((1, EMB), F32)
    natural = jnp.concatenate([g_rate, g_bonus, g_gain_w, g_bias_w] + [zero] * 4, axis=0)
    va, vb, vc = split(natural, 3)
    moved = mm(va, spread[...]) + (mm(vb, spread[...]) + mm(vc, spread[...]))
    table = jnp.concatenate(
        [g_gain1, g_bias1] + g_lerps + [g_gain2, g_bias2, g_lerp_h, g_lerp_g]
        + [moved[0:4], jnp.zeros((114, EMB), F32)],
        axis=0,
    )
    gk[1, :, 768:896] = table.T.astype(BF)
    swap("K")
    run(*steps_b[12:16], *steps_k[:8], *steps_2[6:8], *steps_o[6:8])
    run(*steps_r[8:12], *steps_c[12:16], *steps_k[8:12])

    spread_z = mm(turn_z[:, :96], sums_z["o"]) + mm(turn_z[:, 96:], sums_z["2"])
    piece_z[...] = spread_z.astype(BF).reshape(4, 128, COLS)
    for k in (1, 2, 3):
        net.send(piece_z.at[rem4(at.y + k)], side_z.at[k - 1], at.side(k), "grad side")
    run(steps_b[16], steps_c[16])
    spread_lines(
        1, acc_b[:, 0:LEFT], jnp.concatenate([acc_b[:, LEFT:], acc_c[...]], axis=1), piece_b, line_b
    )
    out_ref[...] = unspread(layer_out)
    run(*steps_r[12:16])
    q1 = grad_n1 * gain1
    grad_x = grad_middle + scale1 * (q1 - mean(q1) - unit1 * mean(q1 * unit1))
    in_grad_ref[...] = unspread(grad_x)
    run(*steps_k[12:16])
    net.wait_group("grad side", side_z, sib)
    total = wide(piece_z.at[at.y])
    for k in (1, 2, 3):
        total += wide(side_z.at[k - 1])
    half_f[...] = total.reshape(2, 64, COLS)
    sent_z[...] = half_f[1 - at.xhi].astype(BF)
    to_pair = net.send(sent_z, got_z, at.pair())
    run(steps_r[16], steps_k[16])
    acc_a = jnp.concatenate([acc_r[...], acc_k[...]], axis=1)
    spread_lines(0, acc_a[:, 0:LEFT], acc_a[:, LEFT:], piece_a, line_a)
    to_pair.wait_recv()
    swap_f[...] = half_f[at.xhi] + wide(got_z)
    away, kept = rows(32 * (1 - c), 32, 8), rows(32 * c, 32, 8)
    last_swap = net.send(swap_f.at[away], end_z.at[c], sib)
    end_z[c] = swap_f[kept]
    sum_lines(1, line_b)
    last_swap.wait_recv()
    sum_lines(0, line_a)
    net.drain()


def layer(*operands):
    bf = lambda *shape: pltpu.VMEM(shape, BF)
    f32 = lambda *shape: pltpu.VMEM(shape, F32)
    a, b, d, r, k = (WIDTH[q] for q in "ABCRK")
    return pl.pallas_call(
        layer_kernel,
        out_shape=(
            jax.ShapeDtypeStruct((TOK, EMB), F32),
            jax.ShapeDtypeStruct((TOK, EMB), F32),
            jax.ShapeDtypeStruct((2, 2, 16, LEFT), F32),
            jax.ShapeDtypeStruct((2, 32, COLS), F32),
        ),
        in_specs=[pl.BlockSpec(memory_space=pl.ANY)] * 8 + [VMEM] * (len(operands) - 8),
        out_specs=(VMEM,) * 4,
        scratch_shapes=[
            bf(TOK, EMB), bf(TOK, EMB), f32(12, 64, 64), bf(EMB, EMB),
            bf(96, 128), bf(432, 512), bf(128, 96), bf(512, 432), f32(6, 128, 128),
            bf(2, EMB, a), bf(2, EMB, b), bf(2, EMB, d), bf(2, EMB, COLS), bf(2, FF, COLS),
            bf(2, EMB, k), bf(2, EMB, b), bf(2, EMB, d), f32(6, 256, 128),
            f32(128, 128), f32(2, 2, 16, LEFT), bf(2, 2, 16, LEFT), bf(8, 16, LEFT), bf(8, 16, LEFT),
            f32(48, EMB), bf(2, 32, COLS), bf(2, 32, COLS), bf(2, 2, 32, COLS), bf(4, 2, 2, 32, COLS),
            *(bf(EMB, w) for w in (r, k, b, d)), *(bf(4, 48, w) for w in (r, k, b, d)),
            *(bf(2, 4, 48, w) for w in (r, k, b, d)), *(bf(3, 48, w) for w in (r, k, b, d)),
            *(f32(48, w) for w in (r, k, b, d)),
            bf(8, 16, LEFT), bf(8, 16, LEFT), bf(8, 16, LEFT), bf(8, 16, LEFT),
            bf(EMB, COLS), bf(FF, COLS),
            bf(2, 96, COLS), bf(2, 336, COLS), bf(2, 2, 96, COLS), bf(2, 2, 336, COLS),
            bf(96, COLS), bf(336, COLS), bf(96, COLS), bf(336, COLS),
            bf(4, 128, COLS), bf(3, 128, COLS), f32(2, 64, COLS), bf(64, COLS), bf(64, COLS),
            f32(64, COLS),
            pltpu.SemaphoreType.DMA((SENDS,)),
            pltpu.SemaphoreType.DMA((ARRIVALS,)),
            pltpu.SemaphoreType.DMA((8,)),
        ],
        compiler_params=pltpu.CompilerParams(
            collective_id=1, has_side_effects=True, vmem_limit_bytes=62 << 20
        ),
        cost_estimate=pl.CostEstimate(
            flops=6 * TOK * 7667712, bytes_accessed=4 * 7667712, transcendentals=10 * TOK * EMB
        ),
        name="layer",
    )(*operands)


def finish_kernel(end_n, end_z, spread, out_in, grad_in, out, grad, *refs):
    vecs, mats = refs[:14], refs[14:]
    acceptor, address, content, sigmoid, mixer, ff_address, ff_content, ff_acceptor = mats
    out[...] = out_in[...]
    grad[...] = grad_in[...]
    acceptor[...] = end_n[0, 0, 0:6, 0:768]
    address[:, 0:128] = end_n[0, 0, 0:6, 768:896]
    address[:, 128:768] = end_n[0, 0, 8:14, 0:640]
    content[...] = end_n[1, 0, 0:6, 0:768]
    sigmoid[:, 0:128] = end_n[1, 0, 0:6, 768:896]
    sigmoid[:, 128:768] = end_n[1, 0, 8:14, 0:640]
    ff_address[:, 0:128] = end_n[0, 0, 8:14, 640:768]
    for h in range(2):
        first_col = 128 + 1280 * h
        ff_address[:, first_col : first_col + 896] = end_n[h, 1, 0:6, 0:896]
        ff_address[:, first_col + 896 : first_col + 1280] = end_n[h, 1, 8:14, 0:384]
    table = jnp.concatenate([end_n[1, 0, 8:16, 640:768], jnp.zeros((120, 128), F32)], axis=0).T
    for i, ref in enumerate(vecs):
        ref[...] = table[i : i + 1, 0:6].reshape(6)
    columns = jnp.concatenate(
        [
            jnp.concatenate([end_z[0], end_z[1]], axis=1),
            jnp.concatenate([end_n[0, 1, 8:16, 384:768], end_n[1, 1, 8:16, 384:768]], axis=1),
        ],
        axis=0,
    )
    a, b, d = split(columns, 3)
    moved = mm_t(a, spread[...]) + (mm_t(b, spread[...]) + mm_t(d, spread[...]))
    mixer[...] = moved[0:6]
    ff_content[...] = moved[8:29]
    ff_acceptor[...] = moved[32:38]


def finish(end_n, end_z, spread, out, grad):
    shapes = [(TOK, EMB), (TOK, EMB)] + [(6,)] * 14
    shapes += [(6, EMB)] * 5 + [(6, FF), (21, EMB), (6, EMB)]
    return pl.pallas_call(
        finish_kernel,
        out_shape=tuple(jax.ShapeDtypeStruct(shape, F32) for shape in shapes),
        in_specs=[VMEM] * 5,
        out_specs=(VMEM,) * len(shapes),
        name="finish",
    )(end_n, end_z, spread, out, grad)


def per_device(
    incoming_activations,
    sequence_opening_memory,
    prior_standardize_factor,
    prior_standardize_offset,
    acceptor_lerp_factor,
    address_lerp_factor,
    content_lerp_factor,
    sigmoid_lerp_factor,
    acceptor_matrix,
    address_matrix,
    content_matrix,
    sigmoid_matrix,
    lane_fading_exponent,
    present_reward_vector,
    cluster_standardize_factor,
    cluster_standardize_offset,
    mixer_result_matrix,
    latter_standardize_factor,
    latter_standardize_offset,
    feedforward_address_lerp,
    feedforward_sigmoid_lerp,
    feedforward_address_matrix,
    feedforward_content_matrix,
    feedforward_acceptor_matrix,
    upstream_derivative,
):
    spread = jnp.asarray(_spread(), BF)
    out, in_grad, end_n, end_z = layer(
        incoming_activations, upstream_derivative,
        sequence_opening_memory.reshape(12, 64, 64), spread,
        jnp.asarray(_line_pick(), BF), jnp.asarray(_plane_pick(), BF),
        jnp.asarray(_line_pick().T, BF), jnp.asarray(_plane_pick().T, BF),
        prior_standardize_factor, prior_standardize_offset, acceptor_lerp_factor,
        address_lerp_factor, content_lerp_factor, sigmoid_lerp_factor,
        latter_standardize_factor, latter_standardize_offset, feedforward_address_lerp,
        feedforward_sigmoid_lerp, lane_fading_exponent, present_reward_vector,
        cluster_standardize_factor, cluster_standardize_offset,
        acceptor_matrix, address_matrix, content_matrix, sigmoid_matrix,
        mixer_result_matrix, feedforward_address_matrix, feedforward_content_matrix,
        feedforward_acceptor_matrix,
    )
    results = finish(end_n, end_z, spread, out, in_grad)
    out, in_grad, v = results[0], results[1], results[2:16]
    acceptor, address, content, sigmoid, mixer, ff_address, ff_content, ff_acceptor = results[16:]
    return (
        out, in_grad,
        v[0], v[1], v[2], v[3], v[4], v[5],
        acceptor, address, content, sigmoid,
        v[10], v[11], v[12], v[13],
        mixer,
        v[6], v[7], v[8], v[9],
        ff_address, ff_content, ff_acceptor,
    )


def solution(mesh):
    r, v = P(("dp", "fsdp"), None), P(("dp", "fsdp"))
    state = P(("dp", "fsdp"), None, None, None)
    return jax.shard_map(
        per_device,
        mesh=mesh,
        in_specs=(r, state) + (v,) * 6 + (r,) * 4 + (v,) * 4 + (r,) + (v,) * 4 + (r,) * 4,
        out_specs=(r, r) + (v,) * 6 + (r,) * 4 + (v,) * 4 + (r,) + (v,) * 4 + (r,) * 3,
        check_vma=False,
    )
```

time: 157 us -> 142 us (0.904)
  Pallas kernels: 150 us -> 141 us
  local copies, waits for them, and re-layouts: 5.34 us -> 0 us
    pallas_call x1, Pallas kernels: 146 us -> 137 us  [layer(): pl.pallas_call(layer_kernel, out_shape=(jax.ShapeDtypeStruct((TOK, EMB),...]
    slice x1 -> x0, local copies, waits for them, and re-layouts: 2.12 us -> none  [per_device(): v = [vec[:6, i] for i in range(14)]]
where the time goes in v3:
time: 142 us
  Pallas kernels  141 us (99%)
    pallas_call x1, Pallas kernels, layer(): pl.pallas_call(layer_kernel, out_shape=(jax.ShapeDtypeStruct((TOK, EMB),...  137 us
    pallas_call x1, Pallas kernels, finish(): pl.pallas_call(finish_kernel, out_shape=tuple((jax.ShapeDtypeStruct(shape...  3.74 us

profile of v3, /device:TPU:1, one launch (start us, length us, event | category | flops | bytes accessed | tf_op | source)
XLA Modules:
  0.0 141.8 jit_solution(6446393460193769534)
XLA Ops:
  0.7 137.2 %layer.1 = (f32[128,768]{1,0:T(8,128)}, f32[128,768]{1,0:T(8,128)}, f32[2,2,16,896]{3,2,1,0:T(8,128)}, f32[2,32,384]{2,1,0:T(8,128)}) custom-call(bf16[128,768]{1,0:T(8,128)(2,1)} %x_in.1, bf16[128,768]{1,0:T(8,128)(2,1)} %up_in.1, f32[12,64,64]{2,1,0:T(8,128)} %bitcast.1, bf16[768,768]{1,0:T(8,128)(2,1)} %constant.10.clone.spread_in.spread, ...), custom_call_target="tpu_custom_call" | custom-call | flops 5888802816 | bytes 30670848 | tf_op jit(solution)/shard_map/layer/pallas_call | solution.py:853
  137.9 3.7 %finish.1 = (f32[128,768]{1,0:T(8,128)}, f32[128,768]{1,0:T(8,128)}, f32[6]{0:T(128)}, f32[6]{0:T(128)}, f32[6]{0:T(128)}, /*index=5*/f32[6]{0:T(128)}, f32[6]{0...) custom-call(f32[2,2,16,896]{3,2,1,0:T(8,128)} %get-tuple-element.52., ...), custom_call_target="tpu_custom_call" | custom-call | tf_op jit(solution)/shard_map/finish/pallas_call | solution.py:929

commit v4 on v3

--- a/solution.py
+++ b/solution.py
@@ -174,10 +174,10 @@
             device_id_type=MESH,
         ).wait_recv()
 
-    def drain(self):
-        for copy in self.open:
-            copy.wait_send()
-        self.open = []
+    def drain(self, until=None):
+        keep = 0 if until is None else self.sends - until
+        while len(self.open) > keep:
+            self.open.pop(0).wait_send()
 
 
 def rows(start, size, unit=16):
@@ -702,6 +702,7 @@
     sums_z = {}
 
     need("2")
+    gathered = net.sends
     steps_2, steps_o = scatter_steps_w("2"), scatter_steps_w("o")
     steps_b, steps_c = scatter_steps("B"), scatter_steps("C")
     steps_r, steps_k = scatter_steps("R"), scatter_steps("K")
@@ -717,20 +718,20 @@
     swap("B")
     value_out = jnp.concatenate([mm(hidden, w2[0]), mm(hidden, w2[1])], axis=1)
     layer_out = middle + gating * value_out
-    net.drain()
+    run(*steps_b[:8])
+    net.drain(gathered)
     for h in range(2):
         w2[h] = t_mm(hidden, grad_vo_low[:, COLS * h : COLS * h + COLS]).astype(BF)
     swap_w("2")
-    run(*steps_b[:8])
     grad_gp = (grad_vo * value_out * (1.0 - gating)).astype(BF)
     for h in range(2):
         gc[h] = t_mm(mixed_g, grad_gp[:, COLS * h : COLS * h + COLS]).astype(BF)
     swap("C")
-    run(*steps_2[:4])
     grad_mg = mm_t(grad_gp[:, :COLS], wc[0]) + mm_t(grad_gp[:, COLS:], wc[1])
     grad_mh = mm_t(grad_pre[:, :128], wa[0, :, 1536:1664])
     grad_mh += mm_t(grad_pre[:, 128:1408], wb[0]) + mm_t(grad_pre[:, 1408:], wb[1])
     gk[0, :, 768:896] = t_mm(mixed_h, grad_pre[:, :128]).astype(BF)
+    run(*steps_2[:4])
     run(*steps_c[:8])
 
     grad_n2 = grad_mh * lerp_h + grad_mg * lerp_g
@@ -766,10 +767,10 @@
         parts_r.append(fine(NN, beside(da), stack(kg)) + fine(NT, dg, memory[g]))
         parts_k.append(fine(TN, da, stack(rg)))
         parts_v.append(fine(TN, scores[g], ds))
-        if g == 0:
+        if g == 2:
             run(*steps_o[:4])
-        if g == 3:
-            run(*steps_2[4:6], *steps_b[8:12])
+        if g == 4:
+            run(*steps_b[8:12])
     grad_r = jnp.concatenate(parts_r, axis=1) * fall_r
     grad_k = jnp.concatenate(parts_k, axis=1) * fall_k
     grad_v = jnp.concatenate(parts_v, axis=1) + grad_wkv * present
@@ -790,7 +791,7 @@
         mm_t(grad_v, wa[1, :, 0:768]),
         mm_t(grad_gate, wa[1, :, 768:1536]),
     ]
-    run(*steps_c[8:12], *steps_o[4:6], *steps_r[:8])
+    run(*steps_2[4:6], *steps_r[:8])
     delta = normed - previous
     g_lerps = [tsum(g * delta) for g in grad_blended]
     grad_n1 = sum(g * l for g, l in zip(grad_blended, lerps))
@@ -808,23 +809,26 @@
     )
     gk[1, :, 768:896] = table.T.astype(BF)
     swap("K")
-    run(*steps_b[12:16], *steps_k[:8], *steps_2[6:8], *steps_o[6:8])
-    run(*steps_r[8:12], *steps_c[12:16], *steps_k[8:12])
-
+    run(*steps_c[8:12], *steps_b[12:16], *steps_k[:8], *steps_o[4:6], *steps_r[8:12])
+    out_ref[...] = unspread(layer_out)
+    run(steps_2[6], steps_o[6], *steps_k[8:12], steps_b[16], *steps_c[12:16])
+    q1 = grad_n1 * gain1
+    grad_x = grad_middle + scale1 * (q1 - mean(q1) - unit1 * mean(q1 * unit1))
+    in_grad_ref[...] = unspread(grad_x)
+    run(*steps_r[12:16], *steps_k[12:16])
+
+    run(steps_2[7], steps_o[7])
     spread_z = mm(turn_z[:, :96], sums_z["o"]) + mm(turn_z[:, 96:], sums_z["2"])
     piece_z[...] = spread_z.astype(BF).reshape(4, 128, COLS)
     for k in (1, 2, 3):
         net.send(piece_z.at[rem4(at.y + k)], side_z.at[k - 1], at.side(k), "grad side")
-    run(steps_b[16], steps_c[16])
+    run(steps_c[16])
     spread_lines(
         1, acc_b[:, 0:LEFT], jnp.concatenate([acc_b[:, LEFT:], acc_c[...]], axis=1), piece_b, line_b
     )
-    out_ref[...] = unspread(layer_out)
-    run(*steps_r[12:16])
-    q1 = grad_n1 * gain1
-    grad_x = grad_middle + scale1 * (q1 - mean(q1) - unit1 * mean(q1 * unit1))
-    in_grad_ref[...] = unspread(grad_x)
-    run(*steps_k[12:16])
+    run(steps_r[16], steps_k[16])
+    acc_a = jnp.concatenate([acc_r[...], acc_k[...]], axis=1)
+    spread_lines(0, acc_a[:, 0:LEFT], acc_a[:, LEFT:], piece_a, line_a)
     net.wait_group("grad side", side_z, sib)
     total = wide(piece_z.at[at.y])
     for k in (1, 2, 3):
@@ -832,15 +836,12 @@
     half_f[...] = total.reshape(2, 64, COLS)
     sent_z[...] = half_f[1 - at.xhi].astype(BF)
     to_pair = net.send(sent_z, got_z, at.pair())
-    run(steps_r[16], steps_k[16])
-    acc_a = jnp.concatenate([acc_r[...], acc_k[...]], axis=1)
-    spread_lines(0, acc_a[:, 0:LEFT], acc_a[:, LEFT:], piece_a, line_a)
+    sum_lines(1, line_b)
     to_pair.wait_recv()
     swap_f[...] = half_f[at.xhi] + wide(got_z)
     away, kept = rows(32 * (1 - c), 32, 8), rows(32 * c, 32, 8)
     last_swap = net.send(swap_f.at[away], end_z.at[c], sib)
     end_z[c] = swap_f[kept]
-    sum_lines(1, line_b)
     last_swap.wait_recv()
     sum_lines(0, line_a)
     net.drain()

time: 142 us -> 130 us (0.915)
  Pallas kernels: 141 us -> 129 us
    pallas_call x1, Pallas kernels: 137 us -> 125 us  [layer(): pl.pallas_call(layer_kernel, out_shape=(jax.ShapeDtypeStruct((TOK, EMB),...]
where the time goes in v4:
time: 130 us
  Pallas kernels  129 us (99%)
    pallas_call x1, Pallas kernels, layer(): pl.pallas_call(layer_kernel, out_shape=(jax.ShapeDtypeStruct((TOK, EMB),...  125 us
    pallas_call x1, Pallas kernels, finish(): pl.pallas_call(finish_kernel, out_shape=tuple((jax.ShapeDtypeStruct(shape...  3.75 us

profile of v4, /device:TPU:1, one launch (start us, length us, event | category | flops | bytes accessed | tf_op | source)
XLA Modules:
  0.0 129.5 jit_solution(170280928248686591)
XLA Ops:
  0.7 124.9 %layer.1 = (f32[128,768]{1,0:T(8,128)}, f32[128,768]{1,0:T(8,128)}, f32[2,2,16,896]{3,2,1,0:T(8,128)}, f32[2,32,384]{2,1,0:T(8,128)}) custom-call(bf16[128,768]{1,0:T(8,128)(2,1)} %x_in.1, bf16[128,768]{1,0:T(8,128)(2,1)} %up_in.1, f32[12,64,64]{2,1,0:T(8,128)} %bitcast.1, bf16[768,768]{1,0:T(8,128)(2,1)} %constant.10.clone.spread_in.spread, ...), custom_call_target="tpu_custom_call" | custom-call | flops 5888802816 | bytes 30670848 | tf_op jit(solution)/shard_map/layer/pallas_call | solution.py:854
  125.6 3.7 %finish.1 = (f32[128,768]{1,0:T(8,128)}, f32[128,768]{1,0:T(8,128)}, f32[6]{0:T(128)}, f32[6]{0:T(128)}, f32[6]{0:T(128)}, /*index=5*/f32[6]{0:T(128)}, f32[6]{0...) custom-call(f32[2,2,16,896]{3,2,1,0:T(8,128)} %get-tuple-element.52., ...), custom_call_target="tpu_custom_call" | custom-call | tf_op jit(solution)/shard_map/finish/pallas_call | solution.py:930

commit v5 on v4

--- a/solution.py
+++ b/solution.py
@@ -23,6 +23,7 @@
 LEFT, RIGHT = 896, 768
 
 WIDTH = {"A": 1664, "B": 1280, "C": 384, "R": 768, "K": 896}
+FIXED = {"C": 1, "S": 0, "K": 1}
 VEC = 1536
 ORDER = (0, 1, 3, 2)
 
@@ -91,7 +92,9 @@
         return self.device(z, self.y, self.x, core), z * 2 + core, core
 
     def turn(self, q, sibling=False):
-        return 1 if q == "C" else (1 - self.c if sibling else self.c)
+        if q in FIXED:
+            return FIXED[q]
+        return 1 - self.c if sibling else self.c
 
     def first(self, q, k):
         t = self.turn(q)
@@ -228,14 +231,15 @@
     (
         out_ref, in_grad_ref, end_n, end_z,
         x_ref, up_ref, state_v, spread, pick_n, pick_z, turn_n, turn_z, memory,
-        wa, wb, wc, wo, w2, gk, gb, gc, scores,
+        wa, wb, wc, wo, w2, gb, scores,
         vec_f, pack_f, pack_n, stage_a, stage_b, cols_f, pack_z, half_z, pair_z, stage_z,
         sib_r, sib_k, sib_b, sib_c, relay_r, relay_k, relay_b, relay_c,
         last_r, last_k, last_b, last_c, first_r, first_k, first_b, first_c,
         acc_r, acc_k, acc_b, acc_c,
         piece_a, piece_b, line_a, line_b,
         sib_o, sib_2, relay_o, relay_2, up_o, up_2, sent_o, sent_2, twin_o, twin_2,
-        piece_z, side_z, half_f, sent_z, got_z, swap_f,
+        piece_z, side_z, half_f, sent_z, got_z, swap_f, swapped_z,
+        pre_h, hid_h, gp_h, gvo_h, turned, turned_w, turned_h, turned_g,
         send_sems, recv_sems, load_sems,
     ) = refs
     at = Place()
@@ -506,6 +510,8 @@
     normed = unit1 * gain1 + bias1
     previous = shift_down(normed)
     blended = [(normed * l + previous * (1.0 - l)).astype(BF) for l in lerps]
+    for i in range(4):
+        turned[i] = blended[i].astype(F32).T.astype(BF)
     recept = mm(blended[0], wa[0, :, 0:768])
     keys = mm(blended[1], wa[0, :, 768:1536])
     vals = mm(blended[2], wa[1, :, 0:768])
@@ -537,6 +543,7 @@
     sig = 1.0 / (1.0 + jnp.exp(-gate_pre))
     silu = gate_pre * sig
     gated = (grouped * silu).astype(BF)
+    turned_w[...] = gated.astype(F32).T.astype(BF)
     need("o")
     middle = tokens + jnp.concatenate([mm(gated, wo[0]), mm(gated, wo[1])], axis=1)
 
@@ -547,17 +554,23 @@
     previous2 = shift_down(normed2)
     mixed_h = (normed2 * lerp_h + previous2 * (1.0 - lerp_h)).astype(BF)
     mixed_g = (normed2 * lerp_g + previous2 * (1.0 - lerp_g)).astype(BF)
+    turned_h[...] = mixed_h.astype(F32).T.astype(BF)
+    turned_g[...] = mixed_g.astype(F32).T.astype(BF)
     need("B")
+    halves = (1 - c, c)
+    pre_s = jnp.maximum(mm(mixed_h, wa[0, :, 1536:1664]), 0.0)
+    hidden_s = (pre_s * pre_s).astype(BF)
+    for h in halves:
+        pre = jnp.maximum(mm(mixed_h, wb[h]), 0.0)
+        pre_h[h] = pre
+        hid_h[h] = (pre * pre).astype(BF)
     need("C")
-    pre = jnp.concatenate(
-        [mm(mixed_h, wa[0, :, 1536:1664]), mm(mixed_h, wb[0]), mm(mixed_h, wb[1])], axis=1
-    )
-    pre = jnp.maximum(pre, 0.0)
-    hidden = (pre * pre).astype(BF)
     gating = jnp.concatenate([mm(mixed_g, wc[0]), mm(mixed_g, wc[1])], axis=1)
     gating = 1.0 / (1.0 + jnp.exp(-gating))
     grad_vo = upstream * gating
-    grad_vo_low = grad_vo.astype(BF)
+    for h in range(2):
+        gvo_h[h] = grad_vo[:, COLS * h : COLS * h + COLS].astype(BF)
+
     swaps = {}
 
     def fold(mine, other, *more):
@@ -567,12 +580,13 @@
         return total
 
     gr, go = wb.at[:, :, 0:768], wb.at[:, :, 768:1152]
-    grads = {"R": gr, "K": gk, "B": gb, "C": gc}
-    sib_of = {"R": sib_r, "K": sib_k, "B": sib_b, "C": sib_c}
-    relay_of = {"R": relay_r, "K": relay_k, "B": relay_b, "C": relay_c}
-    last_of = {"R": last_r, "K": last_k, "B": last_b, "C": last_c}
-    first_of = {"R": first_r, "K": first_k, "B": first_b, "C": first_c}
-    acc_of = {"R": acc_r, "K": acc_k, "B": acc_b, "C": acc_c}
+    gk, gc = wa.at[:, :, 768:1664], wc
+    grads = {"R": gr, "K": gk, "B": gb, "S": gc}
+    sib_of = {"R": sib_r, "K": sib_k, "B": sib_b, "S": sib_c}
+    relay_of = {"R": relay_r, "K": relay_k, "B": relay_b, "S": relay_c}
+    last_of = {"R": last_r, "K": last_k, "B": last_b, "S": last_c}
+    first_of = {"R": first_r, "K": first_k, "B": first_b, "S": first_c}
+    acc_of = {"R": acc_r, "K": acc_k, "B": acc_b, "S": acc_c}
 
     def swap(q):
         swaps[q] = net.send(grads[q].at[1 - c], sib_of[q], sib)
@@ -704,33 +718,46 @@
     need("2")
     gathered = net.sends
     steps_2, steps_o = scatter_steps_w("2"), scatter_steps_w("o")
-    steps_b, steps_c = scatter_steps("B"), scatter_steps("C")
+    steps_b, steps_c = scatter_steps("B"), scatter_steps("S")
     steps_r, steps_k = scatter_steps("R"), scatter_steps("K")
 
     def run(*steps_):
         for step in steps_:
             step()
 
-    grad_hidden = mm_t(grad_vo_low[:, :COLS], w2[0]) + mm_t(grad_vo_low[:, COLS:], w2[1])
-    grad_pre = (grad_hidden * 2.0 * pre).astype(BF)
-    gb[0] = t_mm(mixed_h, grad_pre[:, 128:1408]).astype(BF)
-    gb[1] = t_mm(mixed_h, grad_pre[:, 1408:]).astype(BF)
-    swap("B")
-    value_out = jnp.concatenate([mm(hidden, w2[0]), mm(hidden, w2[1])], axis=1)
+    for h in halves:
+        part = rows(128 + 1280 * h, 1280)
+        grad_hidden = mm_t(gvo_h[0], w2[0, part]) + mm_t(gvo_h[1], w2[1, part])
+        gp_h[h] = (grad_hidden * 2.0 * pre_h[h]).astype(BF)
+        gb[h] = mm(turned_h[...], gp_h[h]).astype(BF)
+        if h is halves[0]:
+            swap("B")
+    grad_hidden = mm_t(gvo_h[0], w2[0, 0:128]) + mm_t(gvo_h[1], w2[1, 0:128])
+    grad_pre_s = (grad_hidden * 2.0 * pre_s).astype(BF)
+    value_out = jnp.concatenate(
+        [
+            mm(hidden_s, w2[n, 0:128]) + mm(hid_h[0], w2[n, 128:1408]) + mm(hid_h[1], w2[n, 1408:2688])
+            for n in range(2)
+        ],
+        axis=1,
+    )
     layer_out = middle + gating * value_out
     run(*steps_b[:8])
     net.drain(gathered)
+    for n in halves:
+        w2[n, 0:128] = t_mm(hidden_s, gvo_h[n]).astype(BF)
+        w2[n, 128:1408] = t_mm(hid_h[0], gvo_h[n]).astype(BF)
+        w2[n, 1408:2688] = t_mm(hid_h[1], gvo_h[n]).astype(BF)
+        if n is halves[0]:
+            swap_w("2")
+    grad_gp = (grad_vo * value_out * (1.0 - gating)).astype(BF)
+    grad_mg = mm_t(grad_gp[:, :COLS], wc[0]) + mm_t(grad_gp[:, COLS:], wc[1])
     for h in range(2):
-        w2[h] = t_mm(hidden, grad_vo_low[:, COLS * h : COLS * h + COLS]).astype(BF)
-    swap_w("2")
-    grad_gp = (grad_vo * value_out * (1.0 - gating)).astype(BF)
-    for h in range(2):
-        gc[h] = t_mm(mixed_g, grad_gp[:, COLS * h : COLS * h + COLS]).astype(BF)
-    swap("C")
-    grad_mg = mm_t(grad_gp[:, :COLS], wc[0]) + mm_t(grad_gp[:, COLS:], wc[1])
-    grad_mh = mm_t(grad_pre[:, :128], wa[0, :, 1536:1664])
-    grad_mh += mm_t(grad_pre[:, 128:1408], wb[0]) + mm_t(grad_pre[:, 1408:], wb[1])
-    gk[0, :, 768:896] = t_mm(mixed_h, grad_pre[:, :128]).astype(BF)
+        gc[h] = mm(turned_g[...], grad_gp[:, COLS * h : COLS * h + COLS]).astype(BF)
+    swap("S")
+    grad_mh = mm_t(grad_pre_s, wa[0, :, 1536:1664])
+    grad_mh += mm_t(gp_h[0], wb[0]) + mm_t(gp_h[1], wb[1])
+    gk[0, :, 768:896] = mm(turned_h[...], grad_pre_s).astype(BF)
     run(*steps_2[:4])
     run(*steps_c[:8])
 
@@ -745,7 +772,7 @@
     grad_attn = grad_middle.astype(BF)
     grad_gated = mm_t(grad_attn[:, :COLS], wo[0]) + mm_t(grad_attn[:, COLS:], wo[1])
     for h in range(2):
-        go[h] = t_mm(gated, grad_attn[:, COLS * h : COLS * h + COLS]).astype(BF)
+        go[h] = mm(turned_w[...], grad_attn[:, COLS * h : COLS * h + COLS]).astype(BF)
     swap_w("o")
     grad_gate = (grad_gated * grouped * (sig * (1.0 + gate_pre * (1.0 - sig)))).astype(BF)
     grad_grouped = grad_gated * silu
@@ -780,17 +807,17 @@
     grad_k = (grad_k + bonus * recept * weight).astype(BF)
     grad_v = grad_v.astype(BF)
 
-    gr[0] = t_mm(blended[0], grad_r).astype(BF)
-    gr[1] = t_mm(blended[2], grad_v).astype(BF)
+    gr[0] = mm(turned[0], grad_r).astype(BF)
+    gr[1] = mm(turned[2], grad_v).astype(BF)
     swap("R")
-    gk[0, :, 0:768] = t_mm(blended[1], grad_k).astype(BF)
-    gk[1, :, 0:768] = t_mm(blended[3], grad_gate).astype(BF)
     grad_blended = [
         mm_t(grad_r, wa[0, :, 0:768]),
         mm_t(grad_k, wa[0, :, 768:1536]),
         mm_t(grad_v, wa[1, :, 0:768]),
         mm_t(grad_gate, wa[1, :, 768:1536]),
     ]
+    gk[0, :, 0:768] = mm(turned[1], grad_k).astype(BF)
+    gk[1, :, 0:768] = mm(turned[3], grad_gate).astype(BF)
     run(*steps_2[4:6], *steps_r[:8])
     delta = normed - previous
     g_lerps = [tsum(g * delta) for g in grad_blended]
@@ -810,12 +837,17 @@
     gk[1, :, 768:896] = table.T.astype(BF)
     swap("K")
     run(*steps_c[8:12], *steps_b[12:16], *steps_k[:8], *steps_o[4:6], *steps_r[8:12])
-    out_ref[...] = unspread(layer_out)
-    run(steps_2[6], steps_o[6], *steps_k[8:12], steps_b[16], *steps_c[12:16])
+    out_v, grad_v_ = pre_h.at[0, :, 0:768], pre_h.at[1, :, 0:768]
+    out_v[...] = unspread(layer_out)
+    out_copy = pltpu.make_async_copy(out_v, out_ref, load_sems.at[8])
+    out_copy.start()
+    run(*steps_k[8:12], steps_2[6], steps_o[6], steps_b[16], *steps_c[12:16])
     q1 = grad_n1 * gain1
     grad_x = grad_middle + scale1 * (q1 - mean(q1) - unit1 * mean(q1 * unit1))
-    in_grad_ref[...] = unspread(grad_x)
-    run(*steps_r[12:16], *steps_k[12:16])
+    grad_v_[...] = unspread(grad_x)
+    grad_copy = pltpu.make_async_copy(grad_v_, in_grad_ref, load_sems.at[9])
+    grad_copy.start()
+    run(*steps_r[12:16])
 
     run(steps_2[7], steps_o[7])
     spread_z = mm(turn_z[:, :96], sums_z["o"]) + mm(turn_z[:, 96:], sums_z["2"])
@@ -826,9 +858,7 @@
     spread_lines(
         1, acc_b[:, 0:LEFT], jnp.concatenate([acc_b[:, LEFT:], acc_c[...]], axis=1), piece_b, line_b
     )
-    run(steps_r[16], steps_k[16])
-    acc_a = jnp.concatenate([acc_r[...], acc_k[...]], axis=1)
-    spread_lines(0, acc_a[:, 0:LEFT], acc_a[:, LEFT:], piece_a, line_a)
+    run(*steps_k[12:16])
     net.wait_group("grad side", side_z, sib)
     total = wide(piece_z.at[at.y])
     for k in (1, 2, 3):
@@ -836,13 +866,26 @@
     half_f[...] = total.reshape(2, 64, COLS)
     sent_z[...] = half_f[1 - at.xhi].astype(BF)
     to_pair = net.send(sent_z, got_z, at.pair())
+    run(steps_r[16], steps_k[16])
+    acc_a = jnp.concatenate([acc_r[...], acc_k[...]], axis=1)
+    spread_lines(0, acc_a[:, 0:LEFT], acc_a[:, LEFT:], piece_a, line_a)
     sum_lines(1, line_b)
     to_pair.wait_recv()
     swap_f[...] = half_f[at.xhi] + wide(got_z)
     away, kept = rows(32 * (1 - c), 32, 8), rows(32 * c, 32, 8)
-    last_swap = net.send(swap_f.at[away], end_z.at[c], sib)
-    end_z[c] = swap_f[kept]
+    last_swap = net.send(swap_f.at[away], swapped_z.at[c], sib)
+    swapped_z[c] = swap_f[kept]
     last_swap.wait_recv()
+    columns = jnp.concatenate(
+        [
+            jnp.concatenate([swapped_z[0], swapped_z[1]], axis=1),
+            jnp.concatenate([end_n[0, 1, 8:16, 384:768], end_n[1, 1, 8:16, 384:768]], axis=1),
+        ],
+        axis=0,
+    )
+    end_z[...] = unspread(columns)
+    out_copy.wait()
+    grad_copy.wait()
     sum_lines(0, line_a)
     net.drain()
 
@@ -857,15 +900,15 @@
             jax.ShapeDtypeStruct((TOK, EMB), F32),
             jax.ShapeDtypeStruct((TOK, EMB), F32),
             jax.ShapeDtypeStruct((2, 2, 16, LEFT), F32),
-            jax.ShapeDtypeStruct((2, 32, COLS), F32),
+            jax.ShapeDtypeStruct((40, EMB), F32),
         ),
         in_specs=[pl.BlockSpec(memory_space=pl.ANY)] * 8 + [VMEM] * (len(operands) - 8),
-        out_specs=(VMEM,) * 4,
+        out_specs=(pl.BlockSpec(memory_space=pl.ANY),) * 2 + (VMEM,) * 2,
         scratch_shapes=[
             bf(TOK, EMB), bf(TOK, EMB), f32(12, 64, 64), bf(EMB, EMB),
             bf(96, 128), bf(432, 512), bf(128, 96), bf(512, 432), f32(6, 128, 128),
             bf(2, EMB, a), bf(2, EMB, b), bf(2, EMB, d), bf(2, EMB, COLS), bf(2, FF, COLS),
-            bf(2, EMB, k), bf(2, EMB, b), bf(2, EMB, d), f32(6, 256, 128),
+            bf(2, EMB, b), f32(6, 256, 128),
             f32(128, 128), f32(2, 2, 16, LEFT), bf(2, 2, 16, LEFT), bf(8, 16, LEFT), bf(8, 16, LEFT),
             f32(48, EMB), bf(2, 32, COLS), bf(2, 32, COLS), bf(2, 2, 32, COLS), bf(4, 2, 2, 32, COLS),
             *(bf(EMB, w) for w in (r, k, b, d)), *(bf(4, 48, w) for w in (r, k, b, d)),
@@ -876,10 +919,12 @@
             bf(2, 96, COLS), bf(2, 336, COLS), bf(2, 2, 96, COLS), bf(2, 2, 336, COLS),
             bf(96, COLS), bf(336, COLS), bf(96, COLS), bf(336, COLS),
             bf(4, 128, COLS), bf(3, 128, COLS), f32(2, 64, COLS), bf(64, COLS), bf(64, COLS),
-            f32(64, COLS),
+            f32(64, COLS), f32(2, 32, COLS),
+            f32(2, TOK, b), bf(2, TOK, b), bf(2, TOK, b), bf(2, TOK, COLS),
+            bf(4, EMB, TOK), bf(EMB, TOK), bf(EMB, TOK), bf(EMB, TOK),
             pltpu.SemaphoreType.DMA((SENDS,)),
             pltpu.SemaphoreType.DMA((ARRIVALS,)),
-            pltpu.SemaphoreType.DMA((8,)),
+            pltpu.SemaphoreType.DMA((10,)),
         ],
         compiler_params=pltpu.CompilerParams(
             collective_id=1, has_side_effects=True, vmem_limit_bytes=62 << 20
@@ -891,7 +936,7 @@
     )(*operands)
 
 
-def finish_kernel(end_n, end_z, spread, out_in, grad_in, out, grad, *refs):
+def finish_kernel(end_n, end_z, out_in, grad_in, out, grad, *refs):
     vecs, mats = refs[:14], refs[14:]
     acceptor, address, content, sigmoid, mixer, ff_address, ff_content, ff_acceptor = mats
     out[...] = out_in[...]
@@ -910,30 +955,21 @@
     table = jnp.concatenate([end_n[1, 0, 8:16, 640:768], jnp.zeros((120, 128), F32)], axis=0).T
     for i, ref in enumerate(vecs):
         ref[...] = table[i : i + 1, 0:6].reshape(6)
-    columns = jnp.concatenate(
-        [
-            jnp.concatenate([end_z[0], end_z[1]], axis=1),
-            jnp.concatenate([end_n[0, 1, 8:16, 384:768], end_n[1, 1, 8:16, 384:768]], axis=1),
-        ],
-        axis=0,
-    )
-    a, b, d = split(columns, 3)
-    moved = mm_t(a, spread[...]) + (mm_t(b, spread[...]) + mm_t(d, spread[...]))
-    mixer[...] = moved[0:6]
-    ff_content[...] = moved[8:29]
-    ff_acceptor[...] = moved[32:38]
-
-
-def finish(end_n, end_z, spread, out, grad):
+    mixer[...] = end_z[0:6]
+    ff_content[...] = end_z[8:29]
+    ff_acceptor[...] = end_z[32:38]
+
+
+def finish(end_n, end_z, out, grad):
     shapes = [(TOK, EMB), (TOK, EMB)] + [(6,)] * 14
     shapes += [(6, EMB)] * 5 + [(6, FF), (21, EMB), (6, EMB)]
     return pl.pallas_call(
         finish_kernel,
         out_shape=tuple(jax.ShapeDtypeStruct(shape, F32) for shape in shapes),
-        in_specs=[VMEM] * 5,
+        in_specs=[VMEM] * 4,
         out_specs=(VMEM,) * len(shapes),
         name="finish",
-    )(end_n, end_z, spread, out, grad)
+    )(end_n, end_z, out, grad)
 
 
 def per_device(
@@ -978,7 +1014,7 @@
         mixer_result_matrix, feedforward_address_matrix, feedforward_content_matrix,
         feedforward_acceptor_matrix,
     )
-    results = finish(end_n, end_z, spread, out, in_grad)
+    results = finish(end_n, end_z, out, in_grad)
     out, in_grad, v = results[0], results[1], results[2:16]
     acceptor, address, content, sigmoid, mixer, ff_address, ff_content, ff_acceptor = results[16:]
     return (

time: 130 us -> 126 us (0.969)
  Pallas kernels: 129 us -> 124 us
    pallas_call x1, Pallas kernels: 125 us -> 122 us  [layer(): pl.pallas_call(layer_kernel, out_shape=(jax.ShapeDtypeStruct((TOK, EMB),...]
    pallas_call x1, Pallas kernels: 3.75 us -> 2.36 us  [finish(): pl.pallas_call(finish_kernel, out_shape=tuple((jax.ShapeDtypeStruct(shape...]
where the time goes in v5:
time: 126 us; the launch traced here: 125 us
  Pallas kernels  124 us (98%)
    pallas_call x1, Pallas kernels, layer(): pl.pallas_call(layer_kernel, out_shape=(jax.ShapeDtypeStruct((TOK, EMB),...  122 us

profile of v5, /device:TPU:1, one launch (start us, length us, event | category | flops | bytes accessed | tf_op | source)
XLA Modules:
  0.0 125.0 jit_solution(11644075898971831909)
XLA Ops:
  0.7 121.8 %layer.1 = (f32[128,768]{1,0:T(8,128)}, f32[128,768]{1,0:T(8,128)}, f32[2,2,16,896]{3,2,1,0:T(8,128)}, f32[40,768]{1,0:T(8,128)}) custom-call(bf16[128,768]{1,0:T(8,128)(2,1)} %x_in.1, bf16[128,768]{1,0:T(8,128)(2,1)} %up_in.1, f32[12,64,64]{2,1,0:T(8,128)} %bitcast.1, bf16[768,768]{1,0:T(8,128)(2,1)} %constant.10.clone.spread_in, ...), custom_call_target="tpu_custom_call" | custom-call | flops 5888802816 | bytes 30670848 | tf_op jit(solution)/shard_map/layer/pallas_call | solution.py:897
  122.4 2.4 %finish.1 = (f32[128,768]{1,0:T(8,128)}, f32[128,768]{1,0:T(8,128)}, f32[6]{0:T(128)}, f32[6]{0:T(128)}, f32[6]{0:T(128)}, /*index=5*/f32[6]{0:T(128)}, f32[6]{0...) custom-call(f32[2,2,16,896]{3,2,1,0:T(8,128)} %get-tuple-element.52., ...), custom_call_target="tpu_custom_call" | custom-call | tf_op jit(solution)/shard_map/finish/pallas_call | solution.py:966

commit v6 on v5

--- a/solution.py
+++ b/solution.py
@@ -23,7 +23,7 @@
 LEFT, RIGHT = 896, 768
 
 WIDTH = {"A": 1664, "B": 1280, "C": 384, "R": 768, "K": 896}
-FIXED = {"C": 1, "S": 0, "K": 1}
+FIXED = {"S": 0}
 VEC = 1536
 ORDER = (0, 1, 3, 2)
 
@@ -58,10 +58,12 @@
 def _plane_pick():
     pick = np.zeros((432, 512), np.float32)
     for member in range(16):
+        y, xhi, core = member // 4, member // 2 % 2, member % 2
+        staged = (xhi * 8 + y * 2 + core) * 32
         for r in range(6):
-            pick[member * 6 + r, member * 32 + r] = 1.0
+            pick[member * 6 + r, staged + r] = 1.0
         for r in range(21):
-            pick[96 + member * 21 + r, member * 32 + 8 + r] = 1.0
+            pick[96 + member * 21 + r, staged + 8 + r] = 1.0
     return pick
 
 
@@ -76,6 +78,10 @@
         self.y, self.xhi = lax.div(fs, 4), lax.rem(lax.div(fs, 2), 2)
         self.c = lax.rem(fs, 2)
         self.x = self.xhi * 2 + self.xlo
+        self.one, self.two = self.by_core(self.y, self.x), self.by_core(self.x, self.y)
+
+    def by_core(self, zero, one):
+        return zero * (1 - self.c) + one * self.c
 
     def device(self, z, y, x, c):
         return (z * 2 + lax.rem(x, 2), y * 4 + lax.div(x, 2) * 2 + c)
@@ -118,14 +124,8 @@
     def side(self, k):
         return self.device(self.z, rem4(self.y + k), self.x, self.c)
 
-    def twin(self):
-        return self.device(self.z, self.y, self.xhi * 2 + 1 - self.xlo, self.c)
-
-    def pair(self):
-        return self.across(2)
-
     def order(self, m, k):
-        return rem4(self.z + k) * 2 + (self.xlo if m == 0 else 1 - self.xlo)
+        return rem4(self.z + k) * 2 + m
 
     def greet(self):
         mates = [self.line(k)[0] for k in range(1, 8)]
@@ -232,13 +232,13 @@
         out_ref, in_grad_ref, end_n, end_z,
         x_ref, up_ref, state_v, spread, pick_n, pick_z, turn_n, turn_z, memory,
         wa, wb, wc, wo, w2, gb, scores,
-        vec_f, pack_f, pack_n, stage_a, stage_b, cols_f, pack_z, half_z, pair_z, stage_z,
+        vec_f, pack_f, pack_n, stage_a, stage_b, cols_f, pack_z, half_z, row_z, stage_z,
         sib_r, sib_k, sib_b, sib_c, relay_r, relay_k, relay_b, relay_c,
         last_r, last_k, last_b, last_c, first_r, first_k, first_b, first_c,
         acc_r, acc_k, acc_b, acc_c,
         piece_a, piece_b, line_a, line_b,
-        sib_o, sib_2, relay_o, relay_2, up_o, up_2, sent_o, sent_2, twin_o, twin_2,
-        piece_z, side_z, half_f, sent_z, got_z, swap_f, swapped_z,
+        sib_o, sib_2, relay_o, relay_2, up_o, up_2, sum_z,
+        piece_z, across_z, row_f, row_b, side_z, swap_f, swapped_z,
         pre_h, hid_h, gp_h, gvo_h, turned, turned_w, turned_h, turned_g,
         send_sems, recv_sems, load_sems,
     ) = refs
@@ -311,8 +311,9 @@
     loads["up"].wait()
     upstream = mm(up_ref[...], spread[...])
     swap_z.wait_recv()
-    to_pair = net.send(half_z, pair_z.at[at.xhi], at.pair())
-    pair_z[at.xhi] = half_z[...]
+    for k in (1, 2, 3):
+        net.send(half_z, row_z.at[at.one], at.first("B", k), "one")
+    row_z[at.one] = half_z[...]
     loads["pick_n"].wait()
     for name in ("state", "turn_n", "turn_z", "pick_z"):
         loads[name].wait()
@@ -371,10 +372,6 @@
             lasts[w, m, k] = net.send(spot, spot, at.up(k))
         net.send(spot, spot, sib, ("sib", w))
 
-    def relay_z(w):
-        firsts[w].wait_recv()
-        pass_z(w, 1)
-
     def arrive_z(w, m, k):
         lasts[w, m, k].wait_recv()
         spot = place_z(w, m, 4 - k)
@@ -389,10 +386,10 @@
 
     picked = pick(0, stage_a)
     begin("A", picked[0:48], picked[48:96, 0:RIGHT])
-    to_pair.wait_recv()
-    for k in (1, 2, 3):
-        net.send(pair_z, stage_z.at[at.y], at.side(k), "side")
-    stage_z[at.y] = pair_z[...]
+    net.wait_group("one", row_z.at[0:3], sib)
+    for k in (1, 3, 2):
+        net.send(row_z, stage_z.at[at.two], at.last("B", k), "two")
+    stage_z[at.two] = row_z[...]
     relay("A", 1)
     relay("A", 3)
     for k in (1, 3):
@@ -401,14 +398,17 @@
     relay("A", 2)
     begin("B", picked[0:48], picked[48:96, 0:384])
     begin("C", picked[48:96, 384:768])
-    net.wait_group("side", stage_z.at[0:3], sib)
-    picked_z = mm(pick_z[...], stage_z[...].reshape(512, COLS)).astype(BF)
-    place_z("o", 0, 0)[...] = picked_z[:96]
-    place_z("2", 0, 0)[...] = picked_z[96:]
-    for w in ("o", "2"):
-        spot = place_z(w, 0, 0)
-        firsts[w] = net.send(spot, spot, at.twin())
-        pass_z(w, 0)
+    net.wait_group("two", stage_z.at[0:3], sib)
+    for m in range(2):
+        staged = []
+        for x in (m, 2 + m):
+            block = jnp.where(c == 0, stage_z[x].astype(F32), stage_z[:, x].astype(F32))
+            staged.append(block.reshape(256, COLS).astype(BF))
+        picked_z = mm(pick_z[...], jnp.concatenate(staged, axis=0)).astype(BF)
+        place_z("o", m, 0)[...] = picked_z[:96]
+        place_z("2", m, 0)[...] = picked_z[96:]
+        pass_z("o", m)
+        pass_z("2", m)
     for m in (1, 3):
         for k in (1, 3):
             arrive("A", m, k)
@@ -417,37 +417,44 @@
     relay("B", 3)
     for k in (1, 3):
         arrive("A", 2, k)
-    for w in ("o", "2"):
-        relay_z(w)
     relay("B", 2)
     for m in (1, 3, 2):
         relay("C", m)
-    for m in (1, 3, 2):
-        arrive_far("A", m)
+    for k in (1, 3):
+        arrive("B", 0, k)
+    for w in ("o", "2"):
+        for k in (1, 3):
+            arrive_z(w, 0, k)
+    arrive_far("A", 1)
+    for k in (1, 3):
+        arrive_z("o", 1, k)
+    arrive_far("A", 3)
+    for k in (1, 3):
+        arrive("B", 1, k)
+    arrive_far("A", 2)
+    for k in (1, 3):
+        arrive("B", 3, k)
+
     tasks = []
 
     def plan(kind, *steps_):
         for step in steps_:
             tasks.append((kind, step))
 
-    for m in (0, 1):
-        for k in (1, 3):
-            plan("B", partial(arrive, "B", m, k))
-            plan("o", partial(arrive_z, "o", m, k))
-            plan("2", partial(arrive_z, "2", m, k))
-    for m in (0, 1):
-        plan("o", partial(arrive_z_far, "o", m))
-    for m in (3, 2):
-        for k in (1, 3):
-            plan("B", partial(arrive, "B", m, k))
+    for k in (1, 3):
+        plan("B", partial(arrive, "B", 2, k))
+    for k in (1, 3):
+        plan("2", partial(arrive_z, "2", 1, k))
     for m in ORDER:
         for k in (1, 3):
             plan("C", partial(arrive, "C", m, k))
     for m in (0, 1):
-        plan("2", partial(arrive_z_far, "2", m))
+        plan("o", partial(arrive_z_far, "o", m))
     for q in ("B", "C"):
         for m in ORDER:
             plan(q, partial(arrive_far, q, m))
+    for m in (0, 1):
+        plan("2", partial(arrive_z_far, "2", m))
 
     def work(count=1000):
         for _ in range(min(count, len(tasks))):
@@ -507,6 +514,7 @@
     def beside(value):
         return jnp.concatenate([value[:TOK], value[TOK:]], axis=1)
 
+    work(2)
     normed = unit1 * gain1 + bias1
     previous = shift_down(normed)
     blended = [(normed * l + previous * (1.0 - l)).astype(BF) for l in lerps]
@@ -516,7 +524,7 @@
     keys = mm(blended[1], wa[0, :, 768:1536])
     vals = mm(blended[2], wa[1, :, 0:768])
     gate_pre = mm(blended[3], wa[1, :, 768:1536])
-    work(6)
+    work(12)
 
     fade = -jnp.exp(rate)
     steps = token.astype(F32)
@@ -532,7 +540,7 @@
         sc = jnp.where(below, fine(NT, stack(rg), kg), 0.0)
         scores[g] = sc
         parts.append(fine(NN, beside(sc), stack(vg)) + fine(NN, rg, memory[g]))
-        if g % 2 == 1:
+        if g in (3, 5):
             work(4)
     wkv = jnp.concatenate(parts, axis=1) + present * vals
 
@@ -546,6 +554,8 @@
     turned_w[...] = gated.astype(F32).T.astype(BF)
     need("o")
     middle = tokens + jnp.concatenate([mm(gated, wo[0]), mm(gated, wo[1])], axis=1)
+
+    work()
 
     centred = middle - mean(middle)
     scale2 = lax.rsqrt(mean(centred * centred) + NORM_EPS)
@@ -662,8 +672,8 @@
         return steps_
 
     z_parts = {
-        "o": (96, go, sib_o, relay_o, up_o, sent_o, twin_o),
-        "2": (336, w2, sib_2, relay_2, up_2, sent_2, twin_2),
+        "o": (96, go, sib_o, relay_o, up_o, sum_z.at[:, 0:96]),
+        "2": (336, w2, sib_2, relay_2, up_2, sum_z.at[:, 96:432]),
     }
 
     def swap_w(w):
@@ -694,26 +704,19 @@
         lasts["g", w, m, k] = net.send(spot, arrived.at[k // 2, m], at.up(k))
 
     def scatter_own_w(w, m):
-        unit, mine, theirs, relayed, arrived, sent, twin = z_parts[w]
+        unit, mine, theirs, relayed, arrived, sums = z_parts[w]
         part = part_w(w, m, 0)
         lasts["g", w, m, 1].wait_recv()
         lasts["g", w, m, 3].wait_recv()
         total = fold(mine.at[c, part], theirs.at[part], arrived.at[0, m], arrived.at[1, m])
-        if m == 1:
-            sent[...] = total.astype(BF)
-            firsts["g", w] = net.send(sent, twin, at.twin())
-        else:
-            firsts["g", w].wait_recv()
-            sums_z[w] = (total + wide(twin)).astype(BF)
+        sums[m] = total.astype(BF)
 
     def scatter_steps_w(w):
         steps_ = [partial(scatter_far_w, w, 0), partial(scatter_far_w, w, 1)]
         steps_ += [partial(scatter_near_w, w, 1, 1), partial(scatter_near_w, w, 0, 3)]
         steps_ += [partial(scatter_near_w, w, 0, 1), partial(scatter_near_w, w, 1, 3)]
-        steps_ += [partial(scatter_own_w, w, 1), partial(scatter_own_w, w, 0)]
+        steps_ += [partial(scatter_own_w, w, 0), partial(scatter_own_w, w, 1)]
         return steps_
-
-    sums_z = {}
 
     need("2")
     gathered = net.sends
@@ -729,9 +732,6 @@
         part = rows(128 + 1280 * h, 1280)
         grad_hidden = mm_t(gvo_h[0], w2[0, part]) + mm_t(gvo_h[1], w2[1, part])
         gp_h[h] = (grad_hidden * 2.0 * pre_h[h]).astype(BF)
-        gb[h] = mm(turned_h[...], gp_h[h]).astype(BF)
-        if h is halves[0]:
-            swap("B")
     grad_hidden = mm_t(gvo_h[0], w2[0, 0:128]) + mm_t(gvo_h[1], w2[1, 0:128])
     grad_pre_s = (grad_hidden * 2.0 * pre_s).astype(BF)
     value_out = jnp.concatenate(
@@ -742,7 +742,6 @@
         axis=1,
     )
     layer_out = middle + gating * value_out
-    run(*steps_b[:8])
     net.drain(gathered)
     for n in halves:
         w2[n, 0:128] = t_mm(hidden_s, gvo_h[n]).astype(BF)
@@ -750,15 +749,20 @@
         w2[n, 1408:2688] = t_mm(hid_h[1], gvo_h[n]).astype(BF)
         if n is halves[0]:
             swap_w("2")
+    for h in halves:
+        gb[h] = mm(turned_h[...], gp_h[h]).astype(BF)
+        if h is halves[0]:
+            swap("B")
+    run(*steps_2[:4])
     grad_gp = (grad_vo * value_out * (1.0 - gating)).astype(BF)
     grad_mg = mm_t(grad_gp[:, :COLS], wc[0]) + mm_t(grad_gp[:, COLS:], wc[1])
     for h in range(2):
         gc[h] = mm(turned_g[...], grad_gp[:, COLS * h : COLS * h + COLS]).astype(BF)
     swap("S")
+    run(*steps_b[:8])
     grad_mh = mm_t(grad_pre_s, wa[0, :, 1536:1664])
     grad_mh += mm_t(gp_h[0], wb[0]) + mm_t(gp_h[1], wb[1])
     gk[0, :, 768:896] = mm(turned_h[...], grad_pre_s).astype(BF)
-    run(*steps_2[:4])
     run(*steps_c[:8])
 
     grad_n2 = grad_mh * lerp_h + grad_mg * lerp_g
@@ -841,37 +845,48 @@
     out_v[...] = unspread(layer_out)
     out_copy = pltpu.make_async_copy(out_v, out_ref, load_sems.at[8])
     out_copy.start()
-    run(*steps_k[8:12], steps_2[6], steps_o[6], steps_b[16], *steps_c[12:16])
+    run(*steps_c[12:16], *steps_k[8:12], *steps_2[6:8])
+
+    def spread_z(m):
+        table = mm(turn_z[...], sum_z[m])
+        for xhi in range(2):
+            for y in range(4):
+                x = xhi * 2 + m
+                at_ = (xhi * 4 + y) * 64
+                piece_z[at.by_core(x, y), at.by_core(y, x)] = table[at_ : at_ + 64].astype(BF)
+
+    run(*steps_o[6:8])
+    spread_z(0)
+    spread_z(1)
+    for k in (1, 3, 2):
+        net.send(piece_z.at[rem4(at.two + k)], across_z.at[k - 1], at.last("B", k), "grad two")
+    run(steps_b[16])
     q1 = grad_n1 * gain1
     grad_x = grad_middle + scale1 * (q1 - mean(q1) - unit1 * mean(q1 * unit1))
     grad_v_[...] = unspread(grad_x)
     grad_copy = pltpu.make_async_copy(grad_v_, in_grad_ref, load_sems.at[9])
     grad_copy.start()
-    run(*steps_r[12:16])
-
-    run(steps_2[7], steps_o[7])
-    spread_z = mm(turn_z[:, :96], sums_z["o"]) + mm(turn_z[:, 96:], sums_z["2"])
-    piece_z[...] = spread_z.astype(BF).reshape(4, 128, COLS)
-    for k in (1, 2, 3):
-        net.send(piece_z.at[rem4(at.y + k)], side_z.at[k - 1], at.side(k), "grad side")
-    run(steps_c[16])
+    run(*steps_r[12:16], *steps_k[12:16], steps_c[16])
     spread_lines(
         1, acc_b[:, 0:LEFT], jnp.concatenate([acc_b[:, LEFT:], acc_c[...]], axis=1), piece_b, line_b
     )
-    run(*steps_k[12:16])
-    net.wait_group("grad side", side_z, sib)
-    total = wide(piece_z.at[at.y])
+    net.wait_group("grad two", across_z, sib)
+    total = wide(piece_z.at[at.two])
     for k in (1, 2, 3):
-        total += wide(side_z.at[k - 1])
-    half_f[...] = total.reshape(2, 64, COLS)
-    sent_z[...] = half_f[1 - at.xhi].astype(BF)
-    to_pair = net.send(sent_z, got_z, at.pair())
+        total += wide(across_z.at[k - 1])
+    row_f[...] = total
+    row_b[...] = row_f[...].astype(BF)
+    for k in (1, 2, 3):
+        net.send(row_b.at[rem4(at.one + k)], side_z.at[k - 1], at.first("B", k), "grad one")
     run(steps_r[16], steps_k[16])
     acc_a = jnp.concatenate([acc_r[...], acc_k[...]], axis=1)
     spread_lines(0, acc_a[:, 0:LEFT], acc_a[:, LEFT:], piece_a, line_a)
     sum_lines(1, line_b)
-    to_pair.wait_recv()
-    swap_f[...] = half_f[at.xhi] + wide(got_z)
+    net.wait_group("grad one", side_z, sib)
+    total = row_f[at.one]
+    for k in (1, 2, 3):
+        total += wide(side_z.at[k - 1])
+    swap_f[...] = total
     away, kept = rows(32 * (1 - c), 32, 8), rows(32 * c, 32, 8)
     last_swap = net.send(swap_f.at[away], swapped_z.at[c], sib)
     swapped_z[c] = swap_f[kept]
@@ -910,15 +925,15 @@
             bf(2, EMB, a), bf(2, EMB, b), bf(2, EMB, d), bf(2, EMB, COLS), bf(2, FF, COLS),
             bf(2, EMB, b), f32(6, 256, 128),
             f32(128, 128), f32(2, 2, 16, LEFT), bf(2, 2, 16, LEFT), bf(8, 16, LEFT), bf(8, 16, LEFT),
-            f32(48, EMB), bf(2, 32, COLS), bf(2, 32, COLS), bf(2, 2, 32, COLS), bf(4, 2, 2, 32, COLS),
+            f32(48, EMB), bf(2, 32, COLS), bf(2, 32, COLS), bf(4, 2, 32, COLS), bf(4, 4, 2, 32, COLS),
             *(bf(EMB, w) for w in (r, k, b, d)), *(bf(4, 48, w) for w in (r, k, b, d)),
             *(bf(2, 4, 48, w) for w in (r, k, b, d)), *(bf(3, 48, w) for w in (r, k, b, d)),
             *(f32(48, w) for w in (r, k, b, d)),
             bf(8, 16, LEFT), bf(8, 16, LEFT), bf(8, 16, LEFT), bf(8, 16, LEFT),
             bf(EMB, COLS), bf(FF, COLS),
             bf(2, 96, COLS), bf(2, 336, COLS), bf(2, 2, 96, COLS), bf(2, 2, 336, COLS),
-            bf(96, COLS), bf(336, COLS), bf(96, COLS), bf(336, COLS),
-            bf(4, 128, COLS), bf(3, 128, COLS), f32(2, 64, COLS), bf(64, COLS), bf(64, COLS),
+            bf(2, 432, COLS),
+            bf(4, 4, 64, COLS), bf(3, 4, 64, COLS), f32(4, 64, COLS), bf(4, 64, COLS), bf(3, 64, COLS),
             f32(64, COLS), f32(2, 32, COLS),
             f32(2, TOK, b), bf(2, TOK, b), bf(2, TOK, b), bf(2, TOK, COLS),
             bf(4, EMB, TOK), bf(EMB, TOK), bf(EMB, TOK), bf(EMB, TOK),

time: 126 us -> 114 us (0.905)
  Pallas kernels: 124 us -> 113 us
    pallas_call x1, Pallas kernels: 122 us -> 111 us  [layer(): pl.pallas_call(layer_kernel, out_shape=(jax.ShapeDtypeStruct((TOK, EMB),...]
where the time goes in v6:
time: 114 us
  Pallas kernels  113 us (99%)
    pallas_call x1, Pallas kernels, layer(): pl.pallas_call(layer_kernel, out_shape=(jax.ShapeDtypeStruct((TOK, EMB),...  111 us
    pallas_call x1, Pallas kernels, finish(): pl.pallas_call(finish_kernel, out_shape=tuple((jax.ShapeDtypeStruct(shape...  2.36 us

profile of v6, /device:TPU:1, one launch (start us, length us, event | category | flops | bytes accessed | tf_op | source)
XLA Modules:
  0.0 114.2 jit_solution(12098060651705573132)
XLA Ops:
  0.7 110.9 %layer.1 = (f32[128,768]{1,0:T(8,128)}, f32[128,768]{1,0:T(8,128)}, f32[2,2,16,896]{3,2,1,0:T(8,128)}, f32[40,768]{1,0:T(8,128)}) custom-call(bf16[128,768]{1,0:T(8,128)(2,1)} %x_in.1, bf16[128,768]{1,0:T(8,128)(2,1)} %up_in.1, f32[12,64,64]{2,1,0:T(8,128)} %bitcast.1, bf16[768,768]{1,0:T(8,128)(2,1)} %constant.10.clone.spread_in, ...), custom_call_target="tpu_custom_call" | custom-call | flops 5888802816 | bytes 30670848 | tf_op jit(solution)/shard_map/layer/pallas_call | solution.py:912
  111.6 2.4 %finish.1 = (f32[128,768]{1,0:T(8,128)}, f32[128,768]{1,0:T(8,128)}, f32[6]{0:T(128)}, f32[6]{0:T(128)}, f32[6]{0:T(128)}, /*index=5*/f32[6]{0:T(128)}, f32[6]{0...) custom-call(f32[2,2,16,896]{3,2,1,0:T(8,128)} %get-tuple-element.52., ...), custom_call_target="tpu_custom_call" | custom-call | tf_op jit(solution)/shard_map/finish/pallas_call | solution.py:981

commit v7 on v6

--- a/solution.py
+++ b/solution.py
@@ -177,10 +177,10 @@
             device_id_type=MESH,
         ).wait_recv()
 
-    def drain(self, until=None):
-        keep = 0 if until is None else self.sends - until
-        while len(self.open) > keep:
-            self.open.pop(0).wait_send()
+    def drain(self):
+        for copy in self.open:
+            copy.wait_send()
+        self.open = []
 
 
 def rows(start, size, unit=16):
@@ -238,7 +238,7 @@
         acc_r, acc_k, acc_b, acc_c,
         piece_a, piece_b, line_a, line_b,
         sib_o, sib_2, relay_o, relay_2, up_o, up_2, sum_z,
-        piece_z, across_z, row_f, row_b, side_z, swap_f, swapped_z,
+        across_z, row_f, row_b, side_z, swap_f, swapped_z,
         pre_h, hid_h, gp_h, gvo_h, turned, turned_w, turned_h, turned_g,
         send_sems, recv_sems, load_sems,
     ) = refs
@@ -299,8 +299,9 @@
         pack_f[h, 1, 8:14, 0:384] = wide(ff_address.at[:, first_col + 896 : first_col + 1280])
         pack_f[h, 1, 8:16, 384:768] = moved[32:40, COLS * h : COLS * h + COLS]
         pack_n[1, h] = pack_f[h, 1].astype(BF)
-    swap_z = net.send(pack_z.at[1 - c], half_z.at[c], sib)
-    half_z[c] = pack_z[c]
+    mine_z = rows(32 * c, 32)
+    swap_z = net.send(pack_z.at[1 - c], half_z.at[mine_z], sib)
+    half_z[mine_z] = pack_z[c]
     send_lines(1, stage_b)
 
     loads["x"].wait()
@@ -581,7 +582,24 @@
     for h in range(2):
         gvo_h[h] = grad_vo[:, COLS * h : COLS * h + COLS].astype(BF)
 
-    swaps = {}
+    def grad_w2(target, low, high, h):
+        for start, width, part in ((0, 128, None), (128, 1280, 0), (1408, 1280, 1)):
+            a, b = max(low, start), min(high, start + width)
+            if a < b:
+                cut_ = slice(a - start, b - start)
+                left = hidden_s[:, cut_] if part is None else hid_h[part, :, cut_]
+                target[a - low : b - low] = t_mm(left, gvo_h[h]).astype(BF)
+
+    for spot, low, high in (
+        (gb.at[1, :, 0:384], 0, 768),
+        (gb.at[1, :, 384:768], 768, 1536),
+        (gb.at[1, :, 768:1152], 1536, 2304),
+        (gb.at[0, 0:384, 0:384], 2304, 2688),
+    ):
+        grad_w2(spot, low, high, 1 - c)
+        net.send(spot, sib_2.at[low:high], sib, "swap 2")
+
+    swaps = {"2": partial(net.wait_group, "swap 2", sib_2, sib)}
 
     def fold(mine, other, *more):
         total = wide(mine) + wide(other)
@@ -599,11 +617,11 @@
     acc_of = {"R": acc_r, "K": acc_k, "B": acc_b, "S": acc_c}
 
     def swap(q):
-        swaps[q] = net.send(grads[q].at[1 - c], sib_of[q], sib)
+        swaps[q] = net.send(grads[q].at[1 - c], sib_of[q], sib).wait_recv
 
     def swapped(q):
         if q in swaps:
-            swaps.pop(q).wait_recv()
+            swaps.pop(q)()
 
     def scatter_far(q, m):
         part = at.band(q, m, 2)
@@ -678,7 +696,7 @@
 
     def swap_w(w):
         unit, mine, theirs = z_parts[w][:3]
-        swaps[w] = net.send(mine.at[1 - c], theirs, sib)
+        swaps[w] = net.send(mine.at[1 - c], theirs, sib).wait_recv
 
     def part_w(w, m, k):
         unit = z_parts[w][0]
@@ -719,7 +737,6 @@
         return steps_
 
     need("2")
-    gathered = net.sends
     steps_2, steps_o = scatter_steps_w("2"), scatter_steps_w("o")
     steps_b, steps_c = scatter_steps("B"), scatter_steps("S")
     steps_r, steps_k = scatter_steps("R"), scatter_steps("K")
@@ -732,6 +749,11 @@
         part = rows(128 + 1280 * h, 1280)
         grad_hidden = mm_t(gvo_h[0], w2[0, part]) + mm_t(gvo_h[1], w2[1, part])
         gp_h[h] = (grad_hidden * 2.0 * pre_h[h]).astype(BF)
+    net.drain()
+    for h in halves:
+        gb[h] = mm(turned_h[...], gp_h[h]).astype(BF)
+        if h is halves[0]:
+            swap("B")
     grad_hidden = mm_t(gvo_h[0], w2[0, 0:128]) + mm_t(gvo_h[1], w2[1, 0:128])
     grad_pre_s = (grad_hidden * 2.0 * pre_s).astype(BF)
     value_out = jnp.concatenate(
@@ -742,24 +764,13 @@
         axis=1,
     )
     layer_out = middle + gating * value_out
-    net.drain(gathered)
-    for n in halves:
-        w2[n, 0:128] = t_mm(hidden_s, gvo_h[n]).astype(BF)
-        w2[n, 128:1408] = t_mm(hid_h[0], gvo_h[n]).astype(BF)
-        w2[n, 1408:2688] = t_mm(hid_h[1], gvo_h[n]).astype(BF)
-        if n is halves[0]:
-            swap_w("2")
-    for h in halves:
-        gb[h] = mm(turned_h[...], gp_h[h]).astype(BF)
-        if h is halves[0]:
-            swap("B")
-    run(*steps_2[:4])
+    grad_w2(w2.at[c], 0, FF, c)
+    run(*steps_2[:4], *steps_b[:8])
     grad_gp = (grad_vo * value_out * (1.0 - gating)).astype(BF)
     grad_mg = mm_t(grad_gp[:, :COLS], wc[0]) + mm_t(grad_gp[:, COLS:], wc[1])
     for h in range(2):
         gc[h] = mm(turned_g[...], grad_gp[:, COLS * h : COLS * h + COLS]).astype(BF)
     swap("S")
-    run(*steps_b[:8])
     grad_mh = mm_t(grad_pre_s, wa[0, :, 1536:1664])
     grad_mh += mm_t(gp_h[0], wb[0]) + mm_t(gp_h[1], wb[1])
     gk[0, :, 768:896] = mm(turned_h[...], grad_pre_s).astype(BF)
@@ -798,10 +809,10 @@
         parts_r.append(fine(NN, beside(da), stack(kg)) + fine(NT, dg, memory[g]))
         parts_k.append(fine(TN, da, stack(rg)))
         parts_v.append(fine(TN, scores[g], ds))
-        if g == 2:
+        if g == 3:
+            run(*steps_b[8:12])
+        if g == 5:
             run(*steps_o[:4])
-        if g == 4:
-            run(*steps_b[8:12])
     grad_r = jnp.concatenate(parts_r, axis=1) * fall_r
     grad_k = jnp.concatenate(parts_k, axis=1) * fall_k
     grad_v = jnp.concatenate(parts_v, axis=1) + grad_wkv * present
@@ -822,7 +833,7 @@
     ]
     gk[0, :, 0:768] = mm(turned[1], grad_k).astype(BF)
     gk[1, :, 0:768] = mm(turned[3], grad_gate).astype(BF)
-    run(*steps_2[4:6], *steps_r[:8])
+    run(*steps_r[:8], *steps_2[4:6])
     delta = normed - previous
     g_lerps = [tsum(g * delta) for g in grad_blended]
     grad_n1 = sum(g * l for g, l in zip(grad_blended, lerps))
@@ -840,12 +851,14 @@
     )
     gk[1, :, 768:896] = table.T.astype(BF)
     swap("K")
-    run(*steps_c[8:12], *steps_b[12:16], *steps_k[:8], *steps_o[4:6], *steps_r[8:12])
+    run(*steps_c[8:12], *steps_b[12:16], *steps_k[:8], *steps_r[8:12])
     out_v, grad_v_ = pre_h.at[0, :, 0:768], pre_h.at[1, :, 0:768]
     out_v[...] = unspread(layer_out)
     out_copy = pltpu.make_async_copy(out_v, out_ref, load_sems.at[8])
     out_copy.start()
-    run(*steps_c[12:16], *steps_k[8:12], *steps_2[6:8])
+    run(*steps_o[4:6], *steps_c[12:16], *steps_k[8:12], *steps_2[6:8])
+
+    piece_z = stage_z
 
     def spread_z(m):
         table = mm(turn_z[...], sum_z[m])
@@ -925,7 +938,7 @@
             bf(2, EMB, a), bf(2, EMB, b), bf(2, EMB, d), bf(2, EMB, COLS), bf(2, FF, COLS),
             bf(2, EMB, b), f32(6, 256, 128),
             f32(128, 128), f32(2, 2, 16, LEFT), bf(2, 2, 16, LEFT), bf(8, 16, LEFT), bf(8, 16, LEFT),
-            f32(48, EMB), bf(2, 32, COLS), bf(2, 32, COLS), bf(4, 2, 32, COLS), bf(4, 4, 2, 32, COLS),
+            f32(48, EMB), bf(2, 32, COLS), bf(64, COLS), bf(4, 64, COLS), bf(4, 4, 64, COLS),
             *(bf(EMB, w) for w in (r, k, b, d)), *(bf(4, 48, w) for w in (r, k, b, d)),
             *(bf(2, 4, 48, w) for w in (r, k, b, d)), *(bf(3, 48, w) for w in (r, k, b, d)),
             *(f32(48, w) for w in (r, k, b, d)),
@@ -933,7 +946,7 @@
             bf(EMB, COLS), bf(FF, COLS),
             bf(2, 96, COLS), bf(2, 336, COLS), bf(2, 2, 96, COLS), bf(2, 2, 336, COLS),
             bf(2, 432, COLS),
-            bf(4, 4, 64, COLS), bf(3, 4, 64, COLS), f32(4, 64, COLS), bf(4, 64, COLS), bf(3, 64, COLS),
+            bf(3, 4, 64, COLS), f32(4, 64, COLS), bf(4, 64, COLS), bf(3, 64, COLS),
             f32(64, COLS), f32(2, 32, COLS),
             f32(2, TOK, b), bf(2, TOK, b), bf(2, TOK, b), bf(2, TOK, COLS),
             bf(4, EMB, TOK), bf(EMB, TOK), bf(EMB, TOK), bf(EMB, TOK),

time: 114 us -> 113 us (level)
    pallas_call x1, Pallas kernels: 111 us -> 109 us  [layer(): pl.pallas_call(layer_kernel, out_shape=(jax.ShapeDtypeStruct((TOK, EMB),...]
where the time goes in v7:
time: 113 us; the launch traced here: 112 us
  Pallas kernels  112 us (99%)
    pallas_call x1, Pallas kernels, layer(): pl.pallas_call(layer_kernel, out_shape=(jax.ShapeDtypeStruct((TOK, EMB),...  109 us
    pallas_call x1, Pallas kernels, finish(): pl.pallas_call(finish_kernel, out_shape=tuple((jax.ShapeDtypeStruct(shape...  2.36 us

profile of v7, /device:TPU:1, one launch (start us, length us, event | category | flops | bytes accessed | tf_op | source)
XLA Modules:
  0.0 112.4 jit_solution(18284112319067799898)
XLA Ops:
  0.7 109.2 %layer.1 = (f32[128,768]{1,0:T(8,128)}, f32[128,768]{1,0:T(8,128)}, f32[2,2,16,896]{3,2,1,0:T(8,128)}, f32[40,768]{1,0:T(8,128)}) custom-call(bf16[128,768]{1,0:T(8,128)(2,1)} %x_in.1, bf16[128,768]{1,0:T(8,128)(2,1)} %up_in.1, f32[12,64,64]{2,1,0:T(8,128)} %bitcast.1, bf16[768,768]{1,0:T(8,128)(2,1)} %constant.10.clone.spread_in, ...), custom_call_target="tpu_custom_call" | custom-call | flops 5888802816 | bytes 30670848 | tf_op jit(solution)/shard_map/layer/pallas_call | solution.py:925
  109.9 2.4 %finish.1 = (f32[128,768]{1,0:T(8,128)}, f32[128,768]{1,0:T(8,128)}, f32[6]{0:T(128)}, f32[6]{0:T(128)}, f32[6]{0:T(128)}, /*index=5*/f32[6]{0:T(128)}, f32[6]{0...) custom-call(f32[2,2,16,896]{3,2,1,0:T(8,128)} %get-tuple-element.52., ...), custom_call_target="tpu_custom_call" | custom-call | tf_op jit(solution)/shard_map/finish/pallas_call | solution.py:994

commit v8 on v7

--- a/solution.py
+++ b/solution.py
@@ -19,7 +19,7 @@
 EMB = 768
 FF = 2688
 COLS = 384
-SENDS, ARRIVALS = 96, 160
+SENDS, ARRIVALS = 64, 150
 LEFT, RIGHT = 896, 768
 
 WIDTH = {"A": 1664, "B": 1280, "C": 384, "R": 768, "K": 896}
@@ -177,10 +177,10 @@
             device_id_type=MESH,
         ).wait_recv()
 
-    def drain(self):
-        for copy in self.open:
-            copy.wait_send()
-        self.open = []
+    def drain(self, until=None):
+        keep = 0 if until is None else self.sends - until
+        while len(self.open) > keep:
+            self.open.pop(0).wait_send()
 
 
 def rows(start, size, unit=16):
@@ -302,7 +302,6 @@
     mine_z = rows(32 * c, 32)
     swap_z = net.send(pack_z.at[1 - c], half_z.at[mine_z], sib)
     half_z[mine_z] = pack_z[c]
-    send_lines(1, stage_b)
 
     loads["x"].wait()
     tokens = mm(x_ref[...], spread[...])
@@ -313,8 +312,8 @@
     upstream = mm(up_ref[...], spread[...])
     swap_z.wait_recv()
     for k in (1, 2, 3):
-        net.send(half_z, row_z.at[at.one], at.first("B", k), "one")
-    row_z[at.one] = half_z[...]
+        net.send(half_z, row_z.at[rows(64 * at.one, 64)], at.first("B", k), "one")
+    row_z[rows(64 * at.one, 64)] = half_z[...]
     loads["pick_n"].wait()
     for name in ("state", "turn_n", "turn_z", "pick_z"):
         loads[name].wait()
@@ -387,7 +386,8 @@
 
     picked = pick(0, stage_a)
     begin("A", picked[0:48], picked[48:96, 0:RIGHT])
-    net.wait_group("one", row_z.at[0:3], sib)
+    send_lines(1, stage_b)
+    net.wait_group("one", row_z.at[0:192], sib)
     for k in (1, 3, 2):
         net.send(row_z, stage_z.at[at.two], at.last("B", k), "two")
     stage_z[at.two] = row_z[...]
@@ -403,8 +403,9 @@
     for m in range(2):
         staged = []
         for x in (m, 2 + m):
-            block = jnp.where(c == 0, stage_z[x].astype(F32), stage_z[:, x].astype(F32))
-            staged.append(block.reshape(256, COLS).astype(BF))
+            other = stage_z[:, 64 * x : 64 * x + 64].reshape(256, COLS)
+            block = jnp.where(c == 0, stage_z[x].astype(F32), other.astype(F32))
+            staged.append(block.astype(BF))
         picked_z = mm(pick_z[...], jnp.concatenate(staged, axis=0)).astype(BF)
         place_z("o", m, 0)[...] = picked_z[:96]
         place_z("2", m, 0)[...] = picked_z[96:]
@@ -485,8 +486,8 @@
         return jnp.sum(value, axis=0, keepdims=True)
 
     def unspread(value):
-        a, b, d = split(value, 3)
-        return mm_t(a, spread[...]) + (mm_t(b, spread[...]) + mm_t(d, spread[...]))
+        high, low = split(value, 2)
+        return mm_t(high, spread[...]) + mm_t(low, spread[...])
 
     vec = mm_t(eye, wa[1, :, VEC:1664])
     gain1, bias1 = vec[0:1], vec[1:2]
@@ -591,10 +592,11 @@
                 target[a - low : b - low] = t_mm(left, gvo_h[h]).astype(BF)
 
     for spot, low, high in (
-        (gb.at[1, :, 0:384], 0, 768),
-        (gb.at[1, :, 384:768], 768, 1536),
-        (gb.at[1, :, 768:1152], 1536, 2304),
-        (gb.at[0, 0:384, 0:384], 2304, 2688),
+        (gb.at[c, :, 0:384], 0, 768),
+        (gb.at[c, :, 384:768], 768, 1536),
+        (gb.at[c, :, 768:1152], 1536, 2304),
+        (stage_z.at[0], 2304, 2560),
+        (stage_z.at[1, 0:128], 2560, 2688),
     ):
         grad_w2(spot, low, high, 1 - c)
         net.send(spot, sib_2.at[low:high], sib, "swap 2")
@@ -749,11 +751,12 @@
         part = rows(128 + 1280 * h, 1280)
         grad_hidden = mm_t(gvo_h[0], w2[0, part]) + mm_t(gvo_h[1], w2[1, part])
         gp_h[h] = (grad_hidden * 2.0 * pre_h[h]).astype(BF)
-    net.drain()
+    sent = net.sends
     for h in halves:
         gb[h] = mm(turned_h[...], gp_h[h]).astype(BF)
         if h is halves[0]:
             swap("B")
+            net.drain(sent)
     grad_hidden = mm_t(gvo_h[0], w2[0, 0:128]) + mm_t(gvo_h[1], w2[1, 0:128])
     grad_pre_s = (grad_hidden * 2.0 * pre_s).astype(BF)
     value_out = jnp.concatenate(
@@ -842,8 +845,8 @@
 
     zero = jnp.zeros((1, EMB), F32)
     natural = jnp.concatenate([g_rate, g_bonus, g_gain_w, g_bias_w] + [zero] * 4, axis=0)
-    va, vb, vc = split(natural, 3)
-    moved = mm(va, spread[...]) + (mm(vb, spread[...]) + mm(vc, spread[...]))
+    high, low = split(natural, 2)
+    moved = mm(high, spread[...]) + mm(low, spread[...])
     table = jnp.concatenate(
         [g_gain1, g_bias1] + g_lerps + [g_gain2, g_bias2, g_lerp_h, g_lerp_g]
         + [moved[0:4], jnp.zeros((114, EMB), F32)],
@@ -866,7 +869,8 @@
             for y in range(4):
                 x = xhi * 2 + m
                 at_ = (xhi * 4 + y) * 64
-                piece_z[at.by_core(x, y), at.by_core(y, x)] = table[at_ : at_ + 64].astype(BF)
+                spot = piece_z.at[at.by_core(x, y), rows(64 * at.by_core(y, x), 64)]
+                spot[...] = table[at_ : at_ + 64].astype(BF)
 
     run(*steps_o[6:8])
     spread_z(0)
@@ -887,7 +891,7 @@
     total = wide(piece_z.at[at.two])
     for k in (1, 2, 3):
         total += wide(across_z.at[k - 1])
-    row_f[...] = total
+    row_f[...] = total.reshape(4, 64, COLS)
     row_b[...] = row_f[...].astype(BF)
     for k in (1, 2, 3):
         net.send(row_b.at[rem4(at.one + k)], side_z.at[k - 1], at.first("B", k), "grad one")
@@ -938,7 +942,7 @@
             bf(2, EMB, a), bf(2, EMB, b), bf(2, EMB, d), bf(2, EMB, COLS), bf(2, FF, COLS),
             bf(2, EMB, b), f32(6, 256, 128),
             f32(128, 128), f32(2, 2, 16, LEFT), bf(2, 2, 16, LEFT), bf(8, 16, LEFT), bf(8, 16, LEFT),
-            f32(48, EMB), bf(2, 32, COLS), bf(64, COLS), bf(4, 64, COLS), bf(4, 4, 64, COLS),
+            f32(48, EMB), bf(2, 32, COLS), bf(64, COLS), bf(256, COLS), bf(4, 256, COLS),
             *(bf(EMB, w) for w in (r, k, b, d)), *(bf(4, 48, w) for w in (r, k, b, d)),
             *(bf(2, 4, 48, w) for w in (r, k, b, d)), *(bf(3, 48, w) for w in (r, k, b, d)),
             *(f32(48, w) for w in (r, k, b, d)),
@@ -946,7 +950,7 @@
             bf(EMB, COLS), bf(FF, COLS),
             bf(2, 96, COLS), bf(2, 336, COLS), bf(2, 2, 96, COLS), bf(2, 2, 336, COLS),
             bf(2, 432, COLS),
-            bf(3, 4, 64, COLS), f32(4, 64, COLS), bf(4, 64, COLS), bf(3, 64, COLS),
+            bf(3, 256, COLS), f32(4, 64, COLS), bf(4, 64, COLS), bf(3, 64, COLS),
             f32(64, COLS), f32(2, 32, COLS),
             f32(2, TOK, b), bf(2, TOK, b), bf(2, TOK, b), bf(2, TOK, COLS),
             bf(4, EMB, TOK), bf(EMB, TOK), bf(EMB, TOK), bf(EMB, TOK),

time: 113 us -> 110 us (0.973)
  Pallas kernels: 112 us -> 109 us
    pallas_call x1, Pallas kernels: 109 us -> 107 us  [layer(): pl.pallas_call(layer_kernel, out_shape=(jax.ShapeDtypeStruct((TOK, EMB),...]
where the time goes in v8:
time: 110 us
  Pallas kernels  109 us (99%)
    pallas_call x1, Pallas kernels, layer(): pl.pallas_call(layer_kernel, out_shape=(jax.ShapeDtypeStruct((TOK, EMB),...  107 us
    pallas_call x1, Pallas kernels, finish(): pl.pallas_call(finish_kernel, out_shape=tuple((jax.ShapeDtypeStruct(shape...  2.36 us

profile of v8, /device:TPU:1, one launch (start us, length us, event | category | flops | bytes accessed | tf_op | source)
XLA Modules:
  0.0 110.0 jit_solution(5323789817981560076)
XLA Ops:
  0.7 106.7 %layer.1 = (f32[128,768]{1,0:T(8,128)}, f32[128,768]{1,0:T(8,128)}, f32[2,2,16,896]{3,2,1,0:T(8,128)}, f32[40,768]{1,0:T(8,128)}) custom-call(bf16[128,768]{1,0:T(8,128)(2,1)} %x_in.1, bf16[128,768]{1,0:T(8,128)(2,1)} %up_in.1, f32[12,64,64]{2,1,0:T(8,128)} %bitcast.1, bf16[768,768]{1,0:T(8,128)(2,1)} %constant.10.clone.spread_in, ...), custom_call_target="tpu_custom_call" | custom-call | flops 5888802816 | bytes 30670848 | tf_op jit(solution)/shard_map/layer/pallas_call | solution.py:929
  107.4 2.4 %finish.1 = (f32[128,768]{1,0:T(8,128)}, f32[128,768]{1,0:T(8,128)}, f32[6]{0:T(128)}, f32[6]{0:T(128)}, f32[6]{0:T(128)}, /*index=5*/f32[6]{0:T(128)}, f32[6]{0...) custom-call(f32[2,2,16,896]{3,2,1,0:T(8,128)} %get-tuple-element.52., ...), custom_call_target="tpu_custom_call" | custom-call | tf_op jit(solution)/shard_map/finish/pallas_call | solution.py:998

commit v9 on v8

--- a/solution.py
+++ b/solution.py
@@ -836,6 +836,7 @@
     ]
     gk[0, :, 0:768] = mm(turned[1], grad_k).astype(BF)
     gk[1, :, 0:768] = mm(turned[3], grad_gate).astype(BF)
+    net.send(gk.at[1 - c, :, 0:768], sib_k.at[:, 0:768], sib, "swap K")
     run(*steps_r[:8], *steps_2[4:6])
     delta = normed - previous
     g_lerps = [tsum(g * delta) for g in grad_blended]
@@ -853,7 +854,8 @@
         axis=0,
     )
     gk[1, :, 768:896] = table.T.astype(BF)
-    swap("K")
+    net.send(gk.at[1 - c, :, 768:896], sib_k.at[:, 768:896], sib, "swap K")
+    swaps["K"] = partial(net.wait_group, "swap K", sib_k, sib)
     run(*steps_c[8:12], *steps_b[12:16], *steps_k[:8], *steps_r[8:12])
     out_v, grad_v_ = pre_h.at[0, :, 0:768], pre_h.at[1, :, 0:768]
     out_v[...] = unspread(layer_out)

time: 110 us -> 110 us (level)
  no operation moved by 1% of the time
where the time goes in v9:
time: 110 us
  Pallas kernels  109 us (99%)
    pallas_call x1, Pallas kernels, layer(): pl.pallas_call(layer_kernel, out_shape=(jax.ShapeDtypeStruct((TOK, EMB),...  107 us
    pallas_call x1, Pallas kernels, finish(): pl.pallas_call(finish_kernel, out_shape=tuple((jax.ShapeDtypeStruct(shape...  2.36 us

profile of v9, /device:TPU:1, one launch (start us, length us, event | category | flops | bytes accessed | tf_op | source)
XLA Modules:
  0.0 110.0 jit_solution(7924783897472195027)
XLA Ops:
  0.7 106.7 %layer.1 = (f32[128,768]{1,0:T(8,128)}, f32[128,768]{1,0:T(8,128)}, f32[2,2,16,896]{3,2,1,0:T(8,128)}, f32[40,768]{1,0:T(8,128)}) custom-call(bf16[128,768]{1,0:T(8,128)(2,1)} %x_in.1, bf16[128,768]{1,0:T(8,128)(2,1)} %up_in.1, f32[12,64,64]{2,1,0:T(8,128)} %bitcast.1, bf16[768,768]{1,0:T(8,128)(2,1)} %constant.10.clone.spread_in, ...), custom_call_target="tpu_custom_call" | custom-call | flops 5888802816 | bytes 30670848 | tf_op jit(solution)/shard_map/layer/pallas_call | solution.py:931
  107.4 2.4 %finish.1 = (f32[128,768]{1,0:T(8,128)}, f32[128,768]{1,0:T(8,128)}, f32[6]{0:T(128)}, f32[6]{0:T(128)}, f32[6]{0:T(128)}, /*index=5*/f32[6]{0:T(128)}, f32[6]{0...) custom-call(f32[2,2,16,896]{3,2,1,0:T(8,128)} %get-tuple-element.52., ...), custom_call_target="tpu_custom_call" | custom-call | tf_op jit(solution)/shard_map/finish/pallas_call | solution.py:1000
